TPU v7x, 512 devices: a whole 4x8x8 slice. The times are simulated.
512 devices in a mesh: pulse: 128 (over x_hi, z, y), range: 4 (over x_lo, core).
Axes of the slice: x: 4 (x_hi: 2, x_lo: 2; x = x_hi * 2 + x_lo), y: 8, z: 8, core: 2. Of those that a mesh axis runs over, the one named last changes fastest.
Arguments:
- grad_image: bfloat16 [128, 2, 16, 16, 2048], P('pulse', None, None, None, 'range'), may hold values from -6 to 6
- range_kernel: bfloat16 [4, 16, 2, 128, 256], P(None, 'range'), may hold values from -0.25 to 0.25
- band_offsets: int32 [4, 16], P(None, 'range'), may hold values from -64 to 64
- beam_mix: bfloat16 [4, 128, 2, 8, 16], P(None, 'pulse'), may hold values from -1.5 to 1.5
- ramp: bfloat16 [4, 128, 2, 8, 2048], P(None, 'pulse', None, None, 'range'), may hold values from -3.140625 to 3.140625
- baseline_ids: int32 [16], replicated, may hold values from 0 to 7
- baseline_scale: float32 [8], replicated, may hold values from 0.5 to 2
Outputs:
- split_grad: bfloat16 [128, 2, 16, 16, 2048], P('pulse', None, None, None, 'range')
All inputs are finite; a program needn't handle non-finite values.
Results may differ from a plain program's by a relative error of at most 0.017.
Values may be sent and summed in bfloat16 or wider, within the bound.
No kernel may reach another device: no remote copies, remote signals or barrier semaphores. Data moves between devices by JAX's collectives and lax.ppermute only.
A program may use at most 128 MiB of HBM per device.

v0:
```python
import jax
import jax.numpy as jnp
from jax import lax
from jax.sharding import PartitionSpec as P

TILE = 128
LEVELS = 4


def swapped(value, axis, apart):
    mask = 2**apart
    pairs = [(source, source ^ mask) for source in range(lax.axis_size(axis))]
    return lax.ppermute(value, axis, pairs)


def extended(block, sides, width):
    for axis, dim in sides:
        count = lax.axis_size(axis)
        forward = [(i, i + 1) for i in range(count - 1)]
        backward = [(target, source) for source, target in forward]
        low = lax.ppermute(
            lax.slice_in_dim(block, block.shape[dim] - width, None, axis=dim), axis, forward
        )
        high = lax.ppermute(lax.slice_in_dim(block, 0, width, axis=dim), axis, backward)
        block = jnp.concatenate([low, block, high], axis=dim)
    return block


def child_half(interp, mixing, ramp_half, channel_phase):
    mixed = jnp.einsum("zcmr,nm->zcnr", interp, mixing, preferred_element_type=jnp.float32)
    theta = ramp_half.astype(jnp.float32)[None, :, :] * channel_phase[:, None, None]
    cosine = jnp.cos(theta)
    sine = jnp.sin(theta)
    out_re = mixed[0] * cosine + mixed[1] * sine
    out_im = mixed[1] * cosine - mixed[0] * sine
    return jnp.stack([out_re, out_im]).astype(jnp.bfloat16)


def trade(outgoing, bit_number):
    return swapped(outgoing, "pulse", bit_number)


def body(grad_image, range_kernel, band_offsets, beam_mix, ramp, baseline_ids, baseline_scale):
    current = grad_image[0]
    onehot_table = (
        baseline_ids[:, None] == jnp.arange(baseline_scale.shape[0], dtype=jnp.int32)[None, :]
    ).astype(jnp.float32)
    channel_phase = jnp.sum(onehot_table * baseline_scale[None, :], axis=1)
    log_slots = lax.axis_size("pulse").bit_length() - 1
    my_index = lax.axis_index("pulse")
    tile_count = current.shape[3] // TILE
    for level_index in range(LEVELS):
        bit_number = (log_slots - 3 - level_index) % log_slots
        starts = (
            jnp.arange(tile_count, dtype=jnp.int32) * TILE + TILE // 2 + band_offsets[level_index]
        )
        padded = extended(current, (("range", 3),), TILE)
        pieces = []
        for tile_index in range(tile_count):
            pieces.append(lax.dynamic_slice_in_dim(padded, starts[tile_index], 2 * TILE, 3))
        windows = jnp.stack(pieces)
        kernel = range_kernel[level_index]
        kern_re = kernel[:, 0]
        kern_im = kernel[:, 1]
        combined = jnp.stack(
            [jnp.stack([kern_re, kern_im], 1), jnp.stack([-kern_im, kern_re], 1)], 1
        )
        interp = jnp.einsum(
            "tzcmk,tzwok->wcmto", windows, combined, preferred_element_type=jnp.float32
        )
        interp = interp.reshape(current.shape).astype(jnp.bfloat16)
        keep_bit = my_index // 2**bit_number % 2
        mixing = beam_mix[level_index, 0]
        ramp_level = ramp[level_index, 0]
        first_half = child_half(interp, mixing[0], ramp_level[0], channel_phase)
        second_half = child_half(interp, mixing[1], ramp_level[1], channel_phase)
        kept = jnp.where(keep_bit == 1, second_half, first_half)
        outgoing = jnp.where(keep_bit == 1, first_half, second_half)
        received = trade(outgoing, bit_number)
        lower_first = jnp.concatenate([kept, received], axis=2)
        upper_first = jnp.concatenate([received, kept], axis=2)
        current = jnp.where(keep_bit == 0, lower_first, upper_first)
    return current[None]


def solution(mesh):
    placed = (
        P("pulse", None, None, None, "range"),
        P(None, "range", None, None, None),
        P(None, "range"),
        P(None, "pulse", None, None, None),
        P(None, "pulse", None, None, "range"),
        P(),
        P(),
    )
    return jax.shard_map(
        body,
        mesh=mesh,
        in_specs=placed,
        out_specs=P("pulse", None, None, None, "range"),
        check_vma=False,
    )
```

profile of v0, /device:TPU:1, one launch (start us, length us, event | category | flops | bytes accessed | tf_op | source)
XLA Modules:
  0.0 145.0 jit_solution(3441138565451010737)
XLA Ops:
  0.0 1.6 %fusion.128 = (bf16[2,16,16,128]{3,2,1,0:T(8,128)(2,1)S(1)}, bf16[2,16,16,128]{3,2,1,0:T(8,128)(2,1)}) fusion(bf16[2,16,16,512]{3,2,1,0:T(8,128)(2,1)} %bitcast.289), kind=kLoop, calls=%fused_computation.239 | loop fusion | bytes 524288 | tf_op jit(solution)/shard_map/slice | solution.py:22
  1.6 8.8 %collective-permute-start.1 = (bf16[2,16,16,128]{3,2,1,0:T(8,128)(2,1)}, bf16[2,16,16,128]{3,2,1,0:T(8,128)(2,1)S(1)}, u32[]{:S(2)}, u32[]{:S(2)}) collective-permute-start(bf16[2,16,16,128]{3,2,1,0:T(8,128)(2,1)} %get-tuple-element.60), channel_id=1, source_target_pairs={{1,0},{2,1},{3,2},{5,4},{6,5},{7,6},{9,8},{10,9},{11,10},{13,12},{... | collective-permute-start | bytes 393224 | tf_op jit(solution)/shard_map/ppermute | solution.py:24
  10.4 2.1 %collective-permute-start = (bf16[2,16,16,128]{3,2,1,0:T(8,128)(2,1)S(1)}, bf16[2,16,16,128]{3,2,1,0:T(8,128)(2,1)S(1)}, u32[]{:S(2)}, u32[]{:S(2)}) collective-permute-start(bf16[2,16,16,128]{3,2,1,0:T(8,128)(2,1)S(1)} %get-tuple-element.59), channel_id=1, source_target_pairs={{0,1},{1,2},{2,3},{4,5},{5,6},{6,7},{8,9},{9,10},{10,11},{12,13},{... | collective-permute-start | bytes 393224 | tf_op jit(solution)/shard_map/ppermute | solution.py:21
  12.5 2.9 %slice_bitcast_fusion.1 = (bf16[4,1,2,128,256]{4,3,1,2,0:T(8,128)(2,1)}, bf16[4,2,128,256]{3,2,1,0:T(8,128)(2,1)S(1)}, bf16[4,2,128,256]{3,2,1,0:T(8,128)(2,1)S(...) fusion(bf16[4,4,2,128,256]{4,3,2,1,0:T(8,128)(2,1)} %param.8), kind=kLoop, calls=%fused_computation.74 | loop fusion | bytes 6291456 | tf_op jit(solution)/shard_map/stack | solution.py:65
  15.4 0.6 bitcast_add_fusion
  16.0 0.7 bitcast_convert_fusion.1
  16.7 0.1 slice_negate_fusion
  16.8 0.6 select_reduce_fusion
  17.4 0.7 fusion.131
  25.6 0.1 maximum_bitcast_fusion.16
  25.7 0.1 pad_maximum_fusion
  25.8 0.4 constant_dynamic-slice_fusion.3
  26.4 0.5 copy-done.3
  26.8 0.5 fusion.7
  27.3 0.2 copy-done.12
  27.5 0.2 convolution_bitcast_fusion.11
  27.8 0.2 convolution_bitcast_fusion.10
  28.0 0.3 copy-done.9
  28.3 2.3 %fusion.102 = (bf16[1,16,8,512]{3,2,1,0:T(8,128)(2,1)S(1)}, bf16[1,16,8,512]{3,2,1,0:T(8,128)(2,1)S(1)}, bf16[1,16,8,512]{3,2,1,0:T(8,128)(2,1)S(1)}, bf16[1,16,8,512]{3,2,1,0:T(8,128)(2,1)S(1)}) fusion(f32[2,16,8,512]{3,2,1,0:T(8,128)S(1)} %convolution_bitcast_fusion.11, f32[16]{0:T(128)S(1)} %copy-done.15, f32[8,512]{1,0:T(8,128)S(1)} %copy-done.10, ...), kind=kLoop, calls=%fused_computation.158 | loop fusion | flops 1179648 | bytes 1605696 | tf_op jit(solution)/shard_map/convert.22
  30.6 0.1 broadcast_select_fusion.1
  30.6 1.9 %collective-permute-start.2 = (bf16[2,16,8,512]{3,2,1,0:T(8,128)(2,1)S(1)}, bf16[2,16,8,512]{3,2,1,0:T(8,128)(2,1)S(1)}, u32[]{:S(2)}, u32[]{:S(2)}) collective-permute-start(bf16[2,16,8,512]{3,2,1,0:T(8,128)(2,1)S(1)} %get-tuple-element.58), channel_id=1, source_target_pairs={{0,64},{4,68},{8,72},{12,76},{16,80},{20,84},{24,88},{28,92},{32,9... | collective-permute-start | bytes 786440 | tf_op jit(solution)/shard_map/ppermute | solution.py:13
  32.6 13.4 %collective-permute-done.2 = bf16[2,16,8,512]{3,2,1,0:T(8,128)(2,1)S(1)} collective-permute-done((bf16[2,16,8,512]{3,2,1,0:T(8,128)(2,1)S(1)}, bf16[2,16,8,512]{3,2,1,0:T(8,128)(2,1)S(1)}, u32[]{:S(2)}, u32[]{:S(2)}) %collective-permute-start.2) | collective-permute-done | bytes 262176 | tf_op jit(solution)/shard_map/ppermute | solution.py:13
  45.9 0.2 maximum_select_fusion
  46.2 2.4 %collective-permute-start.4 = (bf16[2,16,16,128]{3,2,1,0:T(8,128)(2,1)S(1)}, bf16[2,16,16,128]{3,2,1,0:T(8,128)(2,1)S(1)}, u32[]{:S(2)}, u32[]{:S(2)}) collective-permute-start(bf16[2,16,16,128]{3,2,1,0:T(8,128)(2,1)S(1)} %get-tuple-element.56), channel_id=1, source_target_pairs={{1,0},{2,1},{3,2},{5,4},{6,5},{7,6},{9,8},{10,9},{11,10},{13,12},{... | collective-permute-start | bytes 393224 | tf_op jit(solution)/shard_map/ppermute | solution.py:24
  48.6 3.2 %collective-permute-start.3 = (bf16[2,16,16,128]{3,2,1,0:T(8,128)(2,1)S(1)}, bf16[2,16,16,128]{3,2,1,0:T(8,128)(2,1)S(1)}, u32[]{:S(2)}, u32[]{:S(2)}) collective-permute-start(bf16[2,16,16,128]{3,2,1,0:T(8,128)(2,1)S(1)} %get-tuple-element.55), channel_id=1, source_target_pairs={{0,1},{1,2},{2,3},{4,5},{5,6},{6,7},{8,9},{9,10},{10,11},{12,13},{... | collective-permute-start | bytes 393224 | tf_op jit(solution)/shard_map/ppermute | solution.py:21
  59.5 0.1 maximum_bitcast_fusion.15
  59.6 0.1 pad_maximum_fusion.1
  59.7 0.4 dynamic-slice_bitcast_fusion.11
  60.1 0.5 copy-done.2
  60.6 0.5 fusion.6
  61.1 0.2 convolution_bitcast_fusion.9
  61.3 0.2 convolution_bitcast_fusion.8
  61.5 0.3 copy-done.7
  61.8 2.3 %fusion.94 = (bf16[1,16,8,512]{3,2,1,0:T(8,128)(2,1)S(1)}, bf16[1,16,8,512]{3,2,1,0:T(8,128)(2,1)S(1)}, bf16[1,16,8,512]{3,2,1,0:T(8,128)(2,1)S(1)}, bf16[1,16,8,512]{3,2,1,0:T(8,128)(2,1)S(1)}) fusion(f32[2,16,8,512]{3,2,1,0:T(8,128)S(1)} %convolution_bitcast_fusion.9, f32[8,512]{1,0:T(8,128)S(1)} %copy-done.8, f32[16]{0:T(128)S(1)} %copy-done.15, ...), kind=kLoop, calls=%fused_computation.150 | loop fusion | flops 1179648 | bytes 1605696 | tf_op jit(solution)/shard_map/convert.18
  64.2 1.9 %collective-permute-start.5 = (bf16[2,16,8,512]{3,2,1,0:T(8,128)(2,1)S(1)}, bf16[2,16,8,512]{3,2,1,0:T(8,128)(2,1)S(1)}, u32[]{:S(2)}, u32[]{:S(2)}) collective-permute-start(bf16[2,16,8,512]{3,2,1,0:T(8,128)(2,1)S(1)} %get-tuple-element.54), channel_id=1, source_target_pairs={{0,32},{4,36},{8,40},{12,44},{16,48},{20,52},{24,56},{28,60},{32,0... | collective-permute-start | bytes 786440 | tf_op jit(solution)/shard_map/ppermute | solution.py:13
  66.1 0.1 slice_negate_fusion.2
  66.2 7.7 %collective-permute-done.5 = bf16[2,16,8,512]{3,2,1,0:T(8,128)(2,1)S(1)} collective-permute-done((bf16[2,16,8,512]{3,2,1,0:T(8,128)(2,1)S(1)}, bf16[2,16,8,512]{3,2,1,0:T(8,128)(2,1)S(1)}, u32[]{:S(2)}, u32[]{:S(2)}) %collective-permute-start.5) | collective-permute-done | bytes 262176 | tf_op jit(solution)/shard_map/ppermute | solution.py:13
  73.8 0.2 maximum_select_fusion.1
  74.1 2.3 %collective-permute-start.7 = (bf16[2,16,16,128]{3,2,1,0:T(8,128)(2,1)S(1)}, bf16[2,16,16,128]{3,2,1,0:T(8,128)(2,1)S(1)}, u32[]{:S(2)}, u32[]{:S(2)}) collective-permute-start(bf16[2,16,16,128]{3,2,1,0:T(8,128)(2,1)S(1)} %get-tuple-element.52), channel_id=1, source_target_pairs={{1,0},{2,1},{3,2},{5,4},{6,5},{7,6},{9,8},{10,9},{11,10},{13,12},{... | collective-permute-start | bytes 393224 | tf_op jit(solution)/shard_map/ppermute | solution.py:24
  76.4 3.3 %collective-permute-start.6 = (bf16[2,16,16,128]{3,2,1,0:T(8,128)(2,1)S(1)}, bf16[2,16,16,128]{3,2,1,0:T(8,128)(2,1)S(1)}, u32[]{:S(2)}, u32[]{:S(2)}) collective-permute-start(bf16[2,16,16,128]{3,2,1,0:T(8,128)(2,1)S(1)} %get-tuple-element.51), channel_id=1, source_target_pairs={{0,1},{1,2},{2,3},{4,5},{5,6},{6,7},{8,9},{9,10},{10,11},{12,13},{... | collective-permute-start | bytes 393224 | tf_op jit(solution)/shard_map/ppermute | solution.py:21
  79.7 0.7 fusion.129
  88.1 0.1 pad_maximum_fusion.2
  88.2 0.4 dynamic-slice_bitcast_fusion.7
  88.7 0.5 copy-done.1
  89.2 0.5 fusion.5
  89.7 0.2 convolution_bitcast_fusion.7
  89.9 0.2 convolution_bitcast_fusion.6
  90.1 0.3 copy-done.5
  90.4 2.3 %fusion.86 = (bf16[1,16,8,512]{3,2,1,0:T(8,128)(2,1)S(1)}, bf16[1,16,8,512]{3,2,1,0:T(8,128)(2,1)S(1)}, bf16[1,16,8,512]{3,2,1,0:T(8,128)(2,1)S(1)}, bf16[1,16,8,512]{3,2,1,0:T(8,128)(2,1)S(1)}) fusion(f32[2,16,8,512]{3,2,1,0:T(8,128)S(1)} %convolution_bitcast_fusion.7, f32[8,512]{1,0:T(8,128)S(1)} %copy-done.6, f32[16]{0:T(128)S(1)} %copy-done.15, ...), kind=kLoop, calls=%fused_computation.142 | loop fusion | flops 1179648 | bytes 1605696 | tf_op jit(solution)/shard_map/convert.14
  92.7 5.3 %collective-permute-start.8 = (bf16[2,16,8,512]{3,2,1,0:T(8,128)(2,1)S(1)}, bf16[2,16,8,512]{3,2,1,0:T(8,128)(2,1)S(1)}, u32[]{:S(2)}, u32[]{:S(2)}) collective-permute-start(bf16[2,16,8,512]{3,2,1,0:T(8,128)(2,1)S(1)} %get-tuple-element.50), channel_id=1, source_target_pairs={{0,16},{4,20},{8,24},{12,28},{16,0},{20,4},{24,8},{28,12},{32,48},... | collective-permute-start | bytes 786440 | tf_op jit(solution)/shard_map/ppermute | solution.py:13
  98.0 13.8 %collective-permute-done.8 = bf16[2,16,8,512]{3,2,1,0:T(8,128)(2,1)S(1)} collective-permute-done((bf16[2,16,8,512]{3,2,1,0:T(8,128)(2,1)S(1)}, bf16[2,16,8,512]{3,2,1,0:T(8,128)(2,1)S(1)}, u32[]{:S(2)}, u32[]{:S(2)}) %collective-permute-start.8) | collective-permute-done | bytes 262176 | tf_op jit(solution)/shard_map/ppermute | solution.py:13
  111.8 0.2 maximum_select_fusion.2
  112.1 2.3 %collective-permute-start.10 = (bf16[2,16,16,128]{3,2,1,0:T(8,128)(2,1)S(1)}, bf16[2,16,16,128]{3,2,1,0:T(8,128)(2,1)S(1)}, u32[]{:S(2)}, u32[]{:S(2)}) collective-permute-start(bf16[2,16,16,128]{3,2,1,0:T(8,128)(2,1)S(1)} %get-tuple-element.48), channel_id=1, source_target_pairs={{1,0},{2,1},{3,2},{5,4},{6,5},{7,6},{9,8},{10,9},{11,10},{13,12},{... | collective-permute-start | bytes 393224 | tf_op jit(solution)/shard_map/ppermute | solution.py:24
  114.4 3.3 %collective-permute-start.9 = (bf16[2,16,16,128]{3,2,1,0:T(8,128)(2,1)S(1)}, bf16[2,16,16,128]{3,2,1,0:T(8,128)(2,1)S(1)}, u32[]{:S(2)}, u32[]{:S(2)}) collective-permute-start(bf16[2,16,16,128]{3,2,1,0:T(8,128)(2,1)S(1)} %get-tuple-element.47), channel_id=1, source_target_pairs={{0,1},{1,2},{2,3},{4,5},{5,6},{6,7},{8,9},{9,10},{10,11},{12,13},{... | collective-permute-start | bytes 393224 | tf_op jit(solution)/shard_map/ppermute | solution.py:21
  125.2 0.1 pad_maximum_fusion.3
  125.3 0.4 dynamic-slice_bitcast_fusion.3
  125.7 0.5 fusion.4
  126.2 0.2 convolution_bitcast_fusion.5
  126.4 0.2 convolution_bitcast_fusion.4
  126.6 0.3 copy-done.4
  126.9 2.3 %fusion.78 = (bf16[1,16,8,512]{3,2,1,0:T(8,128)(2,1)S(1)}, bf16[1,16,8,512]{3,2,1,0:T(8,128)(2,1)S(1)}, bf16[1,16,8,512]{3,2,1,0:T(8,128)(2,1)S(1)}, bf16[1,16,8,512]{3,2,1,0:T(8,128)(2,1)S(1)}) fusion(f32[2,16,8,512]{3,2,1,0:T(8,128)S(1)} %convolution_bitcast_fusion.5, f32[8,512]{1,0:T(8,128)S(1)} %get-tuple-element.69, f32[16]{0:T(128)S(1)} %copy-done.15, ...), kind=kLoop, calls=%fused_computation.134 | loop fusion | flops 1179648 | bytes 1605696 | tf_op jit(solution)/shard_map/convert.10
  129.3 1.9 %collective-permute-start.11 = (bf16[2,16,8,512]{3,2,1,0:T(8,128)(2,1)S(1)}, bf16[2,16,8,512]{3,2,1,0:T(8,128)(2,1)S(1)}, u32[]{:S(2)}, u32[]{:S(2)}) collective-permute-start(bf16[2,16,8,512]{3,2,1,0:T(8,128)(2,1)S(1)} %get-tuple-element.46), channel_id=1, source_target_pairs={{0,8},{4,12},{8,0},{12,4},{16,24},{20,28},{24,16},{28,20},{32,40},... | collective-permute-start | bytes 786440 | tf_op jit(solution)/shard_map/ppermute | solution.py:13
  131.2 12.8 %collective-permute-done.11 = bf16[2,16,8,512]{3,2,1,0:T(8,128)(2,1)S(1)} collective-permute-done((bf16[2,16,8,512]{3,2,1,0:T(8,128)(2,1)S(1)}, bf16[2,16,8,512]{3,2,1,0:T(8,128)(2,1)S(1)}, u32[]{:S(2)}, u32[]{:S(2)}) %collective-permute-start.11) | collective-permute-done | bytes 262176 | tf_op jit(solution)/shard_map/ppermute | solution.py:13
  144.0 1.0 maximum_select_fusion.3
  (50 shorter events, 0.6 us)
Async XLA Ops:
  1.6 24.0 %collective-permute-start.1 = (bf16[2,16,16,128]{3,2,1,0:T(8,128)(2,1)}, bf16[2,16,16,128]{3,2,1,0:T(8,128)(2,1)S(1)}, u32[]{:S(2)}, u32[]{:S(2)}) collective-permute-start(bf16[2,16,16,128]{3,2,1,0:T(8,128)(2,1)} %get-tuple-element.60), channel_id=1, source_target_pairs={{1,0},{2,1},{3,2},{5,4},{6,5},{7,6},{9,8},{10,9},{11,10},{13,12},{... | collective-permute-start | bytes 393224 | tf_op jit(solution)/shard_map/ppermute | solution.py:24
  10.4 5.0 %copy-start.16 = (s32[4,4]{1,0:T(4,128)S(1)}, s32[4,4]{1,0:T(4,128)}, u32[]{:S(2)}) copy-start(s32[4,4]{1,0:T(4,128)} %param.9) | copy-start | bytes 196
  10.4 5.6 %copy-start.11 = (bf16[4,1,2,8,512]{4,3,2,1,0:T(8,128)(2,1)S(1)}, bf16[4,1,2,8,512]{4,3,2,1,0:T(8,128)(2,1)}, u32[]{:S(2)}) copy-start(bf16[4,1,2,8,512]{4,3,2,1,0:T(8,128)(2,1)} %param.11) | copy-start | bytes 196612
  10.4 15.2 %collective-permute-start = (bf16[2,16,16,128]{3,2,1,0:T(8,128)(2,1)S(1)}, bf16[2,16,16,128]{3,2,1,0:T(8,128)(2,1)S(1)}, u32[]{:S(2)}, u32[]{:S(2)}) collective-permute-start(bf16[2,16,16,128]{3,2,1,0:T(8,128)(2,1)S(1)} %get-tuple-element.59), channel_id=1, source_target_pairs={{0,1},{1,2},{2,3},{4,5},{5,6},{6,7},{8,9},{9,10},{10,11},{12,13},{... | collective-permute-start | bytes 393224 | tf_op jit(solution)/shard_map/ppermute | solution.py:21
  15.4 1.3 copy-start.17
  15.4 1.3 copy-start.18
  15.4 10.2 %copy-start = (bf16[1,2,16,16,512]{4,3,2,1,0:T(8,128)(2,1)S(1)}, bf16[1,2,16,16,512]{4,3,2,1,0:T(8,128)(2,1)}, u32[]{:S(2)}) copy-start(bf16[1,2,16,16,512]{4,3,2,1,0:T(8,128)(2,1)} %param.7) | copy-start | bytes 1572868
  25.8 1.0 copy-start.3
  26.8 0.7 copy-start.12
  27.5 0.7 copy-start.9
  27.5 0.7 copy-start.10
  27.5 0.7 copy-start.15
  30.6 15.3 %collective-permute-start.2 = (bf16[2,16,8,512]{3,2,1,0:T(8,128)(2,1)S(1)}, bf16[2,16,8,512]{3,2,1,0:T(8,128)(2,1)S(1)}, u32[]{:S(2)}, u32[]{:S(2)}) collective-permute-start(bf16[2,16,8,512]{3,2,1,0:T(8,128)(2,1)S(1)} %get-tuple-element.58), channel_id=1, source_target_pairs={{0,64},{4,68},{8,72},{12,76},{16,80},{20,84},{24,88},{28,92},{32,9... | collective-permute-start | bytes 786440 | tf_op jit(solution)/shard_map/ppermute | solution.py:13
  46.2 13.3 %collective-permute-start.4 = (bf16[2,16,16,128]{3,2,1,0:T(8,128)(2,1)S(1)}, bf16[2,16,16,128]{3,2,1,0:T(8,128)(2,1)S(1)}, u32[]{:S(2)}, u32[]{:S(2)}) collective-permute-start(bf16[2,16,16,128]{3,2,1,0:T(8,128)(2,1)S(1)} %get-tuple-element.56), channel_id=1, source_target_pairs={{1,0},{2,1},{3,2},{5,4},{6,5},{7,6},{9,8},{10,9},{11,10},{13,12},{... | collective-permute-start | bytes 393224 | tf_op jit(solution)/shard_map/ppermute | solution.py:24
  48.6 10.9 %collective-permute-start.3 = (bf16[2,16,16,128]{3,2,1,0:T(8,128)(2,1)S(1)}, bf16[2,16,16,128]{3,2,1,0:T(8,128)(2,1)S(1)}, u32[]{:S(2)}, u32[]{:S(2)}) collective-permute-start(bf16[2,16,16,128]{3,2,1,0:T(8,128)(2,1)S(1)} %get-tuple-element.55), channel_id=1, source_target_pairs={{0,1},{1,2},{2,3},{4,5},{5,6},{6,7},{8,9},{9,10},{10,11},{12,13},{... | collective-permute-start | bytes 393224 | tf_op jit(solution)/shard_map/ppermute | solution.py:21
  59.5 1.0 copy-start.2
  61.1 0.7 copy-start.7
  61.1 0.7 copy-start.8
  64.1 15.5 %copy-start.13 = (s32[4]{0:T(128)S(1)}, s32[4]{0:T(128)}, u32[]{:S(2)}) copy-start(s32[4]{0:T(128)} %get-tuple-element.77) | copy-start | bytes 52
  64.1 15.5 %copy-start.14 = (s32[4]{0:T(128)S(1)}, s32[4]{0:T(128)}, u32[]{:S(2)}) copy-start(s32[4]{0:T(128)} %get-tuple-element.80) | copy-start | bytes 52
  64.2 9.7 %collective-permute-start.5 = (bf16[2,16,8,512]{3,2,1,0:T(8,128)(2,1)S(1)}, bf16[2,16,8,512]{3,2,1,0:T(8,128)(2,1)S(1)}, u32[]{:S(2)}, u32[]{:S(2)}) collective-permute-start(bf16[2,16,8,512]{3,2,1,0:T(8,128)(2,1)S(1)} %get-tuple-element.54), channel_id=1, source_target_pairs={{0,32},{4,36},{8,40},{12,44},{16,48},{20,52},{24,56},{28,60},{32,0... | collective-permute-start | bytes 786440 | tf_op jit(solution)/shard_map/ppermute | solution.py:13
  74.1 14.0 %collective-permute-start.7 = (bf16[2,16,16,128]{3,2,1,0:T(8,128)(2,1)S(1)}, bf16[2,16,16,128]{3,2,1,0:T(8,128)(2,1)S(1)}, u32[]{:S(2)}, u32[]{:S(2)}) collective-permute-start(bf16[2,16,16,128]{3,2,1,0:T(8,128)(2,1)S(1)} %get-tuple-element.52), channel_id=1, source_target_pairs={{1,0},{2,1},{3,2},{5,4},{6,5},{7,6},{9,8},{10,9},{11,10},{13,12},{... | collective-permute-start | bytes 393224 | tf_op jit(solution)/shard_map/ppermute | solution.py:24
  76.4 11.7 %collective-permute-start.6 = (bf16[2,16,16,128]{3,2,1,0:T(8,128)(2,1)S(1)}, bf16[2,16,16,128]{3,2,1,0:T(8,128)(2,1)S(1)}, u32[]{:S(2)}, u32[]{:S(2)}) collective-permute-start(bf16[2,16,16,128]{3,2,1,0:T(8,128)(2,1)S(1)} %get-tuple-element.51), channel_id=1, source_target_pairs={{0,1},{1,2},{2,3},{4,5},{5,6},{6,7},{8,9},{9,10},{10,11},{12,13},{... | collective-permute-start | bytes 393224 | tf_op jit(solution)/shard_map/ppermute | solution.py:21
  88.1 1.0 copy-start.1
  89.6 0.7 copy-start.5
  89.6 0.7 copy-start.6
  92.7 19.1 %collective-permute-start.8 = (bf16[2,16,8,512]{3,2,1,0:T(8,128)(2,1)S(1)}, bf16[2,16,8,512]{3,2,1,0:T(8,128)(2,1)S(1)}, u32[]{:S(2)}, u32[]{:S(2)}) collective-permute-start(bf16[2,16,8,512]{3,2,1,0:T(8,128)(2,1)S(1)} %get-tuple-element.50), channel_id=1, source_target_pairs={{0,16},{4,20},{8,24},{12,28},{16,0},{20,4},{24,8},{28,12},{32,48},... | collective-permute-start | bytes 786440 | tf_op jit(solution)/shard_map/ppermute | solution.py:13
  112.1 13.0 %collective-permute-start.10 = (bf16[2,16,16,128]{3,2,1,0:T(8,128)(2,1)S(1)}, bf16[2,16,16,128]{3,2,1,0:T(8,128)(2,1)S(1)}, u32[]{:S(2)}, u32[]{:S(2)}) collective-permute-start(bf16[2,16,16,128]{3,2,1,0:T(8,128)(2,1)S(1)} %get-tuple-element.48), channel_id=1, source_target_pairs={{1,0},{2,1},{3,2},{5,4},{6,5},{7,6},{9,8},{10,9},{11,10},{13,12},{... | collective-permute-start | bytes 393224 | tf_op jit(solution)/shard_map/ppermute | solution.py:24
  114.4 10.7 %collective-permute-start.9 = (bf16[2,16,16,128]{3,2,1,0:T(8,128)(2,1)S(1)}, bf16[2,16,16,128]{3,2,1,0:T(8,128)(2,1)S(1)}, u32[]{:S(2)}, u32[]{:S(2)}) collective-permute-start(bf16[2,16,16,128]{3,2,1,0:T(8,128)(2,1)S(1)} %get-tuple-element.47), channel_id=1, source_target_pairs={{0,1},{1,2},{2,3},{4,5},{5,6},{6,7},{8,9},{9,10},{10,11},{12,13},{... | collective-permute-start | bytes 393224 | tf_op jit(solution)/shard_map/ppermute | solution.py:21
  126.2 0.7 copy-start.4
  129.3 14.7 %collective-permute-start.11 = (bf16[2,16,8,512]{3,2,1,0:T(8,128)(2,1)S(1)}, bf16[2,16,8,512]{3,2,1,0:T(8,128)(2,1)S(1)}, u32[]{:S(2)}, u32[]{:S(2)}) collective-permute-start(bf16[2,16,8,512]{3,2,1,0:T(8,128)(2,1)S(1)} %get-tuple-element.46), channel_id=1, source_target_pairs={{0,8},{4,12},{8,0},{12,4},{16,24},{20,28},{24,16},{28,20},{32,40},... | collective-permute-start | bytes 786440 | tf_op jit(solution)/shard_map/ppermute | solution.py:13
where the time goes:
time: 146 us; the launch traced here: 145 us
  waiting for transfers between devices  47.6 us (33%)
  starting transfers between devices  38.6 us (26%)
  between operations  30.9 us (21%)
  other arithmetic  13.5 us (9%)
  local copies, waits for them, and re-layouts  10.8 us (7%)
  matrix products  3.54 us (2%)
    ppermute x4, waiting for transfers between devices, swapped(): return lax.ppermute(value, axis, pairs)  47.6 us
    ppermute x4, starting transfers between devices, extended(): lax.ppermute(lax.slice_in_dim(block, 0, width, axis=dim), axis, backward)  15.8 us
    ppermute x4, starting transfers between devices, extended(): lax.ppermute(lax.slice_in_dim(block, block.shape[dim] - width, None, axis...  11.7 us
    ppermute x4, starting transfers between devices, swapped(): return lax.ppermute(value, axis, pairs)  11 us
    another operation x4, other arithmetic  9.11 us
    unnamed x38, local copies, waits for them, and re-layouts  2.92 us
  transfers between devices with their start and end apart: 12, of which 4 were waited for; matrix products, arithmetic and copies ran while one was open for 4% of the time, Pallas kernels for 0%

commit v1 on v0

v1 whole, which is shorter than its diff:
```python
import functools
import jax
import jax.numpy as jnp
from jax import lax
from jax.experimental import pallas as pl
from jax.experimental.pallas import tpu as pltpu
from jax.sharding import PartitionSpec as P

TILE = 128
LEVELS = 4
CHANNELS = 16
BEAMS = 8
PART = CHANNELS * BEAMS
BITS = (4, 3, 2, 1)
BLOCK = 512
TILES = BLOCK // TILE
VMEM_LIMIT = 24 * 1024 * 1024
BF = jnp.bfloat16
F32 = jnp.float32
VMEM = pl.BlockSpec(memory_space=pltpu.VMEM)


def call(kernel, out_shape, count, flops, name, scratch=()):
    return pl.pallas_call(
        kernel,
        out_shape=out_shape,
        in_specs=[VMEM] * count,
        out_specs=[VMEM] * len(out_shape),
        scratch_shapes=list(scratch),
        compiler_params=pltpu.CompilerParams(vmem_limit_bytes=VMEM_LIMIT),
        cost_estimate=pl.CostEstimate(flops=flops, bytes_accessed=1 << 20, transcendentals=0),
        name=name,
    )


def shape(*dims, dtype=BF):
    return jax.ShapeDtypeStruct(dims, dtype)


def is_odd():
    return lax.axis_index("range") % 2 == 1


def bit_of(level):
    return lax.axis_index("pulse") // 2 ** BITS[level] % 2


def aligned(lane):
    return pl.multiple_of(lane, TILE)


def sincos(theta):
    turns = jnp.round(theta * 0.6366197723675814)
    rest = theta - turns * 1.5703125
    rest = rest - turns * 4.837512969970703e-4
    rest = rest - turns * 7.549789948768648e-8
    sq = rest * rest
    sine = rest + rest * sq * (-1.6666654611e-1 + sq * (8.3321608736e-3 - sq * 1.9515295891e-4))
    cosine = 1.0 - 0.5 * sq + sq * sq * (
        4.166664568298827e-2 + sq * (-1.388731625493765e-3 + sq * 2.443315711809948e-5)
    )
    quarter = turns.astype(jnp.int32)
    odd = (quarter & 1) == 1
    sin_sign = (quarter & 2) == 2
    cos_sign = ((quarter + 1) & 2) == 2
    out_sin = jnp.where(odd, cosine, sine)
    out_cos = jnp.where(odd, sine, cosine)
    return jnp.where(sin_sign, -out_sin, out_sin), jnp.where(cos_sign, -out_cos, out_cos)


def tables_kernel(level, taps, offsets, ramp, ids, scale, beam, shifted, cos_ref, sin_ref, mix_ref):
    row = lax.broadcasted_iota(jnp.int32, (2 * TILE, 3 * TILE), 0)
    col = lax.broadcasted_iota(jnp.int32, (2 * TILE, 3 * TILE), 1)
    gap = (col - row).astype(F32) - TILE // 2
    moves = offsets[...].astype(F32)
    for tile in range(TILES):
        pick = jnp.where(gap == moves[level : level + 1, tile : tile + 1], 1.0, 0.0).astype(BF)
        flat = taps[0, tile].reshape(2 * TILE, 2 * TILE)
        shifted[tile] = jnp.dot(flat, pick, preferred_element_type=F32).astype(BF)

    phase = jnp.zeros((1, CHANNELS), F32)
    for baseline in range(8):
        phase = phase + jnp.where(ids[...] == baseline, scale[:, baseline : baseline + 1], 0.0)
    bit = bit_of(level)
    angles = ramp[0, 0].astype(F32)
    sent = jnp.where(bit == 1, angles[0], angles[1])
    held = jnp.where(bit == 1, angles[1], angles[0])
    for channel in range(CHANNELS):
        length = phase[:, channel : channel + 1]
        for side, angle in enumerate((sent, held)):
            sine, cosine = sincos(angle * length)
            at = pl.ds(side * PART + channel * BEAMS, BEAMS)
            cos_ref[at, :] = cosine
            sin_ref[at, :] = sine

    size = 2 * PART
    row = lax.broadcasted_iota(jnp.int32, (size, 16), 0)
    want = lax.broadcasted_iota(jnp.int32, (size, 16), 1)
    child = jnp.where(row // PART == 1, bit, 1 - bit)
    choose = jnp.where(want == child * BEAMS + row % BEAMS, 1.0, 0.0).astype(BF)
    beams = beam[0, 0].astype(F32).reshape(16, 16).astype(BF)
    rows = jnp.dot(choose, beams, preferred_element_type=F32).astype(BF)
    have = lax.broadcasted_iota(jnp.int32, (16, size), 0)
    col = lax.broadcasted_iota(jnp.int32, (16, size), 1)
    if level == 0:
        source = col % 16
    else:
        before = bit_of(level - 1)
        source = jnp.where(col // PART == 0, before, 1 - before) * BEAMS + col % BEAMS
    spread = jnp.where(have == source, 1.0, 0.0).astype(BF)
    full = jnp.dot(rows, spread, preferred_element_type=F32)
    at_row = lax.broadcasted_iota(jnp.int32, (size, size), 0) // BEAMS % CHANNELS
    at_col = lax.broadcasted_iota(jnp.int32, (size, size), 1)
    at_col = at_col // 16 if level == 0 else at_col // BEAMS % CHANNELS
    mix_ref[...] = jnp.where(at_row == at_col, full, 0.0).astype(BF)


def make_tables(level, taps, offsets, ramp, ids, scale, beam_mix):
    part = pl.BlockSpec((1, TILES, 2, TILE, 2 * TILE), lambda i: (level, 0, 0, 0, 0))
    angle = pl.BlockSpec((1, 1, 2, BEAMS, BLOCK), lambda i: (level, 0, 0, 0, 0))
    beam = pl.BlockSpec((1, 1, 2, BEAMS, 16), lambda i: (level, 0, 0, 0, 0))
    angles = shape(2 * PART, BLOCK, dtype=F32)
    return pl.pallas_call(
        functools.partial(tables_kernel, level),
        grid=(1,),
        out_shape=[shape(TILES, 2 * TILE, 3 * TILE), angles, angles, shape(2 * PART, 2 * PART)],
        in_specs=[part, VMEM, angle, VMEM, VMEM, beam],
        out_specs=[VMEM] * 4,
        compiler_params=pltpu.CompilerParams(vmem_limit_bytes=VMEM_LIMIT),
        cost_estimate=pl.CostEstimate(flops=1 << 27, bytes_accessed=1 << 21, transcendentals=0),
        name=f"tables{level}",
    )(taps, offsets, ramp, ids, scale, beam_mix)


def merge(spread, shifted, cos_ref, sin_ref, mix_ref, write):
    rows = 2 * PART
    mix = mix_ref[...]
    parts = []
    for tile in range(TILES):
        window = spread[:, tile * TILE : (tile + 3) * TILE]
        both = lax.dot_general(window, shifted[tile], (((1,), (1,)), ((), ())), preferred_element_type=F32)
        real = both[:rows, :TILE] - both[rows:, TILE:]
        imag = both[:rows, TILE:] + both[rows:, :TILE]
        parts.append(jnp.concatenate([real, imag], axis=1).astype(BF))
    for tile in range(TILES):
        lanes = slice(tile * TILE, (tile + 1) * TILE)
        mixed = jnp.dot(mix, parts[tile], preferred_element_type=F32)
        mixed_re = mixed[:, :TILE]
        mixed_im = mixed[:, TILE:]
        cosine = cos_ref[:, lanes]
        sine = sin_ref[:, lanes]
        out_re = (mixed_re * cosine + mixed_im * sine).astype(BF)
        out_im = (mixed_im * cosine - mixed_re * sine).astype(BF)
        write(lanes, out_re, out_im)


def level_kernel(level, *refs):
    count = 3 if level == 0 else 6
    data, rest = refs[:count], refs[count:]
    tables, rest = rest[:4], rest[4:]
    *outs, spread = rest
    odd = is_odd()
    near = pl.ds(aligned(jnp.where(odd, 0, BLOCK + TILE)), TILE)
    far = pl.ds(aligned(jnp.where(odd, BLOCK + TILE, 0)), TILE)
    middle = pl.ds(TILE, BLOCK)
    if level == 0:
        block, near_edge, far_edge = data
        for z in range(2):
            rows = pl.ds(2 * z * PART, 2 * PART)
            spread[rows, middle] = block[z].reshape(2 * PART, BLOCK)
            spread[rows, near] = near_edge[z].reshape(2 * PART, TILE)
            spread[rows, far] = far_edge[z].reshape(2 * PART, TILE)
    else:
        for side in range(2):
            block, near_edge, far_edge = data[3 * side : 3 * side + 3]
            for z in range(2):
                rows = pl.ds((2 * z + side) * PART, PART)
                spread[rows, middle] = block[z]
                spread[rows, near] = near_edge[z]
                spread[rows, far] = far_edge[z]
    edges = level < LEVELS - 1
    held, sent = outs[0], outs[3 if edges else 1]

    def write(lanes, out_re, out_im):
        for z, value in enumerate((out_re, out_im)):
            sent[z, :, lanes] = value[:PART]
            held[z, :, lanes] = value[PART:]

    merge(spread, *tables, write)
    if edges:
        high = pl.ds(aligned(jnp.where(odd, 0, BLOCK - TILE)), TILE)
        low = pl.ds(aligned(jnp.where(odd, BLOCK - TILE, 0)), TILE)
        for block, near_edge, far_edge in (outs[:3], outs[3:]):
            near_edge[...] = block[:, :, high]
            far_edge[...] = block[:, :, low]


def level_call(level, data, tables):
    edge = shape(2, PART, TILE)
    block = shape(2, PART, BLOCK)
    outs = [block] * 2 if level == LEVELS - 1 else [block, edge, edge] * 2
    operands = (*data, *tables)
    return call(
        functools.partial(level_kernel, level),
        outs,
        len(operands),
        TILES * 2 * (4 * PART * 384 * 256 + 4 * PART * PART * 256),
        f"merge{level}",
        [pltpu.VMEM((4 * PART, BLOCK + 2 * TILE), BF)],
    )(*operands)


def body(grad_image, range_kernel, band_offsets, beam_mix, ramp, baseline_ids, baseline_scale):
    pulses = lax.axis_size("pulse")
    ranges = lax.axis_size("range")
    near_pairs = [(i, i ^ 1) for i in range(ranges)]
    far_pairs = [(i, i + 1) for i in range(1, ranges - 1, 2)]
    far_pairs += [(t, s) for s, t in far_pairs]

    def move(value, mask, pairs):
        pairs = [(p * ranges + s, (p ^ mask) * ranges + t) for p in range(pulses) for s, t in pairs]
        return lax.ppermute(value, ("pulse", "range"), pairs)

    block = grad_image[0]
    low = block[..., :TILE]
    high = block[..., BLOCK - TILE :]
    odd = is_odd()
    far_edge = move(jnp.where(odd, high, low), 0, far_pairs)
    near_edge = move(jnp.where(odd, low, high), 0, near_pairs)
    state = (block, near_edge, far_edge)
    for level in range(LEVELS):
        tables = make_tables(
            level, range_kernel, band_offsets, ramp, baseline_ids[None], baseline_scale[None], beam_mix
        )
        outs = level_call(level, state, tables)
        mask = 2 ** BITS[level]
        stay = [(i, i) for i in range(ranges)]
        if level < LEVELS - 1:
            held, held_near, held_far, sent, sent_near, sent_far = outs
            got = move(sent, mask, stay)
            state = (
                held,
                move(held_near, 0, near_pairs),
                move(held_far, 0, far_pairs),
                got,
                move(sent_near, mask, near_pairs),
                move(sent_far, mask, far_pairs),
            )
        else:
            held, sent = outs
            got = move(sent, mask, stay)

    held = held.reshape(2, CHANNELS, BEAMS, BLOCK)
    got = got.reshape(2, CHANNELS, BEAMS, BLOCK)
    mine = bit_of(LEVELS - 1) == 1
    return jnp.concatenate([jnp.where(mine, got, held), jnp.where(mine, held, got)], axis=2)[None]


def solution(mesh):
    placed = (
        P("pulse", None, None, None, "range"),
        P(None, "range", None, None, None),
        P(None, "range"),
        P(None, "pulse", None, None, None),
        P(None, "pulse", None, None, "range"),
        P(),
        P(),
    )
    return jax.shard_map(
        body,
        mesh=mesh,
        in_specs=placed,
        out_specs=P("pulse", None, None, None, "range"),
        check_vma=False,
    )
```

time: 146 us -> 94 us (0.64)
  between operations: 30.9 us -> 0.37 us
  waiting for transfers between devices: 47.6 us -> 17.5 us
  starting transfers between devices: 38.6 us -> 59 us
  other arithmetic: 13.5 us -> 1.94 us
  Pallas kernels: 0 us -> 9.23 us
  local copies, waits for them, and re-layouts: 10.8 us -> 5.15 us
  matrix products: 3.54 us -> 0 us
    ppermute x12 -> x18, waiting for transfers between devices: 47.6 us -> 17.5 us  [move(): return lax.ppermute(value, ('pulse', 'range'), pairs)]
    ppermute x12 -> x18, starting transfers between devices: 38.6 us -> 59 us  [move(): return lax.ppermute(value, ('pulse', 'range'), pairs)]
    another operation x8 -> x0, other arithmetic: 9.32 us -> none
    pallas_call x0 -> x8, Pallas kernels: none -> 9.23 us  [the longest x4 5.05 us: make_tables(): pl.pallas_call(functools.partial(tables_kernel, level), grid=(1,), out_sh...]
    another operation x4 -> x0, local copies, waits for them, and re-layouts: 4.25 us -> none  [the longest x1 2.91 us: body(): jnp.stack([jnp.stack([kern_re, kern_im], 1), jnp.stack([-kern_im, kern_re...]
    dot_general x12 -> x0, matrix products: 3.54 us -> none  [the longest x4 1.88 us: body(): jnp.einsum('tzcmk,tzwok->wcmto', windows, combined, preferred_element_typ...]
    slice x6 -> x0, local copies, waits for them, and re-layouts: 3.13 us -> none  [the longest x4 1.78 us: extended(): lax.slice_in_dim(block, block.shape[dim] - width, None, axis=dim)]
    unnamed x38 -> x20, local copies, waits for them, and re-layouts: 2.92 us -> 5.15 us
  transfers between devices with their start and end apart: 12 -> 18, of which waited for: 4 -> 5; matrix products, arithmetic and copies ran while one was open for 4% -> 0% of each run, Pallas kernels for 0% -> 5%
where the time goes in v1:
time: 94 us; the launch traced here: 93.2 us
  starting transfers between devices  59 us (63%)
  waiting for transfers between devices  17.5 us (19%)
  Pallas kernels  9.23 us (10%)
  local copies, waits for them, and re-layouts  5.15 us (5%)
  other arithmetic  1.94 us (2%)
    ppermute x18, starting transfers between devices, move(): return lax.ppermute(value, ('pulse', 'range'), pairs)  59 us
    ppermute x18, waiting for transfers between devices, move(): return lax.ppermute(value, ('pulse', 'range'), pairs)  17.5 us
    unnamed x20, local copies, waits for them, and re-layouts  5.15 us
    pallas_call x4, Pallas kernels, make_tables(): pl.pallas_call(functools.partial(tables_kernel, level), grid=(1,), out_sh...  5.05 us
    pallas_call x4, Pallas kernels, level_call(): call(functools.partial(level_kernel, level), outs, len(operands), TILES *...  4.18 us
  transfers between devices with their start and end apart: 18, of which 5 were waited for; matrix products, arithmetic and copies ran while one was open for 0% of the time, Pallas kernels for 5%

profile of v1, /device:TPU:1, one launch (start us, length us, event | category | flops | bytes accessed | tf_op | source)
XLA Modules:
  0.0 93.2 jit_solution(7137187018333079421)
XLA Ops:
  0.0 0.0 copy-start.2
  0.0 1.1 %broadcast_select_fusion = (bf16[2,16,16,128]{3,2,1,0:T(8,128)(2,1)S(1)}, bf16[2,16,16,128]{3,2,1,0:T(8,128)(2,1)S(1)}) fusion(pred[]{:T(512)S(6)} %eq.10, bf16[2,16,16,512]{3,2,1,0:T(8,128)(2,1)} %bitcast.9), kind=kLoop, calls=%fused_computation.3 | loop fusion | flops 131072 | bytes 524289 | tf_op jit(solution)/shard_map/jit(_where)/select_n | solution.py:228
  1.1 8.8 %collective-permute-start = (bf16[2,16,16,128]{3,2,1,0:T(8,128)(2,1)S(1)}, bf16[2,16,16,128]{3,2,1,0:T(8,128)(2,1)S(1)}, u32[]{:S(2)}, u32[]{:S(2)}) collective-permute-start(bf16[2,16,16,128]{3,2,1,0:T(8,128)(2,1)S(1)} %get-tuple-element.80), channel_id=1, source_target_pairs={{0,1},{1,0},{2,3},{3,2},{4,5},{5,4},{6,7},{7,6},{8,9},{9,8},{10,11... | collective-permute-start | bytes 393224 | tf_op jit(solution)/shard_map/ppermute | solution.py:222
  9.9 1.9 %collective-permute-start.1 = (bf16[2,16,16,128]{3,2,1,0:T(8,128)(2,1)S(1)}, bf16[2,16,16,128]{3,2,1,0:T(8,128)(2,1)S(1)}, u32[]{:S(2)}, u32[]{:S(2)}) collective-permute-start(bf16[2,16,16,128]{3,2,1,0:T(8,128)(2,1)S(1)} %get-tuple-element.79), channel_id=1, source_target_pairs={{1,2},{2,1},{5,6},{6,5},{9,10},{10,9},{13,14},{14,13},{17,18},{18,... | collective-permute-start | bytes 393224 | tf_op jit(solution)/shard_map/ppermute | solution.py:222
  11.8 0.0 copy-start
  11.8 1.6 %copy-done = bf16[4,4,2,128,256]{4,3,2,1,0:T(8,128)(2,1)S(1)} copy-done((bf16[4,4,2,128,256]{4,3,2,1,0:T(8,128)(2,1)S(1)}, bf16[4,4,2,128,256]{4,3,2,1,0:T(8,128)(2,1)}, u32[]{:S(2)}) %copy-start) | copy-done | bytes 2097176
  13.4 0.0 copy-start.3
  13.4 0.8 copy-done.3
  14.2 0.0 copy-start.5
  14.2 0.7 copy-done.5
  14.9 0.0 copy-start.7
  14.9 0.7 copy-done.7
  15.6 0.0 copy-start.8
  15.6 0.7 copy-done.8
  16.3 0.7 copy-done.9
  16.9 1.3 %tables0.1 = (bf16[4,256,384]{2,1,0:T(8,128)(2,1)S(1)}, f32[256,512]{1,0:T(8,128)S(1)}, f32[256,512]{1,0:T(8,128)S(1)}, bf16[256,256]{1,0:T(8,128)(2,1)S(1)}) custom-call(bf16[4,4,2,128,256]{4,3,2,1,0:T(8,128)(2,1)S(1)} %copy-done, s32[4,4]{1,0:T(4,128)S(1)} %copy-done.7, bf16[4,1,2,8,512]{4,3,2,1,0:T(8,128)(2,1)S(1)} %copy-done.3, s32[1,16]{1,0:T(1,128)S(1)} %bitcast.11, ...), custom_call_target="tpu_custom_call" | custom-call | flops 134217728 | bytes 2097152 | tf_op jit(solution)/shard_map/tables0/pallas_call | solution.py:123
  18.2 0.0 collective-permute-done.refs_1_
  18.2 0.0 collective-permute-done.1.refs_2_
  18.2 0.0 copy-done.2
  18.2 1.1 %merge0.1 = (bf16[2,128,512]{2,1,0:T(8,128)(2,1)S(1)}, bf16[2,128,128]{2,1,0:T(8,128)(2,1)S(1)}, bf16[2,128,128]{2,1,0:T(8,128)(2,1)S(1)}, bf16[2,128,512]{2,1,0...) custom-call(bf16[2,16,16,512]{3,2,1,0:T(8,128)(2,1)S(1)} %bitcast.10, ...), custom_call_target="tpu_custom_call" | custom-call | flops 536870912 | bytes 1048576 | tf_op jit(solution)/shard_map/merge0/pallas_call | solution.py:203
  19.3 1.9 %collective-permute-start.4 = (bf16[2,128,512]{2,1,0:T(8,128)(2,1)S(1)}, bf16[2,128,512]{2,1,0:T(8,128)(2,1)S(1)}, u32[]{:S(2)}, u32[]{:S(2)}) collective-permute-start(bf16[2,128,512]{2,1,0:T(8,128)(2,1)S(1)} %get-tuple-element.48), channel_id=1, source_target_pairs={{0,64},{1,65},{2,66},{3,67},{4,68},{5,69},{6,70},{7,71},{8,72},{9,... | collective-permute-start | bytes 786440 | tf_op jit(solution)/shard_map/ppermute | solution.py:222
  21.2 1.9 %collective-permute-start.2 = (bf16[2,128,128]{2,1,0:T(8,128)(2,1)S(1)}, bf16[2,128,128]{2,1,0:T(8,128)(2,1)S(1)}, u32[]{:S(2)}, u32[]{:S(2)}) collective-permute-start(bf16[2,128,128]{2,1,0:T(8,128)(2,1)S(1)} %get-tuple-element.46), channel_id=1, source_target_pairs={{0,1},{1,0},{2,3},{3,2},{4,5},{5,4},{6,7},{7,6},{8,9},{9,8},{10,11... | collective-permute-start | bytes 196616 | tf_op jit(solution)/shard_map/ppermute | solution.py:222
  23.2 3.6 %collective-permute-start.3 = (bf16[2,128,128]{2,1,0:T(8,128)(2,1)S(1)}, bf16[2,128,128]{2,1,0:T(8,128)(2,1)S(1)}, u32[]{:S(2)}, u32[]{:S(2)}) collective-permute-start(bf16[2,128,128]{2,1,0:T(8,128)(2,1)S(1)} %get-tuple-element.47), channel_id=1, source_target_pairs={{1,2},{2,1},{5,6},{6,5},{9,10},{10,9},{13,14},{14,13},{17,18},{18,... | collective-permute-start | bytes 196616 | tf_op jit(solution)/shard_map/ppermute | solution.py:222
  26.8 1.9 %collective-permute-start.5 = (bf16[2,128,128]{2,1,0:T(8,128)(2,1)S(1)}, bf16[2,128,128]{2,1,0:T(8,128)(2,1)S(1)}, u32[]{:S(2)}, u32[]{:S(2)}) collective-permute-start(bf16[2,128,128]{2,1,0:T(8,128)(2,1)S(1)} %get-tuple-element.49), channel_id=1, source_target_pairs={{0,65},{1,64},{2,67},{3,66},{4,69},{5,68},{6,71},{7,70},{8,73},{9,... | collective-permute-start | bytes 196616 | tf_op jit(solution)/shard_map/ppermute | solution.py:222
  28.7 0.0 copy-start.4
  28.8 0.0 copy-start.6
  28.8 4.4 %collective-permute-start.6 = (bf16[2,128,128]{2,1,0:T(8,128)(2,1)S(1)}, bf16[2,128,128]{2,1,0:T(8,128)(2,1)S(1)}, u32[]{:S(2)}, u32[]{:S(2)}) collective-permute-start(bf16[2,128,128]{2,1,0:T(8,128)(2,1)S(1)} %get-tuple-element.50), channel_id=1, source_target_pairs={{1,66},{2,65},{5,70},{6,69},{9,74},{10,73},{13,78},{14,77},{17,82}... | collective-permute-start | bytes 196616 | tf_op jit(solution)/shard_map/ppermute | solution.py:222
  33.2 0.0 copy-done.1
  33.2 1.3 %tables1.1 = (bf16[4,256,384]{2,1,0:T(8,128)(2,1)S(1)}, f32[256,512]{1,0:T(8,128)S(1)}, f32[256,512]{1,0:T(8,128)S(1)}, bf16[256,256]{1,0:T(8,128)(2,1)S(1)}) custom-call(bf16[4,4,2,128,256]{4,3,2,1,0:T(8,128)(2,1)S(1)} %copy-done.1, s32[4,4]{1,0:T(4,128)S(1)} %copy-done.7, bf16[4,1,2,8,512]{4,3,2,1,0:T(8,128)(2,1)S(1)} %copy-done.3, s32[1,16]{1,0:T(1,128)S(1)} %bitcast.12, ...), custom_call_target="tpu_custom_call" | custom-call | flops 134217728 | bytes 2097152 | tf_op jit(solution)/shard_map/tables1/pallas_call | solution.py:123
  34.5 0.0 collective-permute-done.2.refs_1_
  34.5 0.0 collective-permute-done.3.refs_2_
  34.5 1.9 %collective-permute-done.5.refs_4_ = bf16[2,128,128]{2,1,0:T(8,128)(2,1)S(1)} collective-permute-done((bf16[2,128,128]{2,1,0:T(8,128)(2,1)S(1)}, bf16[2,128,128]{2,1,0:T(8,128)(2,1)S(1)}, u32[]{:S(2)}, u32[]{:S(2)}) %collective-permute-start.5) | collective-permute-done | bytes 65568 | tf_op jit(solution)/shard_map/ppermute | solution.py:222
  36.4 0.0 collective-permute-done.6.refs_5_
  36.4 0.0 collective-permute-done.4.refs_3_
  36.4 1.1 %merge1.1 = (bf16[2,128,512]{2,1,0:T(8,128)(2,1)S(1)}, bf16[2,128,128]{2,1,0:T(8,128)(2,1)S(1)}, bf16[2,128,128]{2,1,0:T(8,128)(2,1)S(1)}, bf16[2,128,512]{2,1,0...) custom-call(bf16[2,128,512]{2,1,0:T(8,128)(2,1)S(1)} %get-tuple-element.45.refs_0_, ...), custom_call_target="tpu_custom_call" | custom-call | flops 536870912 | bytes 1048576 | tf_op jit(solution)/shard_map/merge1/pallas_call | solution.py:203
  37.5 2.8 %collective-permute-start.9 = (bf16[2,128,512]{2,1,0:T(8,128)(2,1)S(1)}, bf16[2,128,512]{2,1,0:T(8,128)(2,1)S(1)}, u32[]{:S(2)}, u32[]{:S(2)}) collective-permute-start(bf16[2,128,512]{2,1,0:T(8,128)(2,1)S(1)} %get-tuple-element.58), channel_id=1, source_target_pairs={{0,32},{1,33},{2,34},{3,35},{4,36},{5,37},{6,38},{7,39},{8,40},{9,... | collective-permute-start | bytes 786440 | tf_op jit(solution)/shard_map/ppermute | solution.py:222
  40.3 3.2 %collective-permute-start.10 = (bf16[2,128,128]{2,1,0:T(8,128)(2,1)S(1)}, bf16[2,128,128]{2,1,0:T(8,128)(2,1)S(1)}, u32[]{:S(2)}, u32[]{:S(2)}) collective-permute-start(bf16[2,128,128]{2,1,0:T(8,128)(2,1)S(1)} %get-tuple-element.59), channel_id=1, source_target_pairs={{0,33},{1,32},{2,35},{3,34},{4,37},{5,36},{6,39},{7,38},{8,41},{9,... | collective-permute-start | bytes 196616 | tf_op jit(solution)/shard_map/ppermute | solution.py:222
  43.4 3.5 %collective-permute-start.11 = (bf16[2,128,128]{2,1,0:T(8,128)(2,1)S(1)}, bf16[2,128,128]{2,1,0:T(8,128)(2,1)S(1)}, u32[]{:S(2)}, u32[]{:S(2)}) collective-permute-start(bf16[2,128,128]{2,1,0:T(8,128)(2,1)S(1)} %get-tuple-element.60), channel_id=1, source_target_pairs={{1,34},{2,33},{5,38},{6,37},{9,42},{10,41},{13,46},{14,45},{17,50}... | collective-permute-start | bytes 196616 | tf_op jit(solution)/shard_map/ppermute | solution.py:222
  46.9 1.9 %collective-permute-start.7 = (bf16[2,128,128]{2,1,0:T(8,128)(2,1)S(1)}, bf16[2,128,128]{2,1,0:T(8,128)(2,1)S(1)}, u32[]{:S(2)}, u32[]{:S(2)}) collective-permute-start(bf16[2,128,128]{2,1,0:T(8,128)(2,1)S(1)} %get-tuple-element.56), channel_id=1, source_target_pairs={{0,1},{1,0},{2,3},{3,2},{4,5},{5,4},{6,7},{7,6},{8,9},{9,8},{10,11... | collective-permute-start | bytes 196616 | tf_op jit(solution)/shard_map/ppermute | solution.py:222
  48.9 1.9 %collective-permute-start.8 = (bf16[2,128,128]{2,1,0:T(8,128)(2,1)S(1)}, bf16[2,128,128]{2,1,0:T(8,128)(2,1)S(1)}, u32[]{:S(2)}, u32[]{:S(2)}) collective-permute-start(bf16[2,128,128]{2,1,0:T(8,128)(2,1)S(1)} %get-tuple-element.57), channel_id=1, source_target_pairs={{1,2},{2,1},{5,6},{6,5},{9,10},{10,9},{13,14},{14,13},{17,18},{18,... | collective-permute-start | bytes 196616 | tf_op jit(solution)/shard_map/ppermute | solution.py:222
  50.8 0.0 copy-done.4
  50.8 0.0 copy-done.6
  50.8 1.3 %tables2.1 = (bf16[4,256,384]{2,1,0:T(8,128)(2,1)S(1)}, f32[256,512]{1,0:T(8,128)S(1)}, f32[256,512]{1,0:T(8,128)S(1)}, bf16[256,256]{1,0:T(8,128)(2,1)S(1)}) custom-call(bf16[4,4,2,128,256]{4,3,2,1,0:T(8,128)(2,1)S(1)} %copy-done.1, s32[4,4]{1,0:T(4,128)S(1)} %copy-done.7, bf16[4,1,2,8,512]{4,3,2,1,0:T(8,128)(2,1)S(1)} %copy-done.4, s32[1,16]{1,0:T(1,128)S(1)} %bitcast.13, ...), custom_call_target="tpu_custom_call" | custom-call | flops 134217728 | bytes 2097152 | tf_op jit(solution)/shard_map/tables2/pallas_call | solution.py:123
  52.1 0.0 collective-permute-done.10.refs_4_
  52.1 0.0 collective-permute-done.11.refs_5_
  52.1 0.0 collective-permute-done.7.refs_1_
  52.1 2.3 %collective-permute-done.8.refs_2_ = bf16[2,128,128]{2,1,0:T(8,128)(2,1)S(1)} collective-permute-done((bf16[2,128,128]{2,1,0:T(8,128)(2,1)S(1)}, bf16[2,128,128]{2,1,0:T(8,128)(2,1)S(1)}, u32[]{:S(2)}, u32[]{:S(2)}) %collective-permute-start.8) | collective-permute-done | bytes 65568 | tf_op jit(solution)/shard_map/ppermute | solution.py:222
  54.5 0.0 collective-permute-done.9.refs_3_
  54.5 1.1 %merge2.1 = (bf16[2,128,512]{2,1,0:T(8,128)(2,1)S(1)}, bf16[2,128,128]{2,1,0:T(8,128)(2,1)S(1)}, bf16[2,128,128]{2,1,0:T(8,128)(2,1)S(1)}, bf16[2,128,512]{2,1,0...) custom-call(bf16[2,128,512]{2,1,0:T(8,128)(2,1)S(1)} %get-tuple-element.55.refs_0_, ...), custom_call_target="tpu_custom_call" | custom-call | flops 536870912 | bytes 1048576 | tf_op jit(solution)/shard_map/merge2/pallas_call | solution.py:203
  55.5 5.2 %collective-permute-start.14 = (bf16[2,128,512]{2,1,0:T(8,128)(2,1)S(1)}, bf16[2,128,512]{2,1,0:T(8,128)(2,1)S(1)}, u32[]{:S(2)}, u32[]{:S(2)}) collective-permute-start(bf16[2,128,512]{2,1,0:T(8,128)(2,1)S(1)} %get-tuple-element.68), channel_id=1, source_target_pairs={{0,16},{1,17},{2,18},{3,19},{4,20},{5,21},{6,22},{7,23},{8,24},{9,... | collective-permute-start | bytes 786440 | tf_op jit(solution)/shard_map/ppermute | solution.py:222
  60.7 1.9 %collective-permute-start.12 = (bf16[2,128,128]{2,1,0:T(8,128)(2,1)S(1)}, bf16[2,128,128]{2,1,0:T(8,128)(2,1)S(1)}, u32[]{:S(2)}, u32[]{:S(2)}) collective-permute-start(bf16[2,128,128]{2,1,0:T(8,128)(2,1)S(1)} %get-tuple-element.66), channel_id=1, source_target_pairs={{0,1},{1,0},{2,3},{3,2},{4,5},{5,4},{6,7},{7,6},{8,9},{9,8},{10,11... | collective-permute-start | bytes 196616 | tf_op jit(solution)/shard_map/ppermute | solution.py:222
  62.6 3.1 %collective-permute-start.13 = (bf16[2,128,128]{2,1,0:T(8,128)(2,1)S(1)}, bf16[2,128,128]{2,1,0:T(8,128)(2,1)S(1)}, u32[]{:S(2)}, u32[]{:S(2)}) collective-permute-start(bf16[2,128,128]{2,1,0:T(8,128)(2,1)S(1)} %get-tuple-element.67), channel_id=1, source_target_pairs={{1,2},{2,1},{5,6},{6,5},{9,10},{10,9},{13,14},{14,13},{17,18},{18,... | collective-permute-start | bytes 196616 | tf_op jit(solution)/shard_map/ppermute | solution.py:222
  65.8 1.9 %collective-permute-start.15 = (bf16[2,128,128]{2,1,0:T(8,128)(2,1)S(1)}, bf16[2,128,128]{2,1,0:T(8,128)(2,1)S(1)}, u32[]{:S(2)}, u32[]{:S(2)}) collective-permute-start(bf16[2,128,128]{2,1,0:T(8,128)(2,1)S(1)} %get-tuple-element.69), channel_id=1, source_target_pairs={{0,17},{1,16},{2,19},{3,18},{4,21},{5,20},{6,23},{7,22},{8,25},{9,... | collective-permute-start | bytes 196616 | tf_op jit(solution)/shard_map/ppermute | solution.py:222
  67.7 6.1 %collective-permute-start.16 = (bf16[2,128,128]{2,1,0:T(8,128)(2,1)S(1)}, bf16[2,128,128]{2,1,0:T(8,128)(2,1)S(1)}, u32[]{:S(2)}, u32[]{:S(2)}) collective-permute-start(bf16[2,128,128]{2,1,0:T(8,128)(2,1)S(1)} %get-tuple-element.70), channel_id=1, source_target_pairs={{1,18},{2,17},{5,22},{6,21},{9,26},{10,25},{13,30},{14,29},{17,2},... | collective-permute-start | bytes 196616 | tf_op jit(solution)/shard_map/ppermute | solution.py:222
  73.8 1.3 %tables3.1 = (bf16[4,256,384]{2,1,0:T(8,128)(2,1)S(1)}, f32[256,512]{1,0:T(8,128)S(1)}, f32[256,512]{1,0:T(8,128)S(1)}, bf16[256,256]{1,0:T(8,128)(2,1)S(1)}) custom-call(bf16[4,4,2,128,256]{4,3,2,1,0:T(8,128)(2,1)S(1)} %copy-done.1, s32[4,4]{1,0:T(4,128)S(1)} %copy-done.7, bf16[4,1,2,8,512]{4,3,2,1,0:T(8,128)(2,1)S(1)} %copy-done.4, s32[1,16]{1,0:T(1,128)S(1)} %bitcast.14, ...), custom_call_target="tpu_custom_call" | custom-call | flops 134217728 | bytes 2097152 | tf_op jit(solution)/shard_map/tables3/pallas_call | solution.py:123
  75.1 0.0 collective-permute-done.12.refs_1_
  75.1 0.0 collective-permute-done.13.refs_2_
  75.1 0.2 collective-permute-done.15.refs_4_
  75.3 2.8 %collective-permute-done.16.refs_5_ = bf16[2,128,128]{2,1,0:T(8,128)(2,1)S(1)} collective-permute-done((bf16[2,128,128]{2,1,0:T(8,128)(2,1)S(1)}, bf16[2,128,128]{2,1,0:T(8,128)(2,1)S(1)}, u32[]{:S(2)}, u32[]{:S(2)}) %collective-permute-start.16) | collective-permute-done | bytes 65568 | tf_op jit(solution)/shard_map/ppermute | solution.py:222
  78.1 0.0 collective-permute-done.14.refs_3_
  78.1 1.0 %merge3.1 = (bf16[2,128,512]{2,1,0:T(8,128)(2,1)S(1)}, bf16[2,128,512]{2,1,0:T(8,128)(2,1)S(1)}) custom-call(bf16[2,128,512]{2,1,0:T(8,128)(2,1)S(1)} %get-tuple-element.65.refs_0_, bf16[2,128,128]{2,1,0:T(8,128)(2,1)S(1)} %collective-permute-done.12.refs_1_, bf16[2,128,128]{2,1,0:T(8,128)(2,1)S(1)} %collective-permute-done.13.refs_2_, ...), custom_call_target="tpu_custom_call" | custom-call | flops 536870912 | bytes 1048576 | tf_op jit(solution)/shard_map/merge3/pallas_call | solution.py:203
  79.1 3.0 %collective-permute-start.17 = (bf16[2,128,512]{2,1,0:T(8,128)(2,1)S(1)}, bf16[2,128,512]{2,1,0:T(8,128)(2,1)S(1)}, u32[]{:S(2)}, u32[]{:S(2)}) collective-permute-start(bf16[2,128,512]{2,1,0:T(8,128)(2,1)S(1)} %get-tuple-element.75), channel_id=1, source_target_pairs={{0,8},{1,9},{2,10},{3,11},{4,12},{5,13},{6,14},{7,15},{8,0},{9,1},... | collective-permute-start | bytes 786440 | tf_op jit(solution)/shard_map/ppermute | solution.py:222
  82.1 10.2 %collective-permute-done.17 = bf16[2,128,512]{2,1,0:T(8,128)(2,1)S(1)} collective-permute-done((bf16[2,128,512]{2,1,0:T(8,128)(2,1)S(1)}, bf16[2,128,512]{2,1,0:T(8,128)(2,1)S(1)}, u32[]{:S(2)}, u32[]{:S(2)}) %collective-permute-start.17) | collective-permute-done | bytes 262176 | tf_op jit(solution)/shard_map/ppermute | solution.py:222
  92.4 0.9 maximum_bitcast_fusion
  (3 shorter events, 0.0 us)
Async XLA Ops:
  0.0 18.2 %copy-start.2 = (bf16[1,2,16,16,512]{4,3,2,1,0:T(8,128)(2,1)S(1)}, bf16[1,2,16,16,512]{4,3,2,1,0:T(8,128)(2,1)}, u32[]{:S(2)}) copy-start(bf16[1,2,16,16,512]{4,3,2,1,0:T(8,128)(2,1)} %param.7) | copy-start | bytes 1572868
  1.1 17.1 %collective-permute-start = (bf16[2,16,16,128]{3,2,1,0:T(8,128)(2,1)S(1)}, bf16[2,16,16,128]{3,2,1,0:T(8,128)(2,1)S(1)}, u32[]{:S(2)}, u32[]{:S(2)}) collective-permute-start(bf16[2,16,16,128]{3,2,1,0:T(8,128)(2,1)S(1)} %get-tuple-element.80), channel_id=1, source_target_pairs={{0,1},{1,0},{2,3},{3,2},{4,5},{5,4},{6,7},{7,6},{8,9},{9,8},{10,11... | collective-permute-start | bytes 393224 | tf_op jit(solution)/shard_map/ppermute | solution.py:222
  9.9 8.4 %collective-permute-start.1 = (bf16[2,16,16,128]{3,2,1,0:T(8,128)(2,1)S(1)}, bf16[2,16,16,128]{3,2,1,0:T(8,128)(2,1)S(1)}, u32[]{:S(2)}, u32[]{:S(2)}) collective-permute-start(bf16[2,16,16,128]{3,2,1,0:T(8,128)(2,1)S(1)} %get-tuple-element.79), channel_id=1, source_target_pairs={{1,2},{2,1},{5,6},{6,5},{9,10},{10,9},{13,14},{14,13},{17,18},{18,... | collective-permute-start | bytes 393224 | tf_op jit(solution)/shard_map/ppermute | solution.py:222
  11.8 1.6 %copy-start = (bf16[4,4,2,128,256]{4,3,2,1,0:T(8,128)(2,1)S(1)}, bf16[4,4,2,128,256]{4,3,2,1,0:T(8,128)(2,1)}, u32[]{:S(2)}) copy-start(bf16[4,4,2,128,256]{4,3,2,1,0:T(8,128)(2,1)} %taps.7) | copy-start | bytes 6291460
  13.4 0.8 copy-start.3
  14.2 0.7 copy-start.5
  14.9 0.7 copy-start.7
  15.6 0.7 copy-start.8
  16.3 0.7 copy-start.9
  16.9 16.2 %copy-start.1 = (bf16[4,4,2,128,256]{4,3,2,1,0:T(8,128)(2,1)S(1)}, bf16[4,4,2,128,256]{4,3,2,1,0:T(8,128)(2,1)}, u32[]{:S(2)}) copy-start(bf16[4,4,2,128,256]{4,3,2,1,0:T(8,128)(2,1)} %taps.7) | copy-start | bytes 6291460
  19.3 17.1 %collective-permute-start.4 = (bf16[2,128,512]{2,1,0:T(8,128)(2,1)S(1)}, bf16[2,128,512]{2,1,0:T(8,128)(2,1)S(1)}, u32[]{:S(2)}, u32[]{:S(2)}) collective-permute-start(bf16[2,128,512]{2,1,0:T(8,128)(2,1)S(1)} %get-tuple-element.48), channel_id=1, source_target_pairs={{0,64},{1,65},{2,66},{3,67},{4,68},{5,69},{6,70},{7,71},{8,72},{9,... | collective-permute-start | bytes 786440 | tf_op jit(solution)/shard_map/ppermute | solution.py:222
  21.2 13.2 %collective-permute-start.2 = (bf16[2,128,128]{2,1,0:T(8,128)(2,1)S(1)}, bf16[2,128,128]{2,1,0:T(8,128)(2,1)S(1)}, u32[]{:S(2)}, u32[]{:S(2)}) collective-permute-start(bf16[2,128,128]{2,1,0:T(8,128)(2,1)S(1)} %get-tuple-element.46), channel_id=1, source_target_pairs={{0,1},{1,0},{2,3},{3,2},{4,5},{5,4},{6,7},{7,6},{8,9},{9,8},{10,11... | collective-permute-start | bytes 196616 | tf_op jit(solution)/shard_map/ppermute | solution.py:222
  23.2 11.3 %collective-permute-start.3 = (bf16[2,128,128]{2,1,0:T(8,128)(2,1)S(1)}, bf16[2,128,128]{2,1,0:T(8,128)(2,1)S(1)}, u32[]{:S(2)}, u32[]{:S(2)}) collective-permute-start(bf16[2,128,128]{2,1,0:T(8,128)(2,1)S(1)} %get-tuple-element.47), channel_id=1, source_target_pairs={{1,2},{2,1},{5,6},{6,5},{9,10},{10,9},{13,14},{14,13},{17,18},{18,... | collective-permute-start | bytes 196616 | tf_op jit(solution)/shard_map/ppermute | solution.py:222
  26.8 9.6 %collective-permute-start.5 = (bf16[2,128,128]{2,1,0:T(8,128)(2,1)S(1)}, bf16[2,128,128]{2,1,0:T(8,128)(2,1)S(1)}, u32[]{:S(2)}, u32[]{:S(2)}) collective-permute-start(bf16[2,128,128]{2,1,0:T(8,128)(2,1)S(1)} %get-tuple-element.49), channel_id=1, source_target_pairs={{0,65},{1,64},{2,67},{3,66},{4,69},{5,68},{6,71},{7,70},{8,73},{9,... | collective-permute-start | bytes 196616 | tf_op jit(solution)/shard_map/ppermute | solution.py:222
  28.7 22.1 %copy-start.4 = (bf16[4,1,2,8,512]{4,3,2,1,0:T(8,128)(2,1)S(1)}, bf16[4,1,2,8,512]{4,3,2,1,0:T(8,128)(2,1)}, u32[]{:S(2)}) copy-start(bf16[4,1,2,8,512]{4,3,2,1,0:T(8,128)(2,1)} %ramp.7) | copy-start | bytes 196612
  28.8 22.1 %copy-start.6 = (bf16[4,1,2,8,16]{4,3,2,1,0:T(8,128)(2,1)S(1)}, bf16[4,1,2,8,16]{4,3,2,1,0:T(8,128)(2,1)}, u32[]{:S(2)}) copy-start(bf16[4,1,2,8,16]{4,3,2,1,0:T(8,128)(2,1)} %beam.7) | copy-start | bytes 6148
  28.8 7.6 %collective-permute-start.6 = (bf16[2,128,128]{2,1,0:T(8,128)(2,1)S(1)}, bf16[2,128,128]{2,1,0:T(8,128)(2,1)S(1)}, u32[]{:S(2)}, u32[]{:S(2)}) collective-permute-start(bf16[2,128,128]{2,1,0:T(8,128)(2,1)S(1)} %get-tuple-element.50), channel_id=1, source_target_pairs={{1,66},{2,65},{5,70},{6,69},{9,74},{10,73},{13,78},{14,77},{17,82}... | collective-permute-start | bytes 196616 | tf_op jit(solution)/shard_map/ppermute | solution.py:222
  37.5 17.0 %collective-permute-start.9 = (bf16[2,128,512]{2,1,0:T(8,128)(2,1)S(1)}, bf16[2,128,512]{2,1,0:T(8,128)(2,1)S(1)}, u32[]{:S(2)}, u32[]{:S(2)}) collective-permute-start(bf16[2,128,512]{2,1,0:T(8,128)(2,1)S(1)} %get-tuple-element.58), channel_id=1, source_target_pairs={{0,32},{1,33},{2,34},{3,35},{4,36},{5,37},{6,38},{7,39},{8,40},{9,... | collective-permute-start | bytes 786440 | tf_op jit(solution)/shard_map/ppermute | solution.py:222
  40.3 11.8 %collective-permute-start.10 = (bf16[2,128,128]{2,1,0:T(8,128)(2,1)S(1)}, bf16[2,128,128]{2,1,0:T(8,128)(2,1)S(1)}, u32[]{:S(2)}, u32[]{:S(2)}) collective-permute-start(bf16[2,128,128]{2,1,0:T(8,128)(2,1)S(1)} %get-tuple-element.59), channel_id=1, source_target_pairs={{0,33},{1,32},{2,35},{3,34},{4,37},{5,36},{6,39},{7,38},{8,41},{9,... | collective-permute-start | bytes 196616 | tf_op jit(solution)/shard_map/ppermute | solution.py:222
  43.4 8.7 %collective-permute-start.11 = (bf16[2,128,128]{2,1,0:T(8,128)(2,1)S(1)}, bf16[2,128,128]{2,1,0:T(8,128)(2,1)S(1)}, u32[]{:S(2)}, u32[]{:S(2)}) collective-permute-start(bf16[2,128,128]{2,1,0:T(8,128)(2,1)S(1)} %get-tuple-element.60), channel_id=1, source_target_pairs={{1,34},{2,33},{5,38},{6,37},{9,42},{10,41},{13,46},{14,45},{17,50}... | collective-permute-start | bytes 196616 | tf_op jit(solution)/shard_map/ppermute | solution.py:222
  46.9 5.2 %collective-permute-start.7 = (bf16[2,128,128]{2,1,0:T(8,128)(2,1)S(1)}, bf16[2,128,128]{2,1,0:T(8,128)(2,1)S(1)}, u32[]{:S(2)}, u32[]{:S(2)}) collective-permute-start(bf16[2,128,128]{2,1,0:T(8,128)(2,1)S(1)} %get-tuple-element.56), channel_id=1, source_target_pairs={{0,1},{1,0},{2,3},{3,2},{4,5},{5,4},{6,7},{7,6},{8,9},{9,8},{10,11... | collective-permute-start | bytes 196616 | tf_op jit(solution)/shard_map/ppermute | solution.py:222
  48.9 5.6 %collective-permute-start.8 = (bf16[2,128,128]{2,1,0:T(8,128)(2,1)S(1)}, bf16[2,128,128]{2,1,0:T(8,128)(2,1)S(1)}, u32[]{:S(2)}, u32[]{:S(2)}) collective-permute-start(bf16[2,128,128]{2,1,0:T(8,128)(2,1)S(1)} %get-tuple-element.57), channel_id=1, source_target_pairs={{1,2},{2,1},{5,6},{6,5},{9,10},{10,9},{13,14},{14,13},{17,18},{18,... | collective-permute-start | bytes 196616 | tf_op jit(solution)/shard_map/ppermute | solution.py:222
  55.5 22.6 %collective-permute-start.14 = (bf16[2,128,512]{2,1,0:T(8,128)(2,1)S(1)}, bf16[2,128,512]{2,1,0:T(8,128)(2,1)S(1)}, u32[]{:S(2)}, u32[]{:S(2)}) collective-permute-start(bf16[2,128,512]{2,1,0:T(8,128)(2,1)S(1)} %get-tuple-element.68), channel_id=1, source_target_pairs={{0,16},{1,17},{2,18},{3,19},{4,20},{5,21},{6,22},{7,23},{8,24},{9,... | collective-permute-start | bytes 786440 | tf_op jit(solution)/shard_map/ppermute | solution.py:222
  60.7 14.4 %collective-permute-start.12 = (bf16[2,128,128]{2,1,0:T(8,128)(2,1)S(1)}, bf16[2,128,128]{2,1,0:T(8,128)(2,1)S(1)}, u32[]{:S(2)}, u32[]{:S(2)}) collective-permute-start(bf16[2,128,128]{2,1,0:T(8,128)(2,1)S(1)} %get-tuple-element.66), channel_id=1, source_target_pairs={{0,1},{1,0},{2,3},{3,2},{4,5},{5,4},{6,7},{7,6},{8,9},{9,8},{10,11... | collective-permute-start | bytes 196616 | tf_op jit(solution)/shard_map/ppermute | solution.py:222
  62.6 12.5 %collective-permute-start.13 = (bf16[2,128,128]{2,1,0:T(8,128)(2,1)S(1)}, bf16[2,128,128]{2,1,0:T(8,128)(2,1)S(1)}, u32[]{:S(2)}, u32[]{:S(2)}) collective-permute-start(bf16[2,128,128]{2,1,0:T(8,128)(2,1)S(1)} %get-tuple-element.67), channel_id=1, source_target_pairs={{1,2},{2,1},{5,6},{6,5},{9,10},{10,9},{13,14},{14,13},{17,18},{18,... | collective-permute-start | bytes 196616 | tf_op jit(solution)/shard_map/ppermute | solution.py:222
  65.8 9.5 %collective-permute-start.15 = (bf16[2,128,128]{2,1,0:T(8,128)(2,1)S(1)}, bf16[2,128,128]{2,1,0:T(8,128)(2,1)S(1)}, u32[]{:S(2)}, u32[]{:S(2)}) collective-permute-start(bf16[2,128,128]{2,1,0:T(8,128)(2,1)S(1)} %get-tuple-element.69), channel_id=1, source_target_pairs={{0,17},{1,16},{2,19},{3,18},{4,21},{5,20},{6,23},{7,22},{8,25},{9,... | collective-permute-start | bytes 196616 | tf_op jit(solution)/shard_map/ppermute | solution.py:222
  67.7 10.4 %collective-permute-start.16 = (bf16[2,128,128]{2,1,0:T(8,128)(2,1)S(1)}, bf16[2,128,128]{2,1,0:T(8,128)(2,1)S(1)}, u32[]{:S(2)}, u32[]{:S(2)}) collective-permute-start(bf16[2,128,128]{2,1,0:T(8,128)(2,1)S(1)} %get-tuple-element.70), channel_id=1, source_target_pairs={{1,18},{2,17},{5,22},{6,21},{9,26},{10,25},{13,30},{14,29},{17,2},... | collective-permute-start | bytes 196616 | tf_op jit(solution)/shard_map/ppermute | solution.py:222
  79.1 13.2 %collective-permute-start.17 = (bf16[2,128,512]{2,1,0:T(8,128)(2,1)S(1)}, bf16[2,128,512]{2,1,0:T(8,128)(2,1)S(1)}, u32[]{:S(2)}, u32[]{:S(2)}) collective-permute-start(bf16[2,128,512]{2,1,0:T(8,128)(2,1)S(1)} %get-tuple-element.75), channel_id=1, source_target_pairs={{0,8},{1,9},{2,10},{3,11},{4,12},{5,13},{6,14},{7,15},{8,0},{9,1},... | collective-permute-start | bytes 786440 | tf_op jit(solution)/shard_map/ppermute | solution.py:222

commit v2 on v1

--- a/solution.py
+++ b/solution.py
@@ -18,6 +18,12 @@
 BF = jnp.bfloat16
 F32 = jnp.float32
 VMEM = pl.BlockSpec(memory_space=pltpu.VMEM)
+ANYWHERE = pl.BlockSpec(memory_space=pl.ANY)
+WIDE = (0, 2)
+REACH = 2 * TILE
+KERNEL_AT = 32
+RAMP_AT = KERNEL_AT + 16 * len(WIDE)
+UNITS = RAMP_AT + len(WIDE)
 
 
 def call(kernel, out_shape, count, flops, name, scratch=()):
@@ -68,23 +74,60 @@
     return jnp.where(sin_sign, -out_sin, out_sin), jnp.where(cos_sign, -out_cos, out_cos)
 
 
-def tables_kernel(level, taps, offsets, ramp, ids, scale, beam, shifted, cos_ref, sin_ref, mix_ref):
+def edges_kernel(image, taps, ramp, offsets, near, far, moves, sems):
+    odd = is_odd()
+    near_lanes = pl.ds(aligned(jnp.where(odd, 0, BLOCK - REACH)), REACH)
+    far_lanes = pl.ds(aligned(jnp.where(odd, BLOCK - TILE, 0)), TILE)
+    ramp_lanes = pl.ds(aligned(jnp.where(odd, 0, BLOCK - TILE)), TILE)
+    copies = [(offsets, moves)]
+    for z in range(2):
+        copies.append((image.at[z, :, :, near_lanes], near.at[pl.ds(16 * z, 16)]))
+        copies.append((image.at[z, :, :, far_lanes], far.at[z]))
+    for at, level in enumerate(WIDE):
+        copies.append((taps.at[level, jnp.where(odd, 0, TILES - 1)], near.at[pl.ds(KERNEL_AT + 16 * at, 16)]))
+        copies.append((ramp.at[level, :, ramp_lanes], near.at[RAMP_AT + at, :, pl.ds(0, TILE)]))
+    copies = [pltpu.make_async_copy(s, t, sems.at[i]) for i, (s, t) in enumerate(copies)]
+    for copy in copies:
+        copy.start()
+    copies[0].wait()
+    values = moves[...].astype(F32)
+    for at, level in enumerate(WIDE):
+        row = values[level : level + 1]
+        value = jnp.where(odd, row[:, 0:1], row[:, TILES - 1 : TILES])
+        near[RAMP_AT + at, :, TILE:] = jnp.broadcast_to(value, (16, REACH - TILE)).astype(BF)
+    for copy in copies[1:]:
+        copy.wait()
+
+
+def take_edges(image, taps, ramp, offsets):
+    return pl.pallas_call(
+        edges_kernel,
+        out_shape=[shape(UNITS, 16, REACH), shape(2, CHANNELS, 2 * BEAMS, TILE)],
+        in_specs=[ANYWHERE] * 4,
+        out_specs=[VMEM] * 2,
+        scratch_shapes=[pltpu.VMEM((LEVELS, TILES), jnp.int32), pltpu.SemaphoreType.DMA((9,))],
+        compiler_params=pltpu.CompilerParams(vmem_limit_bytes=56 * 1024 * 1024),
+        cost_estimate=pl.CostEstimate(flops=1 << 20, bytes_accessed=1 << 20, transcendentals=0),
+        name="edges",
+    )(image, taps, ramp, offsets)
+
+
+def put_shifted(shifted, tile, taps, offset):
     row = lax.broadcasted_iota(jnp.int32, (2 * TILE, 3 * TILE), 0)
     col = lax.broadcasted_iota(jnp.int32, (2 * TILE, 3 * TILE), 1)
     gap = (col - row).astype(F32) - TILE // 2
-    moves = offsets[...].astype(F32)
-    for tile in range(TILES):
-        pick = jnp.where(gap == moves[level : level + 1, tile : tile + 1], 1.0, 0.0).astype(BF)
-        flat = taps[0, tile].reshape(2 * TILE, 2 * TILE)
-        shifted[tile] = jnp.dot(flat, pick, preferred_element_type=F32).astype(BF)
-
+    pick = jnp.where(gap == offset, 1.0, 0.0).astype(BF)
+    flat = taps.reshape(2 * TILE, 2 * TILE)
+    shifted[tile] = jnp.dot(flat, pick, preferred_element_type=F32).astype(BF)
+
+
+def put_angles(level, cos_ref, sin_ref, ids, scale, first, second):
     phase = jnp.zeros((1, CHANNELS), F32)
     for baseline in range(8):
         phase = phase + jnp.where(ids[...] == baseline, scale[:, baseline : baseline + 1], 0.0)
     bit = bit_of(level)
-    angles = ramp[0, 0].astype(F32)
-    sent = jnp.where(bit == 1, angles[0], angles[1])
-    held = jnp.where(bit == 1, angles[1], angles[0])
+    sent = jnp.where(bit == 1, first, second)
+    held = jnp.where(bit == 1, second, first)
     for channel in range(CHANNELS):
         length = phase[:, channel : channel + 1]
         for side, angle in enumerate((sent, held)):
@@ -93,7 +136,16 @@
             cos_ref[at, :] = cosine
             sin_ref[at, :] = sine
 
+
+def tables_kernel(level, taps, offsets, ramp, ids, scale, beam, shifted, cos_ref, sin_ref, mix_ref):
+    moves = offsets[...].astype(F32)
+    for tile in range(TILES):
+        put_shifted(shifted, tile, taps[0, tile], moves[level : level + 1, tile : tile + 1])
+    angles = ramp[0, 0].astype(F32)
+    put_angles(level, cos_ref, sin_ref, ids, scale, angles[0], angles[1])
+
     size = 2 * PART
+    bit = bit_of(level)
     row = lax.broadcasted_iota(jnp.int32, (size, 16), 0)
     want = lax.broadcasted_iota(jnp.int32, (size, 16), 1)
     child = jnp.where(row // PART == 1, bit, 1 - bit)
@@ -132,81 +184,111 @@
     )(taps, offsets, ramp, ids, scale, beam_mix)
 
 
-def merge(spread, shifted, cos_ref, sin_ref, mix_ref, write):
+def reach_kernel(level, near, ids, scale, shifted, cos_ref, sin_ref):
+    at = WIDE.index(level)
+    last = near[RAMP_AT + at].astype(F32)
+    put_shifted(shifted, 0, near[KERNEL_AT + 16 * at : KERNEL_AT + 16 * (at + 1)], last[0:1, TILE : TILE + 1])
+    put_angles(level, cos_ref, sin_ref, ids, scale, last[:BEAMS, :TILE], last[BEAMS:, :TILE])
+
+
+def reach_tables(level, near, ids, scale):
+    angles = shape(2 * PART, TILE, dtype=F32)
+    outs = [shape(1, 2 * TILE, 3 * TILE), angles, angles]
+    return call(functools.partial(reach_kernel, level), outs, 3, 1 << 25, f"reach{level}")(near, ids, scale)
+
+
+def merge(spread, main, reach, mix, write):
     rows = 2 * PART
-    mix = mix_ref[...]
+    wide = len(reach) > 0
+    odd = jnp.where(is_odd(), 1, 0)
+    order = [(main, tile, tile + odd if wide else tile) for tile in range(TILES)]
+    if wide:
+        order.append((reach, 0, jnp.where(odd == 1, 0, TILES)))
     parts = []
-    for tile in range(TILES):
-        window = spread[:, tile * TILE : (tile + 3) * TILE]
-        both = lax.dot_general(window, shifted[tile], (((1,), (1,)), ((), ())), preferred_element_type=F32)
+    for (shifted, _, _), index, place in order:
+        window = spread[:, pl.ds(aligned(place * TILE), 3 * TILE)]
+        both = lax.dot_general(window, shifted[index], (((1,), (1,)), ((), ())), preferred_element_type=F32)
         real = both[:rows, :TILE] - both[rows:, TILE:]
         imag = both[:rows, TILE:] + both[rows:, :TILE]
         parts.append(jnp.concatenate([real, imag], axis=1).astype(BF))
-    for tile in range(TILES):
-        lanes = slice(tile * TILE, (tile + 1) * TILE)
-        mixed = jnp.dot(mix, parts[tile], preferred_element_type=F32)
+    for ((_, cos_ref, sin_ref), index, place), part in zip(order, parts):
+        lanes = slice(index * TILE, (index + 1) * TILE)
+        mixed = jnp.dot(mix, part, preferred_element_type=F32)
         mixed_re = mixed[:, :TILE]
         mixed_im = mixed[:, TILE:]
         cosine = cos_ref[:, lanes]
         sine = sin_ref[:, lanes]
         out_re = (mixed_re * cosine + mixed_im * sine).astype(BF)
         out_im = (mixed_im * cosine - mixed_re * sine).astype(BF)
-        write(lanes, out_re, out_im)
+        write(pl.ds(aligned(place * TILE), TILE), out_re, out_im)
 
 
 def level_kernel(level, *refs):
-    count = 3 if level == 0 else 6
+    wide = level in WIDE
+    count = 3 if level == 0 else 6 if wide else 4
     data, rest = refs[:count], refs[count:]
-    tables, rest = rest[:4], rest[4:]
+    main, mix_ref, rest = rest[:3], rest[3], rest[4:]
+    reach = ()
+    if wide:
+        reach, rest = rest[:3], rest[3:]
     *outs, spread = rest
     odd = is_odd()
-    near = pl.ds(aligned(jnp.where(odd, 0, BLOCK + TILE)), TILE)
-    far = pl.ds(aligned(jnp.where(odd, BLOCK + TILE, 0)), TILE)
-    middle = pl.ds(TILE, BLOCK)
+    if wide:
+        near = pl.ds(aligned(jnp.where(odd, 0, BLOCK + TILE)), REACH)
+        far = pl.ds(aligned(jnp.where(odd, BLOCK + REACH, 0)), TILE)
+        middle = pl.ds(aligned(jnp.where(odd, REACH, TILE)), BLOCK)
+    else:
+        far = pl.ds(aligned(jnp.where(odd, BLOCK + TILE, 0)), TILE)
+        middle = pl.ds(aligned(jnp.where(odd, 0, TILE)), BLOCK + TILE)
     if level == 0:
         block, near_edge, far_edge = data
         for z in range(2):
             rows = pl.ds(2 * z * PART, 2 * PART)
             spread[rows, middle] = block[z].reshape(2 * PART, BLOCK)
-            spread[rows, near] = near_edge[z].reshape(2 * PART, TILE)
+            spread[rows, near] = near_edge[pl.ds(16 * z, 16)].reshape(2 * PART, REACH)
             spread[rows, far] = far_edge[z].reshape(2 * PART, TILE)
     else:
         for side in range(2):
-            block, near_edge, far_edge = data[3 * side : 3 * side + 3]
             for z in range(2):
                 rows = pl.ds((2 * z + side) * PART, PART)
-                spread[rows, middle] = block[z]
-                spread[rows, near] = near_edge[z]
-                spread[rows, far] = far_edge[z]
-    edges = level < LEVELS - 1
-    held, sent = outs[0], outs[3 if edges else 1]
+                spread[rows, middle] = data[side][z]
+                spread[rows, far] = data[2 + side][z]
+                if wide:
+                    spread[rows, near] = data[4 + side][z]
+    held, sent = outs[:2]
 
     def write(lanes, out_re, out_im):
         for z, value in enumerate((out_re, out_im)):
             sent[z, :, lanes] = value[:PART]
             held[z, :, lanes] = value[PART:]
 
-    merge(spread, *tables, write)
-    if edges:
-        high = pl.ds(aligned(jnp.where(odd, 0, BLOCK - TILE)), TILE)
-        low = pl.ds(aligned(jnp.where(odd, BLOCK - TILE, 0)), TILE)
-        for block, near_edge, far_edge in (outs[:3], outs[3:]):
-            near_edge[...] = block[:, :, high]
-            far_edge[...] = block[:, :, low]
-
-
-def level_call(level, data, tables):
-    edge = shape(2, PART, TILE)
-    block = shape(2, PART, BLOCK)
-    outs = [block] * 2 if level == LEVELS - 1 else [block, edge, edge] * 2
-    operands = (*data, *tables)
+    merge(spread, main, reach, mix_ref[...], write)
+    if level < LEVELS - 1:
+        start = BLOCK if wide else BLOCK - TILE
+        far = pl.ds(aligned(jnp.where(odd, start, 0)), TILE)
+        near = pl.ds(aligned(jnp.where(odd, 0, BLOCK - REACH)), REACH)
+        for side in range(2):
+            outs[2 + side][...] = outs[side][:, :, far]
+            if not wide:
+                outs[4 + side][...] = outs[side][:, :, near]
+
+
+def level_call(level, data, tables, reach):
+    wide = level in WIDE
+    outs = [shape(2, PART, BLOCK + TILE if wide else BLOCK)] * 2
+    if level < LEVELS - 1:
+        outs += [shape(2, PART, TILE)] * 2
+        if not wide:
+            outs += [shape(2, PART, REACH)] * 2
+    operands = (*data, *tables, *reach)
+    width = BLOCK + TILE + (REACH if wide else TILE)
     return call(
         functools.partial(level_kernel, level),
         outs,
         len(operands),
         TILES * 2 * (4 * PART * 384 * 256 + 4 * PART * PART * 256),
         f"merge{level}",
-        [pltpu.VMEM((4 * PART, BLOCK + 2 * TILE), BF)],
+        [pltpu.VMEM((4 * PART, width), BF)],
     )(*operands)
 
 
@@ -222,33 +304,31 @@
         return lax.ppermute(value, ("pulse", "range"), pairs)
 
     block = grad_image[0]
-    low = block[..., :TILE]
-    high = block[..., BLOCK - TILE :]
-    odd = is_odd()
-    far_edge = move(jnp.where(odd, high, low), 0, far_pairs)
-    near_edge = move(jnp.where(odd, low, high), 0, near_pairs)
-    state = (block, near_edge, far_edge)
+    ids = baseline_ids[None]
+    scale = baseline_scale[None]
+    near_pack, far_edge = take_edges(
+        block,
+        range_kernel.reshape(LEVELS, TILES, 16, 16, 2 * TILE),
+        ramp.reshape(LEVELS, 2 * BEAMS, BLOCK),
+        band_offsets,
+    )
+    near_pack = move(near_pack, 0, near_pairs)
+    far_edge = move(far_edge, 0, far_pairs)
+    state = (block, near_pack, far_edge)
+    stay = [(i, i) for i in range(ranges)]
+    tables = [make_tables(l, range_kernel, band_offsets, ramp, ids, scale, beam_mix) for l in range(LEVELS)]
+    reach = [reach_tables(l, near_pack, ids, scale) if l in WIDE else () for l in range(LEVELS)]
     for level in range(LEVELS):
-        tables = make_tables(
-            level, range_kernel, band_offsets, ramp, baseline_ids[None], baseline_scale[None], beam_mix
-        )
-        outs = level_call(level, state, tables)
+        if level == 1:
+            state, tables, reach = lax.optimization_barrier((state, tables, reach))
+        held, sent, *edges = level_call(level, state, tables[level], reach[level])
         mask = 2 ** BITS[level]
-        stay = [(i, i) for i in range(ranges)]
-        if level < LEVELS - 1:
-            held, held_near, held_far, sent, sent_near, sent_far = outs
-            got = move(sent, mask, stay)
-            state = (
-                held,
-                move(held_near, 0, near_pairs),
-                move(held_far, 0, far_pairs),
-                got,
-                move(sent_near, mask, near_pairs),
-                move(sent_far, mask, far_pairs),
-            )
-        else:
-            held, sent = outs
-            got = move(sent, mask, stay)
+        got = move(sent, mask, stay)
+        state = [held, got]
+        if edges:
+            state += [move(edges[0], 0, far_pairs), move(edges[1], mask, far_pairs)]
+        if len(edges) > 2:
+            state += [move(edges[2], 0, near_pairs), move(edges[3], mask, near_pairs)]
 
     held = held.reshape(2, CHANNELS, BEAMS, BLOCK)
     got = got.reshape(2, CHANNELS, BEAMS, BLOCK)

time: 94 us -> 87.3 us (0.929)
  the two profiles are of different devices: /device:TPU:1 before, /device:TPU:125 now
where the time goes in v2:
time: 87.3 us; the launch traced here: 86.9 us
  starting transfers between devices  47 us (54%)
  waiting for transfers between devices  26.1 us (30%)
  Pallas kernels  12.5 us (14%)
  other arithmetic  0.89 us (1%)
    ppermute x14, starting transfers between devices, move(): return lax.ppermute(value, ('pulse', 'range'), pairs)  47 us
    ppermute x14, waiting for transfers between devices, move(): return lax.ppermute(value, ('pulse', 'range'), pairs)  26.1 us
    pallas_call x4, Pallas kernels, make_tables(): pl.pallas_call(functools.partial(tables_kernel, level), grid=(1,), out_sh...  5.06 us
    pallas_call x4, Pallas kernels, level_call(): call(functools.partial(level_kernel, level), outs, len(operands), TILES *...  4.49 us
    pallas_call x1, Pallas kernels, take_edges(): pl.pallas_call(edges_kernel, out_shape=[shape(UNITS, 16, REACH), shape(2,...  2.24 us
  transfers between devices with their start and end apart: 14, of which 5 were waited for; matrix products, arithmetic and copies ran while one was open for 0% of the time, Pallas kernels for 7%

profile of v2, /device:TPU:125, one launch (start us, length us, event | category | flops | bytes accessed | tf_op | source)
XLA Modules:
  0.0 86.9 jit_solution(6534454198523917522)
XLA Ops:
  0.0 0.0 copy-start
  0.0 0.0 copy-start.2
  0.0 0.0 copy-start.4
  0.0 0.0 copy-start.5
  0.0 0.0 copy-start.6
  0.0 0.0 copy-start.3
  0.0 0.0 copy-start.1
  0.0 2.2 %edges.1 = (bf16[66,16,256]{2,1,0:T(8,128)(2,1)}, bf16[2,16,16,128]{3,2,1,0:T(8,128)(2,1)}) custom-call(bf16[2,16,16,512]{3,2,1,0:T(8,128)(2,1)} %bitcast.12, bf16[4,4,16,16,256]{4,3,2,1,0:T(8,128)(2,1)} %bitcast.11, bf16[4,16,512]{2,1,0:T(8,128)(2,1)} %bitcast.14, s32[4,4]{1,0:T(4,128)} %offsets.9), custom_call_target="tpu_custom_call" | custom-call | flops 1048576 | bytes 1048576 | tf_op jit(solution)/shard_map/edges/pallas_call | solution.py:103
  2.3 2.6 %collective-permute-start = (bf16[66,16,256]{2,1,0:T(8,128)(2,1)}, bf16[66,16,256]{2,1,0:T(8,128)(2,1)S(1)}, u32[]{:S(2)}, u32[]{:S(2)}) collective-permute-start(bf16[66,16,256]{2,1,0:T(8,128)(2,1)} %get-tuple-element.64), channel_id=1, source_target_pairs={{0,1},{1,0},{2,3},{3,2},{4,5},{5,4},{6,7},{7,6},{8,9},{9,8},{10,11... | collective-permute-start | bytes 1622024 | tf_op jit(solution)/shard_map/ppermute | solution.py:304
  4.9 2.7 %collective-permute-start.1 = (bf16[2,16,16,128]{3,2,1,0:T(8,128)(2,1)}, bf16[2,16,16,128]{3,2,1,0:T(8,128)(2,1)S(1)}, u32[]{:S(2)}, u32[]{:S(2)}) collective-permute-start(bf16[2,16,16,128]{3,2,1,0:T(8,128)(2,1)} %get-tuple-element.65), channel_id=1, source_target_pairs={{1,2},{2,1},{5,6},{6,5},{9,10},{10,9},{13,14},{14,13},{17,18},{18,... | collective-permute-start | bytes 393224 | tf_op jit(solution)/shard_map/ppermute | solution.py:304
  7.6 0.0 copy-done
  7.6 0.0 copy-done.2
  7.6 0.0 copy-done.4
  7.7 0.0 copy-done.5
  7.7 0.0 copy-done.6
  7.7 0.0 copy-done.3
  7.7 1.3 %tables0.1 = (bf16[4,256,384]{2,1,0:T(8,128)(2,1)S(1)}, f32[256,512]{1,0:T(8,128)S(1)}, f32[256,512]{1,0:T(8,128)S(1)}, bf16[256,256]{1,0:T(8,128)(2,1)S(1)}) custom-call(bf16[4,4,2,128,256]{4,3,2,1,0:T(8,128)(2,1)S(1)} %copy-done, s32[4,4]{1,0:T(4,128)S(1)} %copy-done.4, bf16[4,1,2,8,512]{4,3,2,1,0:T(8,128)(2,1)S(1)} %copy-done.2, s32[1,16]{1,0:T(1,128)S(1)} %bitcast.15, ...), custom_call_target="tpu_custom_call" | custom-call | flops 134217728 | bytes 2097152 | tf_op jit(solution)/shard_map/tables0/pallas_call | solution.py:175
  8.9 0.0 collective-permute-done.near.refs_1_
  9.0 0.4 reach0.1
  9.3 2.1 %collective-permute-done.1.refs_2_ = bf16[2,16,16,128]{3,2,1,0:T(8,128)(2,1)S(1)} collective-permute-done((bf16[2,16,16,128]{3,2,1,0:T(8,128)(2,1)}, bf16[2,16,16,128]{3,2,1,0:T(8,128)(2,1)S(1)}, u32[]{:S(2)}, u32[]{:S(2)}) %collective-permute-start.1) | collective-permute-done | bytes 131104 | tf_op jit(solution)/shard_map/ppermute | solution.py:304
  11.4 0.0 copy-done.1
  11.4 1.2 %merge0.1 = (bf16[2,128,640]{2,1,0:T(8,128)(2,1)S(1)}, bf16[2,128,640]{2,1,0:T(8,128)(2,1)S(1)}, bf16[2,128,128]{2,1,0:T(8,128)(2,1)S(1)}, bf16[2,128,128]{2,1,0:T(8,128)(2,1)S(1)}) custom-call(bf16[2,16,16,512]{3,2,1,0:T(8,128)(2,1)S(1)} %bitcast.13, bf16[66,16,256]{2,1,0:T(8,128)(2,1)S(1)} %collective-permute-done.near.refs_1_, ...), custom_call_target="tpu_custom_call" | custom-call | flops 536870912 | bytes 1048576 | tf_op jit(solution)/shard_map/merge0/pallas_call | solution.py:285
  12.6 5.8 %collective-permute-start.2 = (bf16[2,128,640]{2,1,0:T(8,128)(2,1)S(1)}, bf16[2,128,640]{2,1,0:T(8,128)(2,1)S(1)}, u32[]{:S(2)}, u32[]{:S(2)}) collective-permute-start(bf16[2,128,640]{2,1,0:T(8,128)(2,1)S(1)} %get-tuple-element.74), channel_id=1, source_target_pairs={{0,64},{1,65},{2,66},{3,67},{4,68},{5,69},{6,70},{7,71},{8,72},{9,... | collective-permute-start | bytes 983048 | tf_op jit(solution)/shard_map/ppermute | solution.py:304
  18.4 3.0 %collective-permute-start.3 = (bf16[2,128,128]{2,1,0:T(8,128)(2,1)S(1)}, bf16[2,128,128]{2,1,0:T(8,128)(2,1)S(1)}, u32[]{:S(2)}, u32[]{:S(2)}) collective-permute-start(bf16[2,128,128]{2,1,0:T(8,128)(2,1)S(1)} %get-tuple-element.75), channel_id=1, source_target_pairs={{1,2},{2,1},{5,6},{6,5},{9,10},{10,9},{13,14},{14,13},{17,18},{18,... | collective-permute-start | bytes 196616 | tf_op jit(solution)/shard_map/ppermute | solution.py:304
  21.5 2.3 %collective-permute-start.4 = (bf16[2,128,128]{2,1,0:T(8,128)(2,1)S(1)}, bf16[2,128,128]{2,1,0:T(8,128)(2,1)S(1)}, u32[]{:S(2)}, u32[]{:S(2)}) collective-permute-start(bf16[2,128,128]{2,1,0:T(8,128)(2,1)S(1)} %get-tuple-element.76), channel_id=1, source_target_pairs={{1,66},{2,65},{5,70},{6,69},{9,74},{10,73},{13,78},{14,77},{17,82}... | collective-permute-start | bytes 196616 | tf_op jit(solution)/shard_map/ppermute | solution.py:304
  23.8 1.3 %tables1.1 = (bf16[4,256,384]{2,1,0:T(8,128)(2,1)S(1)}, f32[256,512]{1,0:T(8,128)S(1)}, f32[256,512]{1,0:T(8,128)S(1)}, bf16[256,256]{1,0:T(8,128)(2,1)S(1)}) custom-call(bf16[4,4,2,128,256]{4,3,2,1,0:T(8,128)(2,1)S(1)} %copy-done, s32[4,4]{1,0:T(4,128)S(1)} %copy-done.4, bf16[4,1,2,8,512]{4,3,2,1,0:T(8,128)(2,1)S(1)} %copy-done.2, s32[1,16]{1,0:T(1,128)S(1)} %bitcast.17, ...), custom_call_target="tpu_custom_call" | custom-call | flops 134217728 | bytes 2097152 | tf_op jit(solution)/shard_map/tables1/pallas_call | solution.py:175
  25.0 1.3 %tables2.1 = (bf16[4,256,384]{2,1,0:T(8,128)(2,1)S(1)}, f32[256,512]{1,0:T(8,128)S(1)}, f32[256,512]{1,0:T(8,128)S(1)}, bf16[256,256]{1,0:T(8,128)(2,1)S(1)}) custom-call(bf16[4,4,2,128,256]{4,3,2,1,0:T(8,128)(2,1)S(1)} %copy-done, s32[4,4]{1,0:T(4,128)S(1)} %copy-done.4, bf16[4,1,2,8,512]{4,3,2,1,0:T(8,128)(2,1)S(1)} %copy-done.2, s32[1,16]{1,0:T(1,128)S(1)} %bitcast.18, ...), custom_call_target="tpu_custom_call" | custom-call | flops 134217728 | bytes 2097152 | tf_op jit(solution)/shard_map/tables2/pallas_call | solution.py:175
  26.3 1.3 %tables3.1 = (bf16[4,256,384]{2,1,0:T(8,128)(2,1)S(1)}, f32[256,512]{1,0:T(8,128)S(1)}, f32[256,512]{1,0:T(8,128)S(1)}, bf16[256,256]{1,0:T(8,128)(2,1)S(1)}) custom-call(bf16[4,4,2,128,256]{4,3,2,1,0:T(8,128)(2,1)S(1)} %copy-done, s32[4,4]{1,0:T(4,128)S(1)} %copy-done.4, bf16[4,1,2,8,512]{4,3,2,1,0:T(8,128)(2,1)S(1)} %copy-done.2, s32[1,16]{1,0:T(1,128)S(1)} %bitcast.19, ...), custom_call_target="tpu_custom_call" | custom-call | flops 134217728 | bytes 2097152 | tf_op jit(solution)/shard_map/tables3/pallas_call | solution.py:175
  27.6 0.4 reach2.1
  27.9 0.0 collective-permute-done.3.refs_2_
  27.9 2.0 %collective-permute-done.4.refs_3_ = bf16[2,128,128]{2,1,0:T(8,128)(2,1)S(1)} collective-permute-done((bf16[2,128,128]{2,1,0:T(8,128)(2,1)S(1)}, bf16[2,128,128]{2,1,0:T(8,128)(2,1)S(1)}, u32[]{:S(2)}, u32[]{:S(2)}) %collective-permute-start.4) | collective-permute-done | bytes 65568 | tf_op jit(solution)/shard_map/ppermute | solution.py:304
  29.9 0.0 collective-permute-done.2.refs_1_
  29.9 1.0 %merge1.1 = (bf16[2,128,512]{2,1,0:T(8,128)(2,1)S(1)}, bf16[2,128,512]{2,1,0:T(8,128)(2,1)S(1)}, bf16[2,128,128]{2,1,0:T(8,128)(2,1)S(1)}, bf16[2,128,128]{2,1,0...) custom-call(bf16[2,128,640]{2,1,0:T(8,128)(2,1)S(1)} %get-tuple-element.92.refs_0_, ...), custom_call_target="tpu_custom_call" | custom-call | flops 536870912 | bytes 1048576 | tf_op jit(solution)/shard_map/merge1/pallas_call | solution.py:285
  31.0 2.7 %collective-permute-start.5 = (bf16[2,128,512]{2,1,0:T(8,128)(2,1)S(1)}, bf16[2,128,512]{2,1,0:T(8,128)(2,1)S(1)}, u32[]{:S(2)}, u32[]{:S(2)}) collective-permute-start(bf16[2,128,512]{2,1,0:T(8,128)(2,1)S(1)} %get-tuple-element.101), channel_id=1, source_target_pairs={{0,32},{1,33},{2,34},{3,35},{4,36},{5,37},{6,38},{7,39},{8,40},{9,... | collective-permute-start | bytes 786440 | tf_op jit(solution)/shard_map/ppermute | solution.py:304
  33.7 1.9 %collective-permute-start.8 = (bf16[2,128,256]{2,1,0:T(8,128)(2,1)S(1)}, bf16[2,128,256]{2,1,0:T(8,128)(2,1)S(1)}, u32[]{:S(2)}, u32[]{:S(2)}) collective-permute-start(bf16[2,128,256]{2,1,0:T(8,128)(2,1)S(1)} %get-tuple-element.104), channel_id=1, source_target_pairs={{0,1},{1,0},{2,3},{3,2},{4,5},{5,4},{6,7},{7,6},{8,9},{9,8},{10,11... | collective-permute-start | bytes 393224 | tf_op jit(solution)/shard_map/ppermute | solution.py:304
  35.6 3.0 %collective-permute-start.9 = (bf16[2,128,256]{2,1,0:T(8,128)(2,1)S(1)}, bf16[2,128,256]{2,1,0:T(8,128)(2,1)S(1)}, u32[]{:S(2)}, u32[]{:S(2)}) collective-permute-start(bf16[2,128,256]{2,1,0:T(8,128)(2,1)S(1)} %get-tuple-element.105), channel_id=1, source_target_pairs={{0,33},{1,32},{2,35},{3,34},{4,37},{5,36},{6,39},{7,38},{8,41},{9,... | collective-permute-start | bytes 393224 | tf_op jit(solution)/shard_map/ppermute | solution.py:304
  38.6 2.8 %collective-permute-start.6 = (bf16[2,128,128]{2,1,0:T(8,128)(2,1)S(1)}, bf16[2,128,128]{2,1,0:T(8,128)(2,1)S(1)}, u32[]{:S(2)}, u32[]{:S(2)}) collective-permute-start(bf16[2,128,128]{2,1,0:T(8,128)(2,1)S(1)} %get-tuple-element.102), channel_id=1, source_target_pairs={{1,2},{2,1},{5,6},{6,5},{9,10},{10,9},{13,14},{14,13},{17,18},{18,... | collective-permute-start | bytes 196616 | tf_op jit(solution)/shard_map/ppermute | solution.py:304
  41.4 3.3 %collective-permute-start.7 = (bf16[2,128,128]{2,1,0:T(8,128)(2,1)S(1)}, bf16[2,128,128]{2,1,0:T(8,128)(2,1)S(1)}, u32[]{:S(2)}, u32[]{:S(2)}) collective-permute-start(bf16[2,128,128]{2,1,0:T(8,128)(2,1)S(1)} %get-tuple-element.103), channel_id=1, source_target_pairs={{1,34},{2,33},{5,38},{6,37},{9,42},{10,41},{13,46},{14,45},{17,50}... | collective-permute-start | bytes 196616 | tf_op jit(solution)/shard_map/ppermute | solution.py:304
  44.7 0.0 collective-permute-done.6.refs_2_
  44.7 3.2 %collective-permute-done.7.refs_3_ = bf16[2,128,128]{2,1,0:T(8,128)(2,1)S(1)} collective-permute-done((bf16[2,128,128]{2,1,0:T(8,128)(2,1)S(1)}, bf16[2,128,128]{2,1,0:T(8,128)(2,1)S(1)}, u32[]{:S(2)}, u32[]{:S(2)}) %collective-permute-start.7) | collective-permute-done | bytes 65568 | tf_op jit(solution)/shard_map/ppermute | solution.py:304
  47.9 0.0 collective-permute-done.8.refs_4_
  47.9 0.0 collective-permute-done.9.refs_5_
  47.9 0.0 collective-permute-done.5.refs_1_
  47.9 1.2 %merge2.1 = (bf16[2,128,640]{2,1,0:T(8,128)(2,1)S(1)}, bf16[2,128,640]{2,1,0:T(8,128)(2,1)S(1)}, bf16[2,128,128]{2,1,0:T(8,128)(2,1)S(1)}, bf16[2,128,128]{2,1,0:T(8,128)(2,1)S(1)}) custom-call(bf16[2,128,512]{2,1,0:T(8,128)(2,1)S(1)} %get-tuple-element.100.refs_0_, bf16[2,128,512]{2,1,0:T(8,128)(2,1)S(1)} %collective-permute-done.5.refs_1_, ...), custom_call_target="tpu_custom_call" | custom-call | flops 536870912 | bytes 1048576 | tf_op jit(solution)/shard_map/merge2/pallas_call | solution.py:285
  49.2 4.4 %collective-permute-start.10 = (bf16[2,128,640]{2,1,0:T(8,128)(2,1)S(1)}, bf16[2,128,640]{2,1,0:T(8,128)(2,1)S(1)}, u32[]{:S(2)}, u32[]{:S(2)}) collective-permute-start(bf16[2,128,640]{2,1,0:T(8,128)(2,1)S(1)} %get-tuple-element.114), channel_id=1, source_target_pairs={{0,16},{1,17},{2,18},{3,19},{4,20},{5,21},{6,22},{7,23},{8,24},{9,... | collective-permute-start | bytes 983048 | tf_op jit(solution)/shard_map/ppermute | solution.py:304
  53.6 3.0 %collective-permute-start.11 = (bf16[2,128,128]{2,1,0:T(8,128)(2,1)S(1)}, bf16[2,128,128]{2,1,0:T(8,128)(2,1)S(1)}, u32[]{:S(2)}, u32[]{:S(2)}) collective-permute-start(bf16[2,128,128]{2,1,0:T(8,128)(2,1)S(1)} %get-tuple-element.115), channel_id=1, source_target_pairs={{1,2},{2,1},{5,6},{6,5},{9,10},{10,9},{13,14},{14,13},{17,18},{18,... | collective-permute-start | bytes 196616 | tf_op jit(solution)/shard_map/ppermute | solution.py:304
  56.6 5.1 %collective-permute-start.12 = (bf16[2,128,128]{2,1,0:T(8,128)(2,1)S(1)}, bf16[2,128,128]{2,1,0:T(8,128)(2,1)S(1)}, u32[]{:S(2)}, u32[]{:S(2)}) collective-permute-start(bf16[2,128,128]{2,1,0:T(8,128)(2,1)S(1)} %get-tuple-element.116), channel_id=1, source_target_pairs={{1,18},{2,17},{5,22},{6,21},{9,26},{10,25},{13,30},{14,29},{17,2},... | collective-permute-start | bytes 196616 | tf_op jit(solution)/shard_map/ppermute | solution.py:304
  61.7 0.0 collective-permute-done.11.refs_2_
  61.8 6.9 %collective-permute-done.12.refs_3_ = bf16[2,128,128]{2,1,0:T(8,128)(2,1)S(1)} collective-permute-done((bf16[2,128,128]{2,1,0:T(8,128)(2,1)S(1)}, bf16[2,128,128]{2,1,0:T(8,128)(2,1)S(1)}, u32[]{:S(2)}, u32[]{:S(2)}) %collective-permute-start.12) | collective-permute-done | bytes 65568 | tf_op jit(solution)/shard_map/ppermute | solution.py:304
  68.7 0.0 collective-permute-done.10.refs_1_
  68.7 1.0 %merge3.1 = (bf16[2,128,512]{2,1,0:T(8,128)(2,1)S(1)}, bf16[2,128,512]{2,1,0:T(8,128)(2,1)S(1)}) custom-call(bf16[2,128,640]{2,1,0:T(8,128)(2,1)S(1)} %get-tuple-element.113.refs_0_, bf16[2,128,640]{2,1,0:T(8,128)(2,1)S(1)} %collective-permute-done.10.refs_1_, bf16[2,128,128]{2,1,0:T(8,128)(2,1)S(1)} %collective-permute-done.11.refs_2_, ...), custom_call_target="tpu_custom_call" | custom-call | flops 536870912 | bytes 1048576 | tf_op jit(solution)/shard_map/merge3/pallas_call | solution.py:285
  69.7 4.4 %collective-permute-start.13 = (bf16[2,128,512]{2,1,0:T(8,128)(2,1)S(1)}, bf16[2,128,512]{2,1,0:T(8,128)(2,1)S(1)}, u32[]{:S(2)}, u32[]{:S(2)}) collective-permute-start(bf16[2,128,512]{2,1,0:T(8,128)(2,1)S(1)} %get-tuple-element.121), channel_id=1, source_target_pairs={{0,8},{1,9},{2,10},{3,11},{4,12},{5,13},{6,14},{7,15},{8,0},{9,1},... | collective-permute-start | bytes 786440 | tf_op jit(solution)/shard_map/ppermute | solution.py:304
  74.2 11.8 %collective-permute-done.13 = bf16[2,128,512]{2,1,0:T(8,128)(2,1)S(1)} collective-permute-done((bf16[2,128,512]{2,1,0:T(8,128)(2,1)S(1)}, bf16[2,128,512]{2,1,0:T(8,128)(2,1)S(1)}, u32[]{:S(2)}, u32[]{:S(2)}) %collective-permute-start.13) | collective-permute-done | bytes 262176 | tf_op jit(solution)/shard_map/ppermute | solution.py:304
  86.0 0.9 maximum_bitcast_fusion
  (1 shorter events, 0.0 us)
Async XLA Ops:
  0.0 7.6 %copy-start = (bf16[4,4,2,128,256]{4,3,2,1,0:T(8,128)(2,1)S(1)}, bf16[4,4,2,128,256]{4,3,2,1,0:T(8,128)(2,1)}, u32[]{:S(2)}) copy-start(bf16[4,4,2,128,256]{4,3,2,1,0:T(8,128)(2,1)} %taps.7) | copy-start | bytes 6291460
  0.0 7.6 %copy-start.2 = (bf16[4,1,2,8,512]{4,3,2,1,0:T(8,128)(2,1)S(1)}, bf16[4,1,2,8,512]{4,3,2,1,0:T(8,128)(2,1)}, u32[]{:S(2)}) copy-start(bf16[4,1,2,8,512]{4,3,2,1,0:T(8,128)(2,1)} %ramp.7) | copy-start | bytes 196612
  0.0 7.6 %copy-start.4 = (s32[4,4]{1,0:T(4,128)S(1)}, s32[4,4]{1,0:T(4,128)}, u32[]{:S(2)}) copy-start(s32[4,4]{1,0:T(4,128)} %offsets.9) | copy-start | bytes 196
  0.0 7.6 %copy-start.5 = (s32[16]{0:T(128)S(1)}, s32[16]{0:T(128)}, u32[]{:S(2)}) copy-start(s32[16]{0:T(128)} %param.12) | copy-start | bytes 196
  0.0 7.6 %copy-start.6 = (f32[8]{0:T(128)S(1)}, f32[8]{0:T(128)}, u32[]{:S(2)}) copy-start(f32[8]{0:T(128)} %param.13) | copy-start | bytes 100
  0.0 7.6 %copy-start.3 = (bf16[4,1,2,8,16]{4,3,2,1,0:T(8,128)(2,1)S(1)}, bf16[4,1,2,8,16]{4,3,2,1,0:T(8,128)(2,1)}, u32[]{:S(2)}) copy-start(bf16[4,1,2,8,16]{4,3,2,1,0:T(8,128)(2,1)} %beam.7) | copy-start | bytes 6148
  0.0 11.3 %copy-start.1 = (bf16[1,2,16,16,512]{4,3,2,1,0:T(8,128)(2,1)S(1)}, bf16[1,2,16,16,512]{4,3,2,1,0:T(8,128)(2,1)}, u32[]{:S(2)}) copy-start(bf16[1,2,16,16,512]{4,3,2,1,0:T(8,128)(2,1)} %param.7) | copy-start | bytes 1572868
  2.3 6.6 %collective-permute-start = (bf16[66,16,256]{2,1,0:T(8,128)(2,1)}, bf16[66,16,256]{2,1,0:T(8,128)(2,1)S(1)}, u32[]{:S(2)}, u32[]{:S(2)}) collective-permute-start(bf16[66,16,256]{2,1,0:T(8,128)(2,1)} %get-tuple-element.64), channel_id=1, source_target_pairs={{0,1},{1,0},{2,3},{3,2},{4,5},{5,4},{6,7},{7,6},{8,9},{9,8},{10,11... | collective-permute-start | bytes 1622024 | tf_op jit(solution)/shard_map/ppermute | solution.py:304
  4.9 6.5 %collective-permute-start.1 = (bf16[2,16,16,128]{3,2,1,0:T(8,128)(2,1)}, bf16[2,16,16,128]{3,2,1,0:T(8,128)(2,1)S(1)}, u32[]{:S(2)}, u32[]{:S(2)}) collective-permute-start(bf16[2,16,16,128]{3,2,1,0:T(8,128)(2,1)} %get-tuple-element.65), channel_id=1, source_target_pairs={{1,2},{2,1},{5,6},{6,5},{9,10},{10,9},{13,14},{14,13},{17,18},{18,... | collective-permute-start | bytes 393224 | tf_op jit(solution)/shard_map/ppermute | solution.py:304
  12.6 17.3 %collective-permute-start.2 = (bf16[2,128,640]{2,1,0:T(8,128)(2,1)S(1)}, bf16[2,128,640]{2,1,0:T(8,128)(2,1)S(1)}, u32[]{:S(2)}, u32[]{:S(2)}) collective-permute-start(bf16[2,128,640]{2,1,0:T(8,128)(2,1)S(1)} %get-tuple-element.74), channel_id=1, source_target_pairs={{0,64},{1,65},{2,66},{3,67},{4,68},{5,69},{6,70},{7,71},{8,72},{9,... | collective-permute-start | bytes 983048 | tf_op jit(solution)/shard_map/ppermute | solution.py:304
  18.4 9.5 %collective-permute-start.3 = (bf16[2,128,128]{2,1,0:T(8,128)(2,1)S(1)}, bf16[2,128,128]{2,1,0:T(8,128)(2,1)S(1)}, u32[]{:S(2)}, u32[]{:S(2)}) collective-permute-start(bf16[2,128,128]{2,1,0:T(8,128)(2,1)S(1)} %get-tuple-element.75), channel_id=1, source_target_pairs={{1,2},{2,1},{5,6},{6,5},{9,10},{10,9},{13,14},{14,13},{17,18},{18,... | collective-permute-start | bytes 196616 | tf_op jit(solution)/shard_map/ppermute | solution.py:304
  21.5 8.5 %collective-permute-start.4 = (bf16[2,128,128]{2,1,0:T(8,128)(2,1)S(1)}, bf16[2,128,128]{2,1,0:T(8,128)(2,1)S(1)}, u32[]{:S(2)}, u32[]{:S(2)}) collective-permute-start(bf16[2,128,128]{2,1,0:T(8,128)(2,1)S(1)} %get-tuple-element.76), channel_id=1, source_target_pairs={{1,66},{2,65},{5,70},{6,69},{9,74},{10,73},{13,78},{14,77},{17,82}... | collective-permute-start | bytes 196616 | tf_op jit(solution)/shard_map/ppermute | solution.py:304
  31.0 16.9 %collective-permute-start.5 = (bf16[2,128,512]{2,1,0:T(8,128)(2,1)S(1)}, bf16[2,128,512]{2,1,0:T(8,128)(2,1)S(1)}, u32[]{:S(2)}, u32[]{:S(2)}) collective-permute-start(bf16[2,128,512]{2,1,0:T(8,128)(2,1)S(1)} %get-tuple-element.101), channel_id=1, source_target_pairs={{0,32},{1,33},{2,34},{3,35},{4,36},{5,37},{6,38},{7,39},{8,40},{9,... | collective-permute-start | bytes 786440 | tf_op jit(solution)/shard_map/ppermute | solution.py:304
  33.7 14.2 %collective-permute-start.8 = (bf16[2,128,256]{2,1,0:T(8,128)(2,1)S(1)}, bf16[2,128,256]{2,1,0:T(8,128)(2,1)S(1)}, u32[]{:S(2)}, u32[]{:S(2)}) collective-permute-start(bf16[2,128,256]{2,1,0:T(8,128)(2,1)S(1)} %get-tuple-element.104), channel_id=1, source_target_pairs={{0,1},{1,0},{2,3},{3,2},{4,5},{5,4},{6,7},{7,6},{8,9},{9,8},{10,11... | collective-permute-start | bytes 393224 | tf_op jit(solution)/shard_map/ppermute | solution.py:304
  35.6 12.3 %collective-permute-start.9 = (bf16[2,128,256]{2,1,0:T(8,128)(2,1)S(1)}, bf16[2,128,256]{2,1,0:T(8,128)(2,1)S(1)}, u32[]{:S(2)}, u32[]{:S(2)}) collective-permute-start(bf16[2,128,256]{2,1,0:T(8,128)(2,1)S(1)} %get-tuple-element.105), channel_id=1, source_target_pairs={{0,33},{1,32},{2,35},{3,34},{4,37},{5,36},{6,39},{7,38},{8,41},{9,... | collective-permute-start | bytes 393224 | tf_op jit(solution)/shard_map/ppermute | solution.py:304
  38.6 6.1 %collective-permute-start.6 = (bf16[2,128,128]{2,1,0:T(8,128)(2,1)S(1)}, bf16[2,128,128]{2,1,0:T(8,128)(2,1)S(1)}, u32[]{:S(2)}, u32[]{:S(2)}) collective-permute-start(bf16[2,128,128]{2,1,0:T(8,128)(2,1)S(1)} %get-tuple-element.102), channel_id=1, source_target_pairs={{1,2},{2,1},{5,6},{6,5},{9,10},{10,9},{13,14},{14,13},{17,18},{18,... | collective-permute-start | bytes 196616 | tf_op jit(solution)/shard_map/ppermute | solution.py:304
  41.4 6.5 %collective-permute-start.7 = (bf16[2,128,128]{2,1,0:T(8,128)(2,1)S(1)}, bf16[2,128,128]{2,1,0:T(8,128)(2,1)S(1)}, u32[]{:S(2)}, u32[]{:S(2)}) collective-permute-start(bf16[2,128,128]{2,1,0:T(8,128)(2,1)S(1)} %get-tuple-element.103), channel_id=1, source_target_pairs={{1,34},{2,33},{5,38},{6,37},{9,42},{10,41},{13,46},{14,45},{17,50}... | collective-permute-start | bytes 196616 | tf_op jit(solution)/shard_map/ppermute | solution.py:304
  49.2 19.5 %collective-permute-start.10 = (bf16[2,128,640]{2,1,0:T(8,128)(2,1)S(1)}, bf16[2,128,640]{2,1,0:T(8,128)(2,1)S(1)}, u32[]{:S(2)}, u32[]{:S(2)}) collective-permute-start(bf16[2,128,640]{2,1,0:T(8,128)(2,1)S(1)} %get-tuple-element.114), channel_id=1, source_target_pairs={{0,16},{1,17},{2,18},{3,19},{4,20},{5,21},{6,22},{7,23},{8,24},{9,... | collective-permute-start | bytes 983048 | tf_op jit(solution)/shard_map/ppermute | solution.py:304
  53.6 8.1 %collective-permute-start.11 = (bf16[2,128,128]{2,1,0:T(8,128)(2,1)S(1)}, bf16[2,128,128]{2,1,0:T(8,128)(2,1)S(1)}, u32[]{:S(2)}, u32[]{:S(2)}) collective-permute-start(bf16[2,128,128]{2,1,0:T(8,128)(2,1)S(1)} %get-tuple-element.115), channel_id=1, source_target_pairs={{1,2},{2,1},{5,6},{6,5},{9,10},{10,9},{13,14},{14,13},{17,18},{18,... | collective-permute-start | bytes 196616 | tf_op jit(solution)/shard_map/ppermute | solution.py:304
  56.6 12.1 %collective-permute-start.12 = (bf16[2,128,128]{2,1,0:T(8,128)(2,1)S(1)}, bf16[2,128,128]{2,1,0:T(8,128)(2,1)S(1)}, u32[]{:S(2)}, u32[]{:S(2)}) collective-permute-start(bf16[2,128,128]{2,1,0:T(8,128)(2,1)S(1)} %get-tuple-element.116), channel_id=1, source_target_pairs={{1,18},{2,17},{5,22},{6,21},{9,26},{10,25},{13,30},{14,29},{17,2},... | collective-permute-start | bytes 196616 | tf_op jit(solution)/shard_map/ppermute | solution.py:304
  69.7 16.3 %collective-permute-start.13 = (bf16[2,128,512]{2,1,0:T(8,128)(2,1)S(1)}, bf16[2,128,512]{2,1,0:T(8,128)(2,1)S(1)}, u32[]{:S(2)}, u32[]{:S(2)}) collective-permute-start(bf16[2,128,512]{2,1,0:T(8,128)(2,1)S(1)} %get-tuple-element.121), channel_id=1, source_target_pairs={{0,8},{1,9},{2,10},{3,11},{4,12},{5,13},{6,14},{7,15},{8,0},{9,1},... | collective-permute-start | bytes 786440 | tf_op jit(solution)/shard_map/ppermute | solution.py:304

commit v3 on v2

--- a/solution.py
+++ b/solution.py
@@ -252,9 +252,9 @@
             for z in range(2):
                 rows = pl.ds((2 * z + side) * PART, PART)
                 spread[rows, middle] = data[side][z]
-                spread[rows, far] = data[2 + side][z]
+                spread[rows, far] = data[((4, 3) if wide else (3, 2))[side]][z]
                 if wide:
-                    spread[rows, near] = data[4 + side][z]
+                    spread[rows, near] = data[(5, 2)[side]][z]
     held, sent = outs[:2]
 
     def write(lanes, out_re, out_im):
@@ -326,9 +326,15 @@
         got = move(sent, mask, stay)
         state = [held, got]
         if edges:
-            state += [move(edges[0], 0, far_pairs), move(edges[1], mask, far_pairs)]
+            far = edges[:2]
         if len(edges) > 2:
-            state += [move(edges[2], 0, near_pairs), move(edges[3], mask, near_pairs)]
+            state.append(move(edges[3], mask, near_pairs))
+            state.append(move(far[1], mask, far_pairs))
+            state.append(move(far[0], 0, far_pairs))
+            state.append(move(edges[2], 0, near_pairs))
+        elif edges:
+            state.append(move(far[1], mask, far_pairs))
+            state.append(move(far[0], 0, far_pairs))
 
     held = held.reshape(2, CHANNELS, BEAMS, BLOCK)
     got = got.reshape(2, CHANNELS, BEAMS, BLOCK)

time: 87.3 us -> 87.4 us (level)
  the two profiles are of different devices: /device:TPU:125 before, /device:TPU:1 now
where the time goes in v3:
time: 87.4 us; the launch traced here: 86.2 us
  starting transfers between devices  50 us (57%)
  waiting for transfers between devices  22.4 us (26%)
  Pallas kernels  12.5 us (14%)
  other arithmetic  0.89 us (1%)
    ppermute x14, starting transfers between devices, move(): return lax.ppermute(value, ('pulse', 'range'), pairs)  50 us
    ppermute x14, waiting for transfers between devices, move(): return lax.ppermute(value, ('pulse', 'range'), pairs)  22.4 us
    pallas_call x4, Pallas kernels, make_tables(): pl.pallas_call(functools.partial(tables_kernel, level), grid=(1,), out_sh...  5.06 us
    pallas_call x4, Pallas kernels, level_call(): call(functools.partial(level_kernel, level), outs, len(operands), TILES *...  4.49 us
    pallas_call x1, Pallas kernels, take_edges(): pl.pallas_call(edges_kernel, out_shape=[shape(UNITS, 16, REACH), shape(2,...  2.24 us
  transfers between devices with their start and end apart: 14, of which 6 were waited for; matrix products, arithmetic and copies ran while one was open for 0% of the time, Pallas kernels for 7%

profile of v3, /device:TPU:1, one launch (start us, length us, event | category | flops | bytes accessed | tf_op | source)
XLA Modules:
  0.0 86.2 jit_solution(5414963381335009859)
XLA Ops:
  0.0 0.0 copy-start
  0.0 0.0 copy-start.2
  0.0 0.0 copy-start.4
  0.0 0.0 copy-start.5
  0.0 0.0 copy-start.6
  0.0 0.0 copy-start.3
  0.0 0.0 copy-start.1
  0.0 2.2 %edges.1 = (bf16[66,16,256]{2,1,0:T(8,128)(2,1)}, bf16[2,16,16,128]{3,2,1,0:T(8,128)(2,1)}) custom-call(bf16[2,16,16,512]{3,2,1,0:T(8,128)(2,1)} %bitcast.12, bf16[4,4,16,16,256]{4,3,2,1,0:T(8,128)(2,1)} %bitcast.11, bf16[4,16,512]{2,1,0:T(8,128)(2,1)} %bitcast.14, s32[4,4]{1,0:T(4,128)} %offsets.9), custom_call_target="tpu_custom_call" | custom-call | flops 1048576 | bytes 1048576 | tf_op jit(solution)/shard_map/edges/pallas_call | solution.py:103
  2.3 8.8 %collective-permute-start = (bf16[66,16,256]{2,1,0:T(8,128)(2,1)}, bf16[66,16,256]{2,1,0:T(8,128)(2,1)S(1)}, u32[]{:S(2)}, u32[]{:S(2)}) collective-permute-start(bf16[66,16,256]{2,1,0:T(8,128)(2,1)} %get-tuple-element.64), channel_id=1, source_target_pairs={{0,1},{1,0},{2,3},{3,2},{4,5},{5,4},{6,7},{7,6},{8,9},{9,8},{10,11... | collective-permute-start | bytes 1622024 | tf_op jit(solution)/shard_map/ppermute | solution.py:304
  11.1 1.9 %collective-permute-start.1 = (bf16[2,16,16,128]{3,2,1,0:T(8,128)(2,1)}, bf16[2,16,16,128]{3,2,1,0:T(8,128)(2,1)S(1)}, u32[]{:S(2)}, u32[]{:S(2)}) collective-permute-start(bf16[2,16,16,128]{3,2,1,0:T(8,128)(2,1)} %get-tuple-element.65), channel_id=1, source_target_pairs={{1,2},{2,1},{5,6},{6,5},{9,10},{10,9},{13,14},{14,13},{17,18},{18,... | collective-permute-start | bytes 393224 | tf_op jit(solution)/shard_map/ppermute | solution.py:304
  13.0 0.0 copy-done
  13.0 0.0 copy-done.2
  13.0 0.0 copy-done.4
  13.0 0.0 copy-done.5
  13.0 0.0 copy-done.6
  13.1 0.0 copy-done.3
  13.1 1.3 %tables0.1 = (bf16[4,256,384]{2,1,0:T(8,128)(2,1)S(1)}, f32[256,512]{1,0:T(8,128)S(1)}, f32[256,512]{1,0:T(8,128)S(1)}, bf16[256,256]{1,0:T(8,128)(2,1)S(1)}) custom-call(bf16[4,4,2,128,256]{4,3,2,1,0:T(8,128)(2,1)S(1)} %copy-done, s32[4,4]{1,0:T(4,128)S(1)} %copy-done.4, bf16[4,1,2,8,512]{4,3,2,1,0:T(8,128)(2,1)S(1)} %copy-done.2, s32[1,16]{1,0:T(1,128)S(1)} %bitcast.15, ...), custom_call_target="tpu_custom_call" | custom-call | flops 134217728 | bytes 2097152 | tf_op jit(solution)/shard_map/tables0/pallas_call | solution.py:175
  14.3 0.0 collective-permute-done.near.refs_1_
  14.3 0.4 reach0.1
  14.7 2.9 %collective-permute-done.1.refs_2_ = bf16[2,16,16,128]{3,2,1,0:T(8,128)(2,1)S(1)} collective-permute-done((bf16[2,16,16,128]{3,2,1,0:T(8,128)(2,1)}, bf16[2,16,16,128]{3,2,1,0:T(8,128)(2,1)S(1)}, u32[]{:S(2)}, u32[]{:S(2)}) %collective-permute-start.1) | collective-permute-done | bytes 131104 | tf_op jit(solution)/shard_map/ppermute | solution.py:304
  17.6 0.0 copy-done.1
  17.6 1.2 %merge0.1 = (bf16[2,128,640]{2,1,0:T(8,128)(2,1)S(1)}, bf16[2,128,640]{2,1,0:T(8,128)(2,1)S(1)}, bf16[2,128,128]{2,1,0:T(8,128)(2,1)S(1)}, bf16[2,128,128]{2,1,0:T(8,128)(2,1)S(1)}) custom-call(bf16[2,16,16,512]{3,2,1,0:T(8,128)(2,1)S(1)} %bitcast.13, bf16[66,16,256]{2,1,0:T(8,128)(2,1)S(1)} %collective-permute-done.near.refs_1_, ...), custom_call_target="tpu_custom_call" | custom-call | flops 536870912 | bytes 1048576 | tf_op jit(solution)/shard_map/merge0/pallas_call | solution.py:285
  18.8 1.9 %collective-permute-start.2 = (bf16[2,128,640]{2,1,0:T(8,128)(2,1)S(1)}, bf16[2,128,640]{2,1,0:T(8,128)(2,1)S(1)}, u32[]{:S(2)}, u32[]{:S(2)}) collective-permute-start(bf16[2,128,640]{2,1,0:T(8,128)(2,1)S(1)} %get-tuple-element.74), channel_id=1, source_target_pairs={{0,64},{1,65},{2,66},{3,67},{4,68},{5,69},{6,70},{7,71},{8,72},{9,... | collective-permute-start | bytes 983048 | tf_op jit(solution)/shard_map/ppermute | solution.py:304
  20.7 4.3 %collective-permute-start.3 = (bf16[2,128,128]{2,1,0:T(8,128)(2,1)S(1)}, bf16[2,128,128]{2,1,0:T(8,128)(2,1)S(1)}, u32[]{:S(2)}, u32[]{:S(2)}) collective-permute-start(bf16[2,128,128]{2,1,0:T(8,128)(2,1)S(1)} %get-tuple-element.75), channel_id=1, source_target_pairs={{1,66},{2,65},{5,70},{6,69},{9,74},{10,73},{13,78},{14,77},{17,82}... | collective-permute-start | bytes 196616 | tf_op jit(solution)/shard_map/ppermute | solution.py:304
  25.0 3.4 %collective-permute-start.4 = (bf16[2,128,128]{2,1,0:T(8,128)(2,1)S(1)}, bf16[2,128,128]{2,1,0:T(8,128)(2,1)S(1)}, u32[]{:S(2)}, u32[]{:S(2)}) collective-permute-start(bf16[2,128,128]{2,1,0:T(8,128)(2,1)S(1)} %get-tuple-element.76), channel_id=1, source_target_pairs={{1,2},{2,1},{5,6},{6,5},{9,10},{10,9},{13,14},{14,13},{17,18},{18,... | collective-permute-start | bytes 196616 | tf_op jit(solution)/shard_map/ppermute | solution.py:304
  28.4 1.3 %tables1.1 = (bf16[4,256,384]{2,1,0:T(8,128)(2,1)S(1)}, f32[256,512]{1,0:T(8,128)S(1)}, f32[256,512]{1,0:T(8,128)S(1)}, bf16[256,256]{1,0:T(8,128)(2,1)S(1)}) custom-call(bf16[4,4,2,128,256]{4,3,2,1,0:T(8,128)(2,1)S(1)} %copy-done, s32[4,4]{1,0:T(4,128)S(1)} %copy-done.4, bf16[4,1,2,8,512]{4,3,2,1,0:T(8,128)(2,1)S(1)} %copy-done.2, s32[1,16]{1,0:T(1,128)S(1)} %bitcast.17, ...), custom_call_target="tpu_custom_call" | custom-call | flops 134217728 | bytes 2097152 | tf_op jit(solution)/shard_map/tables1/pallas_call | solution.py:175
  29.7 1.3 %tables2.1 = (bf16[4,256,384]{2,1,0:T(8,128)(2,1)S(1)}, f32[256,512]{1,0:T(8,128)S(1)}, f32[256,512]{1,0:T(8,128)S(1)}, bf16[256,256]{1,0:T(8,128)(2,1)S(1)}) custom-call(bf16[4,4,2,128,256]{4,3,2,1,0:T(8,128)(2,1)S(1)} %copy-done, s32[4,4]{1,0:T(4,128)S(1)} %copy-done.4, bf16[4,1,2,8,512]{4,3,2,1,0:T(8,128)(2,1)S(1)} %copy-done.2, s32[1,16]{1,0:T(1,128)S(1)} %bitcast.18, ...), custom_call_target="tpu_custom_call" | custom-call | flops 134217728 | bytes 2097152 | tf_op jit(solution)/shard_map/tables2/pallas_call | solution.py:175
  30.9 1.3 %tables3.1 = (bf16[4,256,384]{2,1,0:T(8,128)(2,1)S(1)}, f32[256,512]{1,0:T(8,128)S(1)}, f32[256,512]{1,0:T(8,128)S(1)}, bf16[256,256]{1,0:T(8,128)(2,1)S(1)}) custom-call(bf16[4,4,2,128,256]{4,3,2,1,0:T(8,128)(2,1)S(1)} %copy-done, s32[4,4]{1,0:T(4,128)S(1)} %copy-done.4, bf16[4,1,2,8,512]{4,3,2,1,0:T(8,128)(2,1)S(1)} %copy-done.2, s32[1,16]{1,0:T(1,128)S(1)} %bitcast.19, ...), custom_call_target="tpu_custom_call" | custom-call | flops 134217728 | bytes 2097152 | tf_op jit(solution)/shard_map/tables3/pallas_call | solution.py:175
  32.2 0.4 reach2.1
  32.6 0.0 collective-permute-done.3.refs_2_
  32.6 0.0 collective-permute-done.4.refs_3_
  32.6 0.4 collective-permute-done.2.refs_1_
  33.0 1.0 %merge1.1 = (bf16[2,128,512]{2,1,0:T(8,128)(2,1)S(1)}, bf16[2,128,512]{2,1,0:T(8,128)(2,1)S(1)}, bf16[2,128,128]{2,1,0:T(8,128)(2,1)S(1)}, bf16[2,128,128]{2,1,0...) custom-call(bf16[2,128,640]{2,1,0:T(8,128)(2,1)S(1)} %get-tuple-element.92.refs_0_, ...), custom_call_target="tpu_custom_call" | custom-call | flops 536870912 | bytes 1048576 | tf_op jit(solution)/shard_map/merge1/pallas_call | solution.py:285
  34.0 2.7 %collective-permute-start.5 = (bf16[2,128,512]{2,1,0:T(8,128)(2,1)S(1)}, bf16[2,128,512]{2,1,0:T(8,128)(2,1)S(1)}, u32[]{:S(2)}, u32[]{:S(2)}) collective-permute-start(bf16[2,128,512]{2,1,0:T(8,128)(2,1)S(1)} %get-tuple-element.101), channel_id=1, source_target_pairs={{0,32},{1,33},{2,34},{3,35},{4,36},{5,37},{6,38},{7,39},{8,40},{9,... | collective-permute-start | bytes 786440 | tf_op jit(solution)/shard_map/ppermute | solution.py:304
  36.7 3.1 %collective-permute-start.6 = (bf16[2,128,256]{2,1,0:T(8,128)(2,1)S(1)}, bf16[2,128,256]{2,1,0:T(8,128)(2,1)S(1)}, u32[]{:S(2)}, u32[]{:S(2)}) collective-permute-start(bf16[2,128,256]{2,1,0:T(8,128)(2,1)S(1)} %get-tuple-element.102), channel_id=1, source_target_pairs={{0,33},{1,32},{2,35},{3,34},{4,37},{5,36},{6,39},{7,38},{8,41},{9,... | collective-permute-start | bytes 393224 | tf_op jit(solution)/shard_map/ppermute | solution.py:304
  39.9 1.9 %collective-permute-start.9 = (bf16[2,128,256]{2,1,0:T(8,128)(2,1)S(1)}, bf16[2,128,256]{2,1,0:T(8,128)(2,1)S(1)}, u32[]{:S(2)}, u32[]{:S(2)}) collective-permute-start(bf16[2,128,256]{2,1,0:T(8,128)(2,1)S(1)} %get-tuple-element.105), channel_id=1, source_target_pairs={{0,1},{1,0},{2,3},{3,2},{4,5},{5,4},{6,7},{7,6},{8,9},{9,8},{10,11... | collective-permute-start | bytes 393224 | tf_op jit(solution)/shard_map/ppermute | solution.py:304
  41.8 3.9 %collective-permute-start.7 = (bf16[2,128,128]{2,1,0:T(8,128)(2,1)S(1)}, bf16[2,128,128]{2,1,0:T(8,128)(2,1)S(1)}, u32[]{:S(2)}, u32[]{:S(2)}) collective-permute-start(bf16[2,128,128]{2,1,0:T(8,128)(2,1)S(1)} %get-tuple-element.103), channel_id=1, source_target_pairs={{1,34},{2,33},{5,38},{6,37},{9,42},{10,41},{13,46},{14,45},{17,50}... | collective-permute-start | bytes 196616 | tf_op jit(solution)/shard_map/ppermute | solution.py:304
  45.7 2.5 %collective-permute-start.8 = (bf16[2,128,128]{2,1,0:T(8,128)(2,1)S(1)}, bf16[2,128,128]{2,1,0:T(8,128)(2,1)S(1)}, u32[]{:S(2)}, u32[]{:S(2)}) collective-permute-start(bf16[2,128,128]{2,1,0:T(8,128)(2,1)S(1)} %get-tuple-element.104), channel_id=1, source_target_pairs={{1,2},{2,1},{5,6},{6,5},{9,10},{10,9},{13,14},{14,13},{17,18},{18,... | collective-permute-start | bytes 196616 | tf_op jit(solution)/shard_map/ppermute | solution.py:304
  48.2 0.1 collective-permute-done.7.refs_3_
  48.3 3.0 %collective-permute-done.8.refs_4_ = bf16[2,128,128]{2,1,0:T(8,128)(2,1)S(1)} collective-permute-done((bf16[2,128,128]{2,1,0:T(8,128)(2,1)S(1)}, bf16[2,128,128]{2,1,0:T(8,128)(2,1)S(1)}, u32[]{:S(2)}, u32[]{:S(2)}) %collective-permute-start.8) | collective-permute-done | bytes 65568 | tf_op jit(solution)/shard_map/ppermute | solution.py:304
  51.3 0.0 collective-permute-done.6.refs_2_
  51.3 0.0 collective-permute-done.9.refs_5_
  51.3 0.0 collective-permute-done.5.refs_1_
  51.3 1.2 %merge2.1 = (bf16[2,128,640]{2,1,0:T(8,128)(2,1)S(1)}, bf16[2,128,640]{2,1,0:T(8,128)(2,1)S(1)}, bf16[2,128,128]{2,1,0:T(8,128)(2,1)S(1)}, bf16[2,128,128]{2,1,0:T(8,128)(2,1)S(1)}) custom-call(bf16[2,128,512]{2,1,0:T(8,128)(2,1)S(1)} %get-tuple-element.100.refs_0_, bf16[2,128,512]{2,1,0:T(8,128)(2,1)S(1)} %collective-permute-done.5.refs_1_, ...), custom_call_target="tpu_custom_call" | custom-call | flops 536870912 | bytes 1048576 | tf_op jit(solution)/shard_map/merge2/pallas_call | solution.py:285
  52.6 6.1 %collective-permute-start.10 = (bf16[2,128,640]{2,1,0:T(8,128)(2,1)S(1)}, bf16[2,128,640]{2,1,0:T(8,128)(2,1)S(1)}, u32[]{:S(2)}, u32[]{:S(2)}) collective-permute-start(bf16[2,128,640]{2,1,0:T(8,128)(2,1)S(1)} %get-tuple-element.114), channel_id=1, source_target_pairs={{0,16},{1,17},{2,18},{3,19},{4,20},{5,21},{6,22},{7,23},{8,24},{9,... | collective-permute-start | bytes 983048 | tf_op jit(solution)/shard_map/ppermute | solution.py:304
  58.7 3.7 %collective-permute-start.11 = (bf16[2,128,128]{2,1,0:T(8,128)(2,1)S(1)}, bf16[2,128,128]{2,1,0:T(8,128)(2,1)S(1)}, u32[]{:S(2)}, u32[]{:S(2)}) collective-permute-start(bf16[2,128,128]{2,1,0:T(8,128)(2,1)S(1)} %get-tuple-element.115), channel_id=1, source_target_pairs={{1,18},{2,17},{5,22},{6,21},{9,26},{10,25},{13,30},{14,29},{17,2},... | collective-permute-start | bytes 196616 | tf_op jit(solution)/shard_map/ppermute | solution.py:304
  62.3 2.8 %collective-permute-start.12 = (bf16[2,128,128]{2,1,0:T(8,128)(2,1)S(1)}, bf16[2,128,128]{2,1,0:T(8,128)(2,1)S(1)}, u32[]{:S(2)}, u32[]{:S(2)}) collective-permute-start(bf16[2,128,128]{2,1,0:T(8,128)(2,1)S(1)} %get-tuple-element.116), channel_id=1, source_target_pairs={{1,2},{2,1},{5,6},{6,5},{9,10},{10,9},{13,14},{14,13},{17,18},{18,... | collective-permute-start | bytes 196616 | tf_op jit(solution)/shard_map/ppermute | solution.py:304
  65.2 6.4 %collective-permute-done.11.refs_2_ = bf16[2,128,128]{2,1,0:T(8,128)(2,1)S(1)} collective-permute-done((bf16[2,128,128]{2,1,0:T(8,128)(2,1)S(1)}, bf16[2,128,128]{2,1,0:T(8,128)(2,1)S(1)}, u32[]{:S(2)}, u32[]{:S(2)}) %collective-permute-start.11) | collective-permute-done | bytes 65568 | tf_op jit(solution)/shard_map/ppermute | solution.py:304
  71.6 0.0 collective-permute-done.12.refs_3_
  71.6 0.0 collective-permute-done.10.refs_1_
  71.6 1.0 %merge3.1 = (bf16[2,128,512]{2,1,0:T(8,128)(2,1)S(1)}, bf16[2,128,512]{2,1,0:T(8,128)(2,1)S(1)}) custom-call(bf16[2,128,640]{2,1,0:T(8,128)(2,1)S(1)} %get-tuple-element.113.refs_0_, bf16[2,128,640]{2,1,0:T(8,128)(2,1)S(1)} %collective-permute-done.10.refs_1_, bf16[2,128,128]{2,1,0:T(8,128)(2,1)S(1)} %collective-permute-done.11.refs_2_, ...), custom_call_target="tpu_custom_call" | custom-call | flops 536870912 | bytes 1048576 | tf_op jit(solution)/shard_map/merge3/pallas_call | solution.py:285
  72.6 3.1 %collective-permute-start.13 = (bf16[2,128,512]{2,1,0:T(8,128)(2,1)S(1)}, bf16[2,128,512]{2,1,0:T(8,128)(2,1)S(1)}, u32[]{:S(2)}, u32[]{:S(2)}) collective-permute-start(bf16[2,128,512]{2,1,0:T(8,128)(2,1)S(1)} %get-tuple-element.121), channel_id=1, source_target_pairs={{0,8},{1,9},{2,10},{3,11},{4,12},{5,13},{6,14},{7,15},{8,0},{9,1},... | collective-permute-start | bytes 786440 | tf_op jit(solution)/shard_map/ppermute | solution.py:304
  75.7 9.6 %collective-permute-done.13 = bf16[2,128,512]{2,1,0:T(8,128)(2,1)S(1)} collective-permute-done((bf16[2,128,512]{2,1,0:T(8,128)(2,1)S(1)}, bf16[2,128,512]{2,1,0:T(8,128)(2,1)S(1)}, u32[]{:S(2)}, u32[]{:S(2)}) %collective-permute-start.13) | collective-permute-done | bytes 262176 | tf_op jit(solution)/shard_map/ppermute | solution.py:304
  85.3 0.9 maximum_bitcast_fusion
  (1 shorter events, 0.0 us)
Async XLA Ops:
  0.0 13.0 %copy-start = (bf16[4,4,2,128,256]{4,3,2,1,0:T(8,128)(2,1)S(1)}, bf16[4,4,2,128,256]{4,3,2,1,0:T(8,128)(2,1)}, u32[]{:S(2)}) copy-start(bf16[4,4,2,128,256]{4,3,2,1,0:T(8,128)(2,1)} %taps.7) | copy-start | bytes 6291460
  0.0 13.0 %copy-start.2 = (bf16[4,1,2,8,512]{4,3,2,1,0:T(8,128)(2,1)S(1)}, bf16[4,1,2,8,512]{4,3,2,1,0:T(8,128)(2,1)}, u32[]{:S(2)}) copy-start(bf16[4,1,2,8,512]{4,3,2,1,0:T(8,128)(2,1)} %ramp.7) | copy-start | bytes 196612
  0.0 13.0 %copy-start.4 = (s32[4,4]{1,0:T(4,128)S(1)}, s32[4,4]{1,0:T(4,128)}, u32[]{:S(2)}) copy-start(s32[4,4]{1,0:T(4,128)} %offsets.9) | copy-start | bytes 196
  0.0 13.0 %copy-start.5 = (s32[16]{0:T(128)S(1)}, s32[16]{0:T(128)}, u32[]{:S(2)}) copy-start(s32[16]{0:T(128)} %param.12) | copy-start | bytes 196
  0.0 13.0 %copy-start.6 = (f32[8]{0:T(128)S(1)}, f32[8]{0:T(128)}, u32[]{:S(2)}) copy-start(f32[8]{0:T(128)} %param.13) | copy-start | bytes 100
  0.0 13.0 %copy-start.3 = (bf16[4,1,2,8,16]{4,3,2,1,0:T(8,128)(2,1)S(1)}, bf16[4,1,2,8,16]{4,3,2,1,0:T(8,128)(2,1)}, u32[]{:S(2)}) copy-start(bf16[4,1,2,8,16]{4,3,2,1,0:T(8,128)(2,1)} %beam.7) | copy-start | bytes 6148
  0.0 17.5 %copy-start.1 = (bf16[1,2,16,16,512]{4,3,2,1,0:T(8,128)(2,1)S(1)}, bf16[1,2,16,16,512]{4,3,2,1,0:T(8,128)(2,1)}, u32[]{:S(2)}) copy-start(bf16[1,2,16,16,512]{4,3,2,1,0:T(8,128)(2,1)} %param.7) | copy-start | bytes 1572868
  2.3 12.0 %collective-permute-start = (bf16[66,16,256]{2,1,0:T(8,128)(2,1)}, bf16[66,16,256]{2,1,0:T(8,128)(2,1)S(1)}, u32[]{:S(2)}, u32[]{:S(2)}) collective-permute-start(bf16[66,16,256]{2,1,0:T(8,128)(2,1)} %get-tuple-element.64), channel_id=1, source_target_pairs={{0,1},{1,0},{2,3},{3,2},{4,5},{5,4},{6,7},{7,6},{8,9},{9,8},{10,11... | collective-permute-start | bytes 1622024 | tf_op jit(solution)/shard_map/ppermute | solution.py:304
  11.1 6.5 %collective-permute-start.1 = (bf16[2,16,16,128]{3,2,1,0:T(8,128)(2,1)}, bf16[2,16,16,128]{3,2,1,0:T(8,128)(2,1)S(1)}, u32[]{:S(2)}, u32[]{:S(2)}) collective-permute-start(bf16[2,16,16,128]{3,2,1,0:T(8,128)(2,1)} %get-tuple-element.65), channel_id=1, source_target_pairs={{1,2},{2,1},{5,6},{6,5},{9,10},{10,9},{13,14},{14,13},{17,18},{18,... | collective-permute-start | bytes 393224 | tf_op jit(solution)/shard_map/ppermute | solution.py:304
  18.8 14.1 %collective-permute-start.2 = (bf16[2,128,640]{2,1,0:T(8,128)(2,1)S(1)}, bf16[2,128,640]{2,1,0:T(8,128)(2,1)S(1)}, u32[]{:S(2)}, u32[]{:S(2)}) collective-permute-start(bf16[2,128,640]{2,1,0:T(8,128)(2,1)S(1)} %get-tuple-element.74), channel_id=1, source_target_pairs={{0,64},{1,65},{2,66},{3,67},{4,68},{5,69},{6,70},{7,71},{8,72},{9,... | collective-permute-start | bytes 983048 | tf_op jit(solution)/shard_map/ppermute | solution.py:304
  20.7 11.8 %collective-permute-start.3 = (bf16[2,128,128]{2,1,0:T(8,128)(2,1)S(1)}, bf16[2,128,128]{2,1,0:T(8,128)(2,1)S(1)}, u32[]{:S(2)}, u32[]{:S(2)}) collective-permute-start(bf16[2,128,128]{2,1,0:T(8,128)(2,1)S(1)} %get-tuple-element.75), channel_id=1, source_target_pairs={{1,66},{2,65},{5,70},{6,69},{9,74},{10,73},{13,78},{14,77},{17,82}... | collective-permute-start | bytes 196616 | tf_op jit(solution)/shard_map/ppermute | solution.py:304
  25.0 7.6 %collective-permute-start.4 = (bf16[2,128,128]{2,1,0:T(8,128)(2,1)S(1)}, bf16[2,128,128]{2,1,0:T(8,128)(2,1)S(1)}, u32[]{:S(2)}, u32[]{:S(2)}) collective-permute-start(bf16[2,128,128]{2,1,0:T(8,128)(2,1)S(1)} %get-tuple-element.76), channel_id=1, source_target_pairs={{1,2},{2,1},{5,6},{6,5},{9,10},{10,9},{13,14},{14,13},{17,18},{18,... | collective-permute-start | bytes 196616 | tf_op jit(solution)/shard_map/ppermute | solution.py:304
  34.0 17.3 %collective-permute-start.5 = (bf16[2,128,512]{2,1,0:T(8,128)(2,1)S(1)}, bf16[2,128,512]{2,1,0:T(8,128)(2,1)S(1)}, u32[]{:S(2)}, u32[]{:S(2)}) collective-permute-start(bf16[2,128,512]{2,1,0:T(8,128)(2,1)S(1)} %get-tuple-element.101), channel_id=1, source_target_pairs={{0,32},{1,33},{2,34},{3,35},{4,36},{5,37},{6,38},{7,39},{8,40},{9,... | collective-permute-start | bytes 786440 | tf_op jit(solution)/shard_map/ppermute | solution.py:304
  36.7 14.6 %collective-permute-start.6 = (bf16[2,128,256]{2,1,0:T(8,128)(2,1)S(1)}, bf16[2,128,256]{2,1,0:T(8,128)(2,1)S(1)}, u32[]{:S(2)}, u32[]{:S(2)}) collective-permute-start(bf16[2,128,256]{2,1,0:T(8,128)(2,1)S(1)} %get-tuple-element.102), channel_id=1, source_target_pairs={{0,33},{1,32},{2,35},{3,34},{4,37},{5,36},{6,39},{7,38},{8,41},{9,... | collective-permute-start | bytes 393224 | tf_op jit(solution)/shard_map/ppermute | solution.py:304
  39.9 11.5 %collective-permute-start.9 = (bf16[2,128,256]{2,1,0:T(8,128)(2,1)S(1)}, bf16[2,128,256]{2,1,0:T(8,128)(2,1)S(1)}, u32[]{:S(2)}, u32[]{:S(2)}) collective-permute-start(bf16[2,128,256]{2,1,0:T(8,128)(2,1)S(1)} %get-tuple-element.105), channel_id=1, source_target_pairs={{0,1},{1,0},{2,3},{3,2},{4,5},{5,4},{6,7},{7,6},{8,9},{9,8},{10,11... | collective-permute-start | bytes 393224 | tf_op jit(solution)/shard_map/ppermute | solution.py:304
  41.8 6.5 %collective-permute-start.7 = (bf16[2,128,128]{2,1,0:T(8,128)(2,1)S(1)}, bf16[2,128,128]{2,1,0:T(8,128)(2,1)S(1)}, u32[]{:S(2)}, u32[]{:S(2)}) collective-permute-start(bf16[2,128,128]{2,1,0:T(8,128)(2,1)S(1)} %get-tuple-element.103), channel_id=1, source_target_pairs={{1,34},{2,33},{5,38},{6,37},{9,42},{10,41},{13,46},{14,45},{17,50}... | collective-permute-start | bytes 196616 | tf_op jit(solution)/shard_map/ppermute | solution.py:304
  45.7 5.6 %collective-permute-start.8 = (bf16[2,128,128]{2,1,0:T(8,128)(2,1)S(1)}, bf16[2,128,128]{2,1,0:T(8,128)(2,1)S(1)}, u32[]{:S(2)}, u32[]{:S(2)}) collective-permute-start(bf16[2,128,128]{2,1,0:T(8,128)(2,1)S(1)} %get-tuple-element.104), channel_id=1, source_target_pairs={{1,2},{2,1},{5,6},{6,5},{9,10},{10,9},{13,14},{14,13},{17,18},{18,... | collective-permute-start | bytes 196616 | tf_op jit(solution)/shard_map/ppermute | solution.py:304
  52.6 19.0 %collective-permute-start.10 = (bf16[2,128,640]{2,1,0:T(8,128)(2,1)S(1)}, bf16[2,128,640]{2,1,0:T(8,128)(2,1)S(1)}, u32[]{:S(2)}, u32[]{:S(2)}) collective-permute-start(bf16[2,128,640]{2,1,0:T(8,128)(2,1)S(1)} %get-tuple-element.114), channel_id=1, source_target_pairs={{0,16},{1,17},{2,18},{3,19},{4,20},{5,21},{6,22},{7,23},{8,24},{9,... | collective-permute-start | bytes 983048 | tf_op jit(solution)/shard_map/ppermute | solution.py:304
  58.7 12.9 %collective-permute-start.11 = (bf16[2,128,128]{2,1,0:T(8,128)(2,1)S(1)}, bf16[2,128,128]{2,1,0:T(8,128)(2,1)S(1)}, u32[]{:S(2)}, u32[]{:S(2)}) collective-permute-start(bf16[2,128,128]{2,1,0:T(8,128)(2,1)S(1)} %get-tuple-element.115), channel_id=1, source_target_pairs={{1,18},{2,17},{5,22},{6,21},{9,26},{10,25},{13,30},{14,29},{17,2},... | collective-permute-start | bytes 196616 | tf_op jit(solution)/shard_map/ppermute | solution.py:304
  62.3 9.3 %collective-permute-start.12 = (bf16[2,128,128]{2,1,0:T(8,128)(2,1)S(1)}, bf16[2,128,128]{2,1,0:T(8,128)(2,1)S(1)}, u32[]{:S(2)}, u32[]{:S(2)}) collective-permute-start(bf16[2,128,128]{2,1,0:T(8,128)(2,1)S(1)} %get-tuple-element.116), channel_id=1, source_target_pairs={{1,2},{2,1},{5,6},{6,5},{9,10},{10,9},{13,14},{14,13},{17,18},{18,... | collective-permute-start | bytes 196616 | tf_op jit(solution)/shard_map/ppermute | solution.py:304
  72.6 12.7 %collective-permute-start.13 = (bf16[2,128,512]{2,1,0:T(8,128)(2,1)S(1)}, bf16[2,128,512]{2,1,0:T(8,128)(2,1)S(1)}, u32[]{:S(2)}, u32[]{:S(2)}) collective-permute-start(bf16[2,128,512]{2,1,0:T(8,128)(2,1)S(1)} %get-tuple-element.121), channel_id=1, source_target_pairs={{0,8},{1,9},{2,10},{3,11},{4,12},{5,13},{6,14},{7,15},{8,0},{9,1},... | collective-permute-start | bytes 786440 | tf_op jit(solution)/shard_map/ppermute | solution.py:304

commit v4 on v3

--- a/solution.py
+++ b/solution.py
@@ -14,6 +14,7 @@
 BITS = (4, 3, 2, 1)
 BLOCK = 512
 TILES = BLOCK // TILE
+LAG = 2
 VMEM_LIMIT = 24 * 1024 * 1024
 BF = jnp.bfloat16
 F32 = jnp.float32
@@ -205,15 +206,11 @@
     if wide:
         order.append((reach, 0, jnp.where(odd == 1, 0, TILES)))
     parts = []
-    for (shifted, _, _), index, place in order:
-        window = spread[:, pl.ds(aligned(place * TILE), 3 * TILE)]
-        both = lax.dot_general(window, shifted[index], (((1,), (1,)), ((), ())), preferred_element_type=F32)
-        real = both[:rows, :TILE] - both[rows:, TILE:]
-        imag = both[:rows, TILE:] + both[rows:, :TILE]
-        parts.append(jnp.concatenate([real, imag], axis=1).astype(BF))
-    for ((_, cos_ref, sin_ref), index, place), part in zip(order, parts):
+
+    def finish(step):
+        (_, cos_ref, sin_ref), index, place = order[step]
         lanes = slice(index * TILE, (index + 1) * TILE)
-        mixed = jnp.dot(mix, part, preferred_element_type=F32)
+        mixed = jnp.dot(mix, parts[step], preferred_element_type=F32)
         mixed_re = mixed[:, :TILE]
         mixed_im = mixed[:, TILE:]
         cosine = cos_ref[:, lanes]
@@ -221,6 +218,17 @@
         out_re = (mixed_re * cosine + mixed_im * sine).astype(BF)
         out_im = (mixed_im * cosine - mixed_re * sine).astype(BF)
         write(pl.ds(aligned(place * TILE), TILE), out_re, out_im)
+
+    for (shifted, _, _), index, place in order:
+        window = spread[:, pl.ds(aligned(place * TILE), 3 * TILE)]
+        both = lax.dot_general(window, shifted[index], (((1,), (1,)), ((), ())), preferred_element_type=F32)
+        real = both[:rows, :TILE] - both[rows:, TILE:]
+        imag = both[:rows, TILE:] + both[rows:, :TILE]
+        parts.append(jnp.concatenate([real, imag], axis=1).astype(BF))
+        if len(parts) > LAG:
+            finish(len(parts) - 1 - LAG)
+    for step in range(max(len(order) - LAG, 0), len(order)):
+        finish(step)
 
 
 def level_kernel(level, *refs):

time: 87.4 us -> 87.8 us (level)
  no operation moved by 1% of the time
where the time goes in v4:
time: 87.8 us; the launch traced here: 86.6 us
  starting transfers between devices  50.1 us (57%)
  waiting for transfers between devices  22.3 us (25%)
  Pallas kernels  12.9 us (15%)
  other arithmetic  0.89 us (1%)
    ppermute x14, starting transfers between devices, move(): return lax.ppermute(value, ('pulse', 'range'), pairs)  50.1 us
    ppermute x14, waiting for transfers between devices, move(): return lax.ppermute(value, ('pulse', 'range'), pairs)  22.3 us
    pallas_call x4, Pallas kernels, make_tables(): pl.pallas_call(functools.partial(tables_kernel, level), grid=(1,), out_sh...  5.06 us
    pallas_call x4, Pallas kernels, level_call(): call(functools.partial(level_kernel, level), outs, len(operands), TILES *...  4.92 us
    pallas_call x1, Pallas kernels, take_edges(): pl.pallas_call(edges_kernel, out_shape=[shape(UNITS, 16, REACH), shape(2,...  2.24 us
  transfers between devices with their start and end apart: 14, of which 6 were waited for; matrix products, arithmetic and copies ran while one was open for 0% of the time, Pallas kernels for 7%

profile of v4, /device:TPU:1, one launch (start us, length us, event | category | flops | bytes accessed | tf_op | source)
XLA Modules:
  0.0 86.6 jit_solution(12584385999596822397)
XLA Ops:
  0.0 0.0 copy-start
  0.0 0.0 copy-start.2
  0.0 0.0 copy-start.4
  0.0 0.0 copy-start.5
  0.0 0.0 copy-start.6
  0.0 0.0 copy-start.3
  0.0 0.0 copy-start.1
  0.0 2.2 %edges.1 = (bf16[66,16,256]{2,1,0:T(8,128)(2,1)}, bf16[2,16,16,128]{3,2,1,0:T(8,128)(2,1)}) custom-call(bf16[2,16,16,512]{3,2,1,0:T(8,128)(2,1)} %bitcast.12, bf16[4,4,16,16,256]{4,3,2,1,0:T(8,128)(2,1)} %bitcast.11, bf16[4,16,512]{2,1,0:T(8,128)(2,1)} %bitcast.14, s32[4,4]{1,0:T(4,128)} %offsets.9), custom_call_target="tpu_custom_call" | custom-call | flops 1048576 | bytes 1048576 | tf_op jit(solution)/shard_map/edges/pallas_call | solution.py:104
  2.3 8.8 %collective-permute-start = (bf16[66,16,256]{2,1,0:T(8,128)(2,1)}, bf16[66,16,256]{2,1,0:T(8,128)(2,1)S(1)}, u32[]{:S(2)}, u32[]{:S(2)}) collective-permute-start(bf16[66,16,256]{2,1,0:T(8,128)(2,1)} %get-tuple-element.64), channel_id=1, source_target_pairs={{0,1},{1,0},{2,3},{3,2},{4,5},{5,4},{6,7},{7,6},{8,9},{9,8},{10,11... | collective-permute-start | bytes 1622024 | tf_op jit(solution)/shard_map/ppermute | solution.py:312
  11.1 1.9 %collective-permute-start.1 = (bf16[2,16,16,128]{3,2,1,0:T(8,128)(2,1)}, bf16[2,16,16,128]{3,2,1,0:T(8,128)(2,1)S(1)}, u32[]{:S(2)}, u32[]{:S(2)}) collective-permute-start(bf16[2,16,16,128]{3,2,1,0:T(8,128)(2,1)} %get-tuple-element.65), channel_id=1, source_target_pairs={{1,2},{2,1},{5,6},{6,5},{9,10},{10,9},{13,14},{14,13},{17,18},{18,... | collective-permute-start | bytes 393224 | tf_op jit(solution)/shard_map/ppermute | solution.py:312
  13.0 0.0 copy-done
  13.0 0.0 copy-done.2
  13.0 0.0 copy-done.4
  13.0 0.0 copy-done.5
  13.0 0.0 copy-done.6
  13.1 0.0 copy-done.3
  13.1 1.3 %tables0.1 = (bf16[4,256,384]{2,1,0:T(8,128)(2,1)S(1)}, f32[256,512]{1,0:T(8,128)S(1)}, f32[256,512]{1,0:T(8,128)S(1)}, bf16[256,256]{1,0:T(8,128)(2,1)S(1)}) custom-call(bf16[4,4,2,128,256]{4,3,2,1,0:T(8,128)(2,1)S(1)} %copy-done, s32[4,4]{1,0:T(4,128)S(1)} %copy-done.4, bf16[4,1,2,8,512]{4,3,2,1,0:T(8,128)(2,1)S(1)} %copy-done.2, s32[1,16]{1,0:T(1,128)S(1)} %bitcast.15, ...), custom_call_target="tpu_custom_call" | custom-call | flops 134217728 | bytes 2097152 | tf_op jit(solution)/shard_map/tables0/pallas_call | solution.py:176
  14.3 0.0 collective-permute-done.near.refs_1_
  14.3 0.4 reach0.1
  14.7 2.9 %collective-permute-done.1.refs_2_ = bf16[2,16,16,128]{3,2,1,0:T(8,128)(2,1)S(1)} collective-permute-done((bf16[2,16,16,128]{3,2,1,0:T(8,128)(2,1)}, bf16[2,16,16,128]{3,2,1,0:T(8,128)(2,1)S(1)}, u32[]{:S(2)}, u32[]{:S(2)}) %collective-permute-start.1) | collective-permute-done | bytes 131104 | tf_op jit(solution)/shard_map/ppermute | solution.py:312
  17.6 0.0 copy-done.1
  17.6 1.3 %merge0.1 = (bf16[2,128,640]{2,1,0:T(8,128)(2,1)S(1)}, bf16[2,128,640]{2,1,0:T(8,128)(2,1)S(1)}, bf16[2,128,128]{2,1,0:T(8,128)(2,1)S(1)}, bf16[2,128,128]{2,1,0:T(8,128)(2,1)S(1)}) custom-call(bf16[2,16,16,512]{3,2,1,0:T(8,128)(2,1)S(1)} %bitcast.13, bf16[66,16,256]{2,1,0:T(8,128)(2,1)S(1)} %collective-permute-done.near.refs_1_, ...), custom_call_target="tpu_custom_call" | custom-call | flops 536870912 | bytes 1048576 | tf_op jit(solution)/shard_map/merge0/pallas_call | solution.py:293
  18.9 1.9 %collective-permute-start.2 = (bf16[2,128,640]{2,1,0:T(8,128)(2,1)S(1)}, bf16[2,128,640]{2,1,0:T(8,128)(2,1)S(1)}, u32[]{:S(2)}, u32[]{:S(2)}) collective-permute-start(bf16[2,128,640]{2,1,0:T(8,128)(2,1)S(1)} %get-tuple-element.74), channel_id=1, source_target_pairs={{0,64},{1,65},{2,66},{3,67},{4,68},{5,69},{6,70},{7,71},{8,72},{9,... | collective-permute-start | bytes 983048 | tf_op jit(solution)/shard_map/ppermute | solution.py:312
  20.8 4.3 %collective-permute-start.3 = (bf16[2,128,128]{2,1,0:T(8,128)(2,1)S(1)}, bf16[2,128,128]{2,1,0:T(8,128)(2,1)S(1)}, u32[]{:S(2)}, u32[]{:S(2)}) collective-permute-start(bf16[2,128,128]{2,1,0:T(8,128)(2,1)S(1)} %get-tuple-element.75), channel_id=1, source_target_pairs={{1,66},{2,65},{5,70},{6,69},{9,74},{10,73},{13,78},{14,77},{17,82}... | collective-permute-start | bytes 196616 | tf_op jit(solution)/shard_map/ppermute | solution.py:312
  25.1 3.4 %collective-permute-start.4 = (bf16[2,128,128]{2,1,0:T(8,128)(2,1)S(1)}, bf16[2,128,128]{2,1,0:T(8,128)(2,1)S(1)}, u32[]{:S(2)}, u32[]{:S(2)}) collective-permute-start(bf16[2,128,128]{2,1,0:T(8,128)(2,1)S(1)} %get-tuple-element.76), channel_id=1, source_target_pairs={{1,2},{2,1},{5,6},{6,5},{9,10},{10,9},{13,14},{14,13},{17,18},{18,... | collective-permute-start | bytes 196616 | tf_op jit(solution)/shard_map/ppermute | solution.py:312
  28.4 1.3 %tables1.1 = (bf16[4,256,384]{2,1,0:T(8,128)(2,1)S(1)}, f32[256,512]{1,0:T(8,128)S(1)}, f32[256,512]{1,0:T(8,128)S(1)}, bf16[256,256]{1,0:T(8,128)(2,1)S(1)}) custom-call(bf16[4,4,2,128,256]{4,3,2,1,0:T(8,128)(2,1)S(1)} %copy-done, s32[4,4]{1,0:T(4,128)S(1)} %copy-done.4, bf16[4,1,2,8,512]{4,3,2,1,0:T(8,128)(2,1)S(1)} %copy-done.2, s32[1,16]{1,0:T(1,128)S(1)} %bitcast.17, ...), custom_call_target="tpu_custom_call" | custom-call | flops 134217728 | bytes 2097152 | tf_op jit(solution)/shard_map/tables1/pallas_call | solution.py:176
  29.7 1.3 %tables2.1 = (bf16[4,256,384]{2,1,0:T(8,128)(2,1)S(1)}, f32[256,512]{1,0:T(8,128)S(1)}, f32[256,512]{1,0:T(8,128)S(1)}, bf16[256,256]{1,0:T(8,128)(2,1)S(1)}) custom-call(bf16[4,4,2,128,256]{4,3,2,1,0:T(8,128)(2,1)S(1)} %copy-done, s32[4,4]{1,0:T(4,128)S(1)} %copy-done.4, bf16[4,1,2,8,512]{4,3,2,1,0:T(8,128)(2,1)S(1)} %copy-done.2, s32[1,16]{1,0:T(1,128)S(1)} %bitcast.18, ...), custom_call_target="tpu_custom_call" | custom-call | flops 134217728 | bytes 2097152 | tf_op jit(solution)/shard_map/tables2/pallas_call | solution.py:176
  31.0 1.3 %tables3.1 = (bf16[4,256,384]{2,1,0:T(8,128)(2,1)S(1)}, f32[256,512]{1,0:T(8,128)S(1)}, f32[256,512]{1,0:T(8,128)S(1)}, bf16[256,256]{1,0:T(8,128)(2,1)S(1)}) custom-call(bf16[4,4,2,128,256]{4,3,2,1,0:T(8,128)(2,1)S(1)} %copy-done, s32[4,4]{1,0:T(4,128)S(1)} %copy-done.4, bf16[4,1,2,8,512]{4,3,2,1,0:T(8,128)(2,1)S(1)} %copy-done.2, s32[1,16]{1,0:T(1,128)S(1)} %bitcast.19, ...), custom_call_target="tpu_custom_call" | custom-call | flops 134217728 | bytes 2097152 | tf_op jit(solution)/shard_map/tables3/pallas_call | solution.py:176
  32.3 0.4 reach2.1
  32.6 0.0 collective-permute-done.3.refs_2_
  32.6 0.0 collective-permute-done.4.refs_3_
  32.6 0.4 collective-permute-done.2.refs_1_
  33.0 1.2 %merge1.1 = (bf16[2,128,512]{2,1,0:T(8,128)(2,1)S(1)}, bf16[2,128,512]{2,1,0:T(8,128)(2,1)S(1)}, bf16[2,128,128]{2,1,0:T(8,128)(2,1)S(1)}, bf16[2,128,128]{2,1,0...) custom-call(bf16[2,128,640]{2,1,0:T(8,128)(2,1)S(1)} %get-tuple-element.92.refs_0_, ...), custom_call_target="tpu_custom_call" | custom-call | flops 536870912 | bytes 1048576 | tf_op jit(solution)/shard_map/merge1/pallas_call | solution.py:293
  34.2 2.7 %collective-permute-start.5 = (bf16[2,128,512]{2,1,0:T(8,128)(2,1)S(1)}, bf16[2,128,512]{2,1,0:T(8,128)(2,1)S(1)}, u32[]{:S(2)}, u32[]{:S(2)}) collective-permute-start(bf16[2,128,512]{2,1,0:T(8,128)(2,1)S(1)} %get-tuple-element.101), channel_id=1, source_target_pairs={{0,32},{1,33},{2,34},{3,35},{4,36},{5,37},{6,38},{7,39},{8,40},{9,... | collective-permute-start | bytes 786440 | tf_op jit(solution)/shard_map/ppermute | solution.py:312
  37.0 3.1 %collective-permute-start.6 = (bf16[2,128,256]{2,1,0:T(8,128)(2,1)S(1)}, bf16[2,128,256]{2,1,0:T(8,128)(2,1)S(1)}, u32[]{:S(2)}, u32[]{:S(2)}) collective-permute-start(bf16[2,128,256]{2,1,0:T(8,128)(2,1)S(1)} %get-tuple-element.102), channel_id=1, source_target_pairs={{0,33},{1,32},{2,35},{3,34},{4,37},{5,36},{6,39},{7,38},{8,41},{9,... | collective-permute-start | bytes 393224 | tf_op jit(solution)/shard_map/ppermute | solution.py:312
  40.1 1.9 %collective-permute-start.9 = (bf16[2,128,256]{2,1,0:T(8,128)(2,1)S(1)}, bf16[2,128,256]{2,1,0:T(8,128)(2,1)S(1)}, u32[]{:S(2)}, u32[]{:S(2)}) collective-permute-start(bf16[2,128,256]{2,1,0:T(8,128)(2,1)S(1)} %get-tuple-element.105), channel_id=1, source_target_pairs={{0,1},{1,0},{2,3},{3,2},{4,5},{5,4},{6,7},{7,6},{8,9},{9,8},{10,11... | collective-permute-start | bytes 393224 | tf_op jit(solution)/shard_map/ppermute | solution.py:312
  42.0 3.9 %collective-permute-start.7 = (bf16[2,128,128]{2,1,0:T(8,128)(2,1)S(1)}, bf16[2,128,128]{2,1,0:T(8,128)(2,1)S(1)}, u32[]{:S(2)}, u32[]{:S(2)}) collective-permute-start(bf16[2,128,128]{2,1,0:T(8,128)(2,1)S(1)} %get-tuple-element.103), channel_id=1, source_target_pairs={{1,34},{2,33},{5,38},{6,37},{9,42},{10,41},{13,46},{14,45},{17,50}... | collective-permute-start | bytes 196616 | tf_op jit(solution)/shard_map/ppermute | solution.py:312
  45.9 2.5 %collective-permute-start.8 = (bf16[2,128,128]{2,1,0:T(8,128)(2,1)S(1)}, bf16[2,128,128]{2,1,0:T(8,128)(2,1)S(1)}, u32[]{:S(2)}, u32[]{:S(2)}) collective-permute-start(bf16[2,128,128]{2,1,0:T(8,128)(2,1)S(1)} %get-tuple-element.104), channel_id=1, source_target_pairs={{1,2},{2,1},{5,6},{6,5},{9,10},{10,9},{13,14},{14,13},{17,18},{18,... | collective-permute-start | bytes 196616 | tf_op jit(solution)/shard_map/ppermute | solution.py:312
  48.4 0.1 collective-permute-done.7.refs_3_
  48.5 3.0 %collective-permute-done.8.refs_4_ = bf16[2,128,128]{2,1,0:T(8,128)(2,1)S(1)} collective-permute-done((bf16[2,128,128]{2,1,0:T(8,128)(2,1)S(1)}, bf16[2,128,128]{2,1,0:T(8,128)(2,1)S(1)}, u32[]{:S(2)}, u32[]{:S(2)}) %collective-permute-start.8) | collective-permute-done | bytes 65568 | tf_op jit(solution)/shard_map/ppermute | solution.py:312
  51.5 0.0 collective-permute-done.6.refs_2_
  51.5 0.0 collective-permute-done.9.refs_5_
  51.5 0.0 collective-permute-done.5.refs_1_
  51.5 1.3 %merge2.1 = (bf16[2,128,640]{2,1,0:T(8,128)(2,1)S(1)}, bf16[2,128,640]{2,1,0:T(8,128)(2,1)S(1)}, bf16[2,128,128]{2,1,0:T(8,128)(2,1)S(1)}, bf16[2,128,128]{2,1,0:T(8,128)(2,1)S(1)}) custom-call(bf16[2,128,512]{2,1,0:T(8,128)(2,1)S(1)} %get-tuple-element.100.refs_0_, bf16[2,128,512]{2,1,0:T(8,128)(2,1)S(1)} %collective-permute-done.5.refs_1_, ...), custom_call_target="tpu_custom_call" | custom-call | flops 536870912 | bytes 1048576 | tf_op jit(solution)/shard_map/merge2/pallas_call | solution.py:293
  52.8 6.1 %collective-permute-start.10 = (bf16[2,128,640]{2,1,0:T(8,128)(2,1)S(1)}, bf16[2,128,640]{2,1,0:T(8,128)(2,1)S(1)}, u32[]{:S(2)}, u32[]{:S(2)}) collective-permute-start(bf16[2,128,640]{2,1,0:T(8,128)(2,1)S(1)} %get-tuple-element.114), channel_id=1, source_target_pairs={{0,16},{1,17},{2,18},{3,19},{4,20},{5,21},{6,22},{7,23},{8,24},{9,... | collective-permute-start | bytes 983048 | tf_op jit(solution)/shard_map/ppermute | solution.py:312
  59.0 3.7 %collective-permute-start.11 = (bf16[2,128,128]{2,1,0:T(8,128)(2,1)S(1)}, bf16[2,128,128]{2,1,0:T(8,128)(2,1)S(1)}, u32[]{:S(2)}, u32[]{:S(2)}) collective-permute-start(bf16[2,128,128]{2,1,0:T(8,128)(2,1)S(1)} %get-tuple-element.115), channel_id=1, source_target_pairs={{1,18},{2,17},{5,22},{6,21},{9,26},{10,25},{13,30},{14,29},{17,2},... | collective-permute-start | bytes 196616 | tf_op jit(solution)/shard_map/ppermute | solution.py:312
  62.6 2.8 %collective-permute-start.12 = (bf16[2,128,128]{2,1,0:T(8,128)(2,1)S(1)}, bf16[2,128,128]{2,1,0:T(8,128)(2,1)S(1)}, u32[]{:S(2)}, u32[]{:S(2)}) collective-permute-start(bf16[2,128,128]{2,1,0:T(8,128)(2,1)S(1)} %get-tuple-element.116), channel_id=1, source_target_pairs={{1,2},{2,1},{5,6},{6,5},{9,10},{10,9},{13,14},{14,13},{17,18},{18,... | collective-permute-start | bytes 196616 | tf_op jit(solution)/shard_map/ppermute | solution.py:312
  65.4 6.4 %collective-permute-done.11.refs_2_ = bf16[2,128,128]{2,1,0:T(8,128)(2,1)S(1)} collective-permute-done((bf16[2,128,128]{2,1,0:T(8,128)(2,1)S(1)}, bf16[2,128,128]{2,1,0:T(8,128)(2,1)S(1)}, u32[]{:S(2)}, u32[]{:S(2)}) %collective-permute-start.11) | collective-permute-done | bytes 65568 | tf_op jit(solution)/shard_map/ppermute | solution.py:312
  71.8 0.0 collective-permute-done.12.refs_3_
  71.8 0.0 collective-permute-done.10.refs_1_
  71.8 1.1 %merge3.1 = (bf16[2,128,512]{2,1,0:T(8,128)(2,1)S(1)}, bf16[2,128,512]{2,1,0:T(8,128)(2,1)S(1)}) custom-call(bf16[2,128,640]{2,1,0:T(8,128)(2,1)S(1)} %get-tuple-element.113.refs_0_, bf16[2,128,640]{2,1,0:T(8,128)(2,1)S(1)} %collective-permute-done.10.refs_1_, bf16[2,128,128]{2,1,0:T(8,128)(2,1)S(1)} %collective-permute-done.11.refs_2_, ...), custom_call_target="tpu_custom_call" | custom-call | flops 536870912 | bytes 1048576 | tf_op jit(solution)/shard_map/merge3/pallas_call | solution.py:293
  73.0 3.1 %collective-permute-start.13 = (bf16[2,128,512]{2,1,0:T(8,128)(2,1)S(1)}, bf16[2,128,512]{2,1,0:T(8,128)(2,1)S(1)}, u32[]{:S(2)}, u32[]{:S(2)}) collective-permute-start(bf16[2,128,512]{2,1,0:T(8,128)(2,1)S(1)} %get-tuple-element.121), channel_id=1, source_target_pairs={{0,8},{1,9},{2,10},{3,11},{4,12},{5,13},{6,14},{7,15},{8,0},{9,1},... | collective-permute-start | bytes 786440 | tf_op jit(solution)/shard_map/ppermute | solution.py:312
  76.1 9.6 %collective-permute-done.13 = bf16[2,128,512]{2,1,0:T(8,128)(2,1)S(1)} collective-permute-done((bf16[2,128,512]{2,1,0:T(8,128)(2,1)S(1)}, bf16[2,128,512]{2,1,0:T(8,128)(2,1)S(1)}, u32[]{:S(2)}, u32[]{:S(2)}) %collective-permute-start.13) | collective-permute-done | bytes 262176 | tf_op jit(solution)/shard_map/ppermute | solution.py:312
  85.7 0.9 maximum_bitcast_fusion
  (1 shorter events, 0.0 us)
Async XLA Ops:
  0.0 13.0 %copy-start = (bf16[4,4,2,128,256]{4,3,2,1,0:T(8,128)(2,1)S(1)}, bf16[4,4,2,128,256]{4,3,2,1,0:T(8,128)(2,1)}, u32[]{:S(2)}) copy-start(bf16[4,4,2,128,256]{4,3,2,1,0:T(8,128)(2,1)} %taps.7) | copy-start | bytes 6291460
  0.0 13.0 %copy-start.2 = (bf16[4,1,2,8,512]{4,3,2,1,0:T(8,128)(2,1)S(1)}, bf16[4,1,2,8,512]{4,3,2,1,0:T(8,128)(2,1)}, u32[]{:S(2)}) copy-start(bf16[4,1,2,8,512]{4,3,2,1,0:T(8,128)(2,1)} %ramp.7) | copy-start | bytes 196612
  0.0 13.0 %copy-start.4 = (s32[4,4]{1,0:T(4,128)S(1)}, s32[4,4]{1,0:T(4,128)}, u32[]{:S(2)}) copy-start(s32[4,4]{1,0:T(4,128)} %offsets.9) | copy-start | bytes 196
  0.0 13.0 %copy-start.5 = (s32[16]{0:T(128)S(1)}, s32[16]{0:T(128)}, u32[]{:S(2)}) copy-start(s32[16]{0:T(128)} %param.12) | copy-start | bytes 196
  0.0 13.0 %copy-start.6 = (f32[8]{0:T(128)S(1)}, f32[8]{0:T(128)}, u32[]{:S(2)}) copy-start(f32[8]{0:T(128)} %param.13) | copy-start | bytes 100
  0.0 13.0 %copy-start.3 = (bf16[4,1,2,8,16]{4,3,2,1,0:T(8,128)(2,1)S(1)}, bf16[4,1,2,8,16]{4,3,2,1,0:T(8,128)(2,1)}, u32[]{:S(2)}) copy-start(bf16[4,1,2,8,16]{4,3,2,1,0:T(8,128)(2,1)} %beam.7) | copy-start | bytes 6148
  0.0 17.5 %copy-start.1 = (bf16[1,2,16,16,512]{4,3,2,1,0:T(8,128)(2,1)S(1)}, bf16[1,2,16,16,512]{4,3,2,1,0:T(8,128)(2,1)}, u32[]{:S(2)}) copy-start(bf16[1,2,16,16,512]{4,3,2,1,0:T(8,128)(2,1)} %param.7) | copy-start | bytes 1572868
  2.3 12.0 %collective-permute-start = (bf16[66,16,256]{2,1,0:T(8,128)(2,1)}, bf16[66,16,256]{2,1,0:T(8,128)(2,1)S(1)}, u32[]{:S(2)}, u32[]{:S(2)}) collective-permute-start(bf16[66,16,256]{2,1,0:T(8,128)(2,1)} %get-tuple-element.64), channel_id=1, source_target_pairs={{0,1},{1,0},{2,3},{3,2},{4,5},{5,4},{6,7},{7,6},{8,9},{9,8},{10,11... | collective-permute-start | bytes 1622024 | tf_op jit(solution)/shard_map/ppermute | solution.py:312
  11.1 6.5 %collective-permute-start.1 = (bf16[2,16,16,128]{3,2,1,0:T(8,128)(2,1)}, bf16[2,16,16,128]{3,2,1,0:T(8,128)(2,1)S(1)}, u32[]{:S(2)}, u32[]{:S(2)}) collective-permute-start(bf16[2,16,16,128]{3,2,1,0:T(8,128)(2,1)} %get-tuple-element.65), channel_id=1, source_target_pairs={{1,2},{2,1},{5,6},{6,5},{9,10},{10,9},{13,14},{14,13},{17,18},{18,... | collective-permute-start | bytes 393224 | tf_op jit(solution)/shard_map/ppermute | solution.py:312
  18.9 14.1 %collective-permute-start.2 = (bf16[2,128,640]{2,1,0:T(8,128)(2,1)S(1)}, bf16[2,128,640]{2,1,0:T(8,128)(2,1)S(1)}, u32[]{:S(2)}, u32[]{:S(2)}) collective-permute-start(bf16[2,128,640]{2,1,0:T(8,128)(2,1)S(1)} %get-tuple-element.74), channel_id=1, source_target_pairs={{0,64},{1,65},{2,66},{3,67},{4,68},{5,69},{6,70},{7,71},{8,72},{9,... | collective-permute-start | bytes 983048 | tf_op jit(solution)/shard_map/ppermute | solution.py:312
  20.8 11.8 %collective-permute-start.3 = (bf16[2,128,128]{2,1,0:T(8,128)(2,1)S(1)}, bf16[2,128,128]{2,1,0:T(8,128)(2,1)S(1)}, u32[]{:S(2)}, u32[]{:S(2)}) collective-permute-start(bf16[2,128,128]{2,1,0:T(8,128)(2,1)S(1)} %get-tuple-element.75), channel_id=1, source_target_pairs={{1,66},{2,65},{5,70},{6,69},{9,74},{10,73},{13,78},{14,77},{17,82}... | collective-permute-start | bytes 196616 | tf_op jit(solution)/shard_map/ppermute | solution.py:312
  25.1 7.6 %collective-permute-start.4 = (bf16[2,128,128]{2,1,0:T(8,128)(2,1)S(1)}, bf16[2,128,128]{2,1,0:T(8,128)(2,1)S(1)}, u32[]{:S(2)}, u32[]{:S(2)}) collective-permute-start(bf16[2,128,128]{2,1,0:T(8,128)(2,1)S(1)} %get-tuple-element.76), channel_id=1, source_target_pairs={{1,2},{2,1},{5,6},{6,5},{9,10},{10,9},{13,14},{14,13},{17,18},{18,... | collective-permute-start | bytes 196616 | tf_op jit(solution)/shard_map/ppermute | solution.py:312
  34.2 17.3 %collective-permute-start.5 = (bf16[2,128,512]{2,1,0:T(8,128)(2,1)S(1)}, bf16[2,128,512]{2,1,0:T(8,128)(2,1)S(1)}, u32[]{:S(2)}, u32[]{:S(2)}) collective-permute-start(bf16[2,128,512]{2,1,0:T(8,128)(2,1)S(1)} %get-tuple-element.101), channel_id=1, source_target_pairs={{0,32},{1,33},{2,34},{3,35},{4,36},{5,37},{6,38},{7,39},{8,40},{9,... | collective-permute-start | bytes 786440 | tf_op jit(solution)/shard_map/ppermute | solution.py:312
  37.0 14.6 %collective-permute-start.6 = (bf16[2,128,256]{2,1,0:T(8,128)(2,1)S(1)}, bf16[2,128,256]{2,1,0:T(8,128)(2,1)S(1)}, u32[]{:S(2)}, u32[]{:S(2)}) collective-permute-start(bf16[2,128,256]{2,1,0:T(8,128)(2,1)S(1)} %get-tuple-element.102), channel_id=1, source_target_pairs={{0,33},{1,32},{2,35},{3,34},{4,37},{5,36},{6,39},{7,38},{8,41},{9,... | collective-permute-start | bytes 393224 | tf_op jit(solution)/shard_map/ppermute | solution.py:312
  40.1 11.5 %collective-permute-start.9 = (bf16[2,128,256]{2,1,0:T(8,128)(2,1)S(1)}, bf16[2,128,256]{2,1,0:T(8,128)(2,1)S(1)}, u32[]{:S(2)}, u32[]{:S(2)}) collective-permute-start(bf16[2,128,256]{2,1,0:T(8,128)(2,1)S(1)} %get-tuple-element.105), channel_id=1, source_target_pairs={{0,1},{1,0},{2,3},{3,2},{4,5},{5,4},{6,7},{7,6},{8,9},{9,8},{10,11... | collective-permute-start | bytes 393224 | tf_op jit(solution)/shard_map/ppermute | solution.py:312
  42.0 6.5 %collective-permute-start.7 = (bf16[2,128,128]{2,1,0:T(8,128)(2,1)S(1)}, bf16[2,128,128]{2,1,0:T(8,128)(2,1)S(1)}, u32[]{:S(2)}, u32[]{:S(2)}) collective-permute-start(bf16[2,128,128]{2,1,0:T(8,128)(2,1)S(1)} %get-tuple-element.103), channel_id=1, source_target_pairs={{1,34},{2,33},{5,38},{6,37},{9,42},{10,41},{13,46},{14,45},{17,50}... | collective-permute-start | bytes 196616 | tf_op jit(solution)/shard_map/ppermute | solution.py:312
  45.9 5.6 %collective-permute-start.8 = (bf16[2,128,128]{2,1,0:T(8,128)(2,1)S(1)}, bf16[2,128,128]{2,1,0:T(8,128)(2,1)S(1)}, u32[]{:S(2)}, u32[]{:S(2)}) collective-permute-start(bf16[2,128,128]{2,1,0:T(8,128)(2,1)S(1)} %get-tuple-element.104), channel_id=1, source_target_pairs={{1,2},{2,1},{5,6},{6,5},{9,10},{10,9},{13,14},{14,13},{17,18},{18,... | collective-permute-start | bytes 196616 | tf_op jit(solution)/shard_map/ppermute | solution.py:312
  52.8 19.0 %collective-permute-start.10 = (bf16[2,128,640]{2,1,0:T(8,128)(2,1)S(1)}, bf16[2,128,640]{2,1,0:T(8,128)(2,1)S(1)}, u32[]{:S(2)}, u32[]{:S(2)}) collective-permute-start(bf16[2,128,640]{2,1,0:T(8,128)(2,1)S(1)} %get-tuple-element.114), channel_id=1, source_target_pairs={{0,16},{1,17},{2,18},{3,19},{4,20},{5,21},{6,22},{7,23},{8,24},{9,... | collective-permute-start | bytes 983048 | tf_op jit(solution)/shard_map/ppermute | solution.py:312
  59.0 12.9 %collective-permute-start.11 = (bf16[2,128,128]{2,1,0:T(8,128)(2,1)S(1)}, bf16[2,128,128]{2,1,0:T(8,128)(2,1)S(1)}, u32[]{:S(2)}, u32[]{:S(2)}) collective-permute-start(bf16[2,128,128]{2,1,0:T(8,128)(2,1)S(1)} %get-tuple-element.115), channel_id=1, source_target_pairs={{1,18},{2,17},{5,22},{6,21},{9,26},{10,25},{13,30},{14,29},{17,2},... | collective-permute-start | bytes 196616 | tf_op jit(solution)/shard_map/ppermute | solution.py:312
  62.6 9.2 %collective-permute-start.12 = (bf16[2,128,128]{2,1,0:T(8,128)(2,1)S(1)}, bf16[2,128,128]{2,1,0:T(8,128)(2,1)S(1)}, u32[]{:S(2)}, u32[]{:S(2)}) collective-permute-start(bf16[2,128,128]{2,1,0:T(8,128)(2,1)S(1)} %get-tuple-element.116), channel_id=1, source_target_pairs={{1,2},{2,1},{5,6},{6,5},{9,10},{10,9},{13,14},{14,13},{17,18},{18,... | collective-permute-start | bytes 196616 | tf_op jit(solution)/shard_map/ppermute | solution.py:312
  73.0 12.7 %collective-permute-start.13 = (bf16[2,128,512]{2,1,0:T(8,128)(2,1)S(1)}, bf16[2,128,512]{2,1,0:T(8,128)(2,1)S(1)}, u32[]{:S(2)}, u32[]{:S(2)}) collective-permute-start(bf16[2,128,512]{2,1,0:T(8,128)(2,1)S(1)} %get-tuple-element.121), channel_id=1, source_target_pairs={{0,8},{1,9},{2,10},{3,11},{4,12},{5,13},{6,14},{7,15},{8,0},{9,1},... | collective-permute-start | bytes 786440 | tf_op jit(solution)/shard_map/ppermute | solution.py:312
